TPU v7x, 32 devices: a whole 2x2x4 slice. The times are simulated.
32 devices in a mesh: space: 8 (over y, x, core), bins: 4 (over z).
Axes of the slice: x: 2, y: 2, z: 4, core: 2. Of those that a mesh axis runs over, the one named last changes fastest.
Arguments:
- population: float32 [256, 24, 32, 128], P('bins', 'space'), may hold values from 0 to 2
- velocity: bfloat16 [3, 24, 32, 128], P(None, 'space'), may hold values from -1 to 1
- supersat: float32 [24, 32, 128], P('space', 'bins'), may hold values from 0.2 to 1.5
- kernel: float32 [256], replicated, may hold values from 0.0005 to 0.004
Outputs:
- new_population: float32 [256, 24, 32, 128], P(None, 'space', 'bins')
- depletion: float32 [24, 32, 128], P('space')
All inputs are finite; a program needn't handle non-finite values.
Results may differ from a plain program's by a relative error of at most 0.0006.
Values may be sent and summed in bfloat16 or wider, within the bound.
No kernel may reach another device: no remote copies, remote signals or barrier semaphores. Data moves between devices by JAX's collectives and lax.ppermute only.
A program may use at most 64 MiB of HBM per device.

v0:
```python
import jax
import jax.numpy as jnp
from jax import lax
from jax.sharding import PartitionSpec as P

STEPS = 3
KSTEPS = 8


COURANT = 0.3
GROW = 0.4
BETA = 0.5


def passed_along(array, axis, by):
    count = lax.axis_size(axis)
    pairs = [(i, i + by) for i in range(count) if 0 <= i + by < count]
    return lax.ppermute(array, axis, pairs)


def padded(array, sides, width):
    for axis, dim in sides:
        count, length = (lax.axis_size(axis), array.shape[dim])
        up = [(i, (i + 1) % count) for i in range(count - 1)]
        down = [(j, i) for i, j in up]
        last = lax.slice_in_dim(array, length - width, length, axis=dim)
        initial = lax.slice_in_dim(array, 0, width, axis=dim)
        before = lax.ppermute(last, axis, up)
        after = lax.ppermute(initial, axis, down)
        array = jnp.concatenate([before, array, after], axis=dim)
    return array


def advance(density, vel_padded):
    vel = vel_padded.astype(jnp.float32)
    span_x = density.shape[1] - 2
    span_y = density.shape[2] - 2
    vel_x = vel[0, 1 : span_x + 2, 1 : span_y + 1]
    flux_x = (
        jnp.maximum(vel_x, 0.0) * density[:, 0 : span_x + 1, 1 : span_y + 1]
        + jnp.minimum(vel_x, 0.0) * density[:, 1 : span_x + 2, 1 : span_y + 1]
    )
    outflow = flux_x[:, 1:] - flux_x[:, :-1]
    vel_y = vel[1, 1 : span_x + 1, 1 : span_y + 2]
    flux_y = (
        jnp.maximum(vel_y, 0.0) * density[:, 1 : span_x + 1, 0 : span_y + 1]
        + jnp.minimum(vel_y, 0.0) * density[:, 1 : span_x + 1, 1 : span_y + 2]
    )
    outflow = outflow + flux_y[:, :, 1:] - flux_y[:, :, :-1]
    centre = density[:, 1 : span_x + 1, 1 : span_y + 1]
    count_z = centre.shape[3]
    padded_z = jnp.pad(centre, ((0, 0), (0, 0), (0, 0), (1, 1)))
    vel_z = jnp.pad(vel[2, 1 : span_x + 1, 1 : span_y + 1], ((0, 0), (0, 0), (0, 1)))
    flux_z = (
        jnp.maximum(vel_z, 0.0) * padded_z[..., 0 : count_z + 1]
        + jnp.minimum(vel_z, 0.0) * padded_z[..., 1 : count_z + 2]
    )
    outflow = outflow + flux_z[..., 1:] - flux_z[..., :-1]
    return centre - COURANT * outflow


def kinetics(columns, supersat, kernel):
    bin_count = kernel.shape[0]
    row_index = jnp.arange(bin_count, dtype=jnp.int32)[:, None]
    col_index = jnp.arange(bin_count, dtype=jnp.int32)[None, :]
    offsets = row_index - col_index
    toeplitz = jnp.where(offsets >= 0, kernel[jnp.clip(offsets, 0, bin_count - 1)], 0.0).astype(
        jnp.bfloat16
    )
    colsum = jnp.cumsum(kernel)[::-1][:, None]
    masses = ((jnp.arange(bin_count, dtype=jnp.float32) + 1.0) / bin_count) ** 3
    initial = columns
    for substep in range(KSTEPS):
        product = jnp.dot(
            toeplitz, columns.astype(jnp.bfloat16), preferred_element_type=jnp.float32
        )
        lower_bins = jnp.pad(columns[:-1], ((1, 0), (0, 0)))
        columns = (
            columns
            + GROW * supersat * (lower_bins - columns)
            + BETA * supersat * (product - colsum * columns)
        )
    depletion = jnp.sum(masses[:, None] * (columns - initial), axis=0)
    return (columns, depletion)


def pad_second(values):
    return jnp.pad(values, ((0, 0), (0, 0), (1, 1), (0, 0)))


def body(population, velocity, supersat, kernel):
    slab_steps = STEPS
    density = population
    above = passed_along(velocity[:, 0:1], "space", -1)
    vel_rows = jnp.concatenate([jnp.zeros_like(above), velocity, above], axis=1)
    vel_near = pad_second(vel_rows)
    for sweep in range(slab_steps):
        rimmed = padded(density, (("space", 1),), 1)
        density = advance(pad_second(rimmed), vel_near)
    batches = lax.all_to_all(density, "bins", split_axis=2, concat_axis=0, tiled=True)
    bin_count = batches.shape[0]
    updated, depletion = kinetics(batches.reshape(bin_count, -1), supersat.reshape(-1), kernel)
    new_population = updated.reshape(batches.shape)
    depletion = lax.all_gather(depletion.reshape(supersat.shape), "bins", axis=1, tiled=True)
    return (new_population, depletion)


def solution(mesh):
    in_specs = (
        P("bins", "space", None, None),
        P(None, "space", None, None),
        P("space", "bins", None),
        P(),
    )
    out_specs = (P(None, "space", "bins", None), P("space", None, None))
    return jax.shard_map(body, mesh=mesh, in_specs=in_specs, out_specs=out_specs, check_vma=False)
```

profile of v0, /device:TPU:2, one launch (start us, length us, event | category | flops | bytes accessed | tf_op | source)
XLA Modules:
  0.0 542.6 jit_solution(10205654135011114617)
XLA Ops:
  1.5 2.0 collective-permute-start
  3.6 1.7 fusion.53
  5.3 2.4 collective-permute-start.1
  7.7 3.2 collective-permute-start.2
  12.8 8.6 %collective-permute-done.1 = f32[64,1,32,128]{3,2,1,0:T(8,128)S(1)} collective-permute-done((f32[64,1,32,128]{3,2,1,0:T(8,128)S(1)}, f32[64,1,32,128]{3,2,1,0:T(8,128)S(1)}, u32[]{:S(2)}, u32[]{:S(2)}) %collective-permute-start.1) | collective-permute-done | bytes 1048608 | tf_op jit(solution)/shard_map/ppermute | solution.py:28
  21.4 11.1 %collective-permute-done.2 = f32[64,1,32,128]{3,2,1,0:T(8,128)S(1)} collective-permute-done((f32[64,1,32,128]{3,2,1,0:T(8,128)S(1)}, f32[64,1,32,128]{3,2,1,0:T(8,128)S(1)}, u32[]{:S(2)}, u32[]{:S(2)}) %collective-permute-start.2) | collective-permute-done | bytes 1048608 | tf_op jit(solution)/shard_map/ppermute | solution.py:29
  35.0 1.9 fusion.37
  37.1 2.8 collective-permute-start.3
  39.9 2.9 collective-permute-start.4
  44.6 8.8 %collective-permute-done.3 = f32[64,1,32,128]{3,2,1,0:T(8,128)S(1)} collective-permute-done((f32[64,1,32,128]{3,2,1,0:T(8,128)S(1)}, f32[64,1,32,128]{3,2,1,0:T(8,128)S(1)}, u32[]{:S(2)}, u32[]{:S(2)}) %collective-permute-start.3) | collective-permute-done | bytes 1048608 | tf_op jit(solution)/shard_map/ppermute | solution.py:28
  53.4 10.0 %collective-permute-done.4 = f32[64,1,32,128]{3,2,1,0:T(8,128)S(1)} collective-permute-done((f32[64,1,32,128]{3,2,1,0:T(8,128)S(1)}, f32[64,1,32,128]{3,2,1,0:T(8,128)S(1)}, u32[]{:S(2)}, u32[]{:S(2)}) %collective-permute-start.4) | collective-permute-done | bytes 1048608 | tf_op jit(solution)/shard_map/ppermute | solution.py:29
  65.9 1.9 fusion.35
  68.0 1.9 collective-permute-start.5
  69.9 4.0 collective-permute-start.6
  75.6 8.7 %collective-permute-done.5 = f32[64,1,32,128]{3,2,1,0:T(8,128)S(1)} collective-permute-done((f32[64,1,32,128]{3,2,1,0:T(8,128)S(1)}, f32[64,1,32,128]{3,2,1,0:T(8,128)S(1)}, u32[]{:S(2)}, u32[]{:S(2)}) %collective-permute-start.5) | collective-permute-done | bytes 1048608 | tf_op jit(solution)/shard_map/ppermute | solution.py:28
  84.3 8.9 %collective-permute-done.6 = f32[64,1,32,128]{3,2,1,0:T(8,128)S(1)} collective-permute-done((f32[64,1,32,128]{3,2,1,0:T(8,128)S(1)}, f32[64,1,32,128]{3,2,1,0:T(8,128)S(1)}, u32[]{:S(2)}, u32[]{:S(2)}) %collective-permute-start.6) | collective-permute-done | bytes 1048608 | tf_op jit(solution)/shard_map/ppermute | solution.py:29
  95.7 1.9 fusion.33
  97.6 3.5 copy.22
  101.1 5.0 all-to-all-start
  107.0 401.2 %gather_fusion = bf16[65536]{0:T(1024)(128)(2,1)S(1)} fusion(f32[256]{0:T(256)S(1)} %copy-done, s32[65536]{0:T(1024)S(1)} %broadcast_clamp_fusion), kind=kCustom, calls=%fused_computation | custom fusion | bytes 524288 | tf_op jit(solution)/shard_map/gather | solution.py:67
  509.1 3.5 copy.27
  512.5 3.0 reshape.81
  526.2 2.2 copy.25
  528.4 13.6 %all_gather.3 = f32[3,32,128]{2,1,0:T(8,128)S(1)} all-gather(f32[3,8,128]{2,1,0:T(8,128)S(1)} %bitcast.54), channel_id=1, replica_groups=mesh['space'=8,'bins'=4] {'bins'}, dimensions={1}, use_global_device_ids=true | all-gather | bytes 61440 | tf_op jit(solution)/shard_map/all_gather | solution.py:104
  (52 shorter events, 26.7 us)
Async XLA Ops:
  0.6 10.3 %copy-start.2 = (bf16[3,3,32,128]{3,2,1,0:T(8,128)(2,1)S(1)}, bf16[3,3,32,128]{3,2,1,0:T(8,128)(2,1)}, u32[]{:S(2)}) copy-start(bf16[3,3,32,128]{3,2,1,0:T(8,128)(2,1)} %param.5) | copy-start | bytes 221188
  0.6 10.5 %copy-start.1 = (f32[64,3,32,128]{3,2,1,0:T(8,128)S(1)}, f32[64,3,32,128]{3,2,1,0:T(8,128)}, u32[]{:S(2)}) copy-start(f32[64,3,32,128]{3,2,1,0:T(8,128)} %param.4) | copy-start | bytes 9437188
  1.5 9.4 %collective-permute-start = (bf16[3,1,32,128]{3,2,1,0:T(8,128)(2,1)S(1)}, bf16[3,1,32,128]{3,2,1,0:T(8,128)(2,1)S(1)}, u32[]{:S(2)}, u32[]{:S(2)}) collective-permute-start(bf16[3,1,32,128]{3,2,1,0:T(8,128)(2,1)S(1)} %slice.181), channel_id=1, source_target_pairs={{4,0},{8,4},{12,8},{16,12},{20,16},{24,20},{28,24},{5,1},{9,5},{13... | collective-permute-start | bytes 73736 | tf_op jit(solution)/shard_map/ppermute | solution.py:18
  5.3 16.1 %collective-permute-start.1 = (f32[64,1,32,128]{3,2,1,0:T(8,128)S(1)}, f32[64,1,32,128]{3,2,1,0:T(8,128)S(1)}, u32[]{:S(2)}, u32[]{:S(2)}) collective-permute-start(f32[64,1,32,128]{3,2,1,0:T(8,128)S(1)} %get-tuple-element.10), channel_id=1, source_target_pairs={{0,4},{4,8},{8,12},{12,16},{16,20},{20,24},{24,28},{1,5},{5,9},{9,... | collective-permute-start | bytes 3145736 | tf_op jit(solution)/shard_map/ppermute | solution.py:28
  7.7 24.8 %collective-permute-start.2 = (f32[64,1,32,128]{3,2,1,0:T(8,128)S(1)}, f32[64,1,32,128]{3,2,1,0:T(8,128)S(1)}, u32[]{:S(2)}, u32[]{:S(2)}) collective-permute-start(f32[64,1,32,128]{3,2,1,0:T(8,128)S(1)} %get-tuple-element.11), channel_id=1, source_target_pairs={{4,0},{8,4},{12,8},{16,12},{20,16},{24,20},{28,24},{5,1},{9,5},{13... | collective-permute-start | bytes 3145736 | tf_op jit(solution)/shard_map/ppermute | solution.py:29
  37.1 16.3 %collective-permute-start.3 = (f32[64,1,32,128]{3,2,1,0:T(8,128)S(1)}, f32[64,1,32,128]{3,2,1,0:T(8,128)S(1)}, u32[]{:S(2)}, u32[]{:S(2)}) collective-permute-start(f32[64,1,32,128]{3,2,1,0:T(8,128)S(1)} %get-tuple-element.8), channel_id=1, source_target_pairs={{0,4},{4,8},{8,12},{12,16},{16,20},{20,24},{24,28},{1,5},{5,9},{9,... | collective-permute-start | bytes 3145736 | tf_op jit(solution)/shard_map/ppermute | solution.py:28
  39.9 23.5 %collective-permute-start.4 = (f32[64,1,32,128]{3,2,1,0:T(8,128)S(1)}, f32[64,1,32,128]{3,2,1,0:T(8,128)S(1)}, u32[]{:S(2)}, u32[]{:S(2)}) collective-permute-start(f32[64,1,32,128]{3,2,1,0:T(8,128)S(1)} %get-tuple-element.9), channel_id=1, source_target_pairs={{4,0},{8,4},{12,8},{16,12},{20,16},{24,20},{28,24},{5,1},{9,5},{13... | collective-permute-start | bytes 3145736 | tf_op jit(solution)/shard_map/ppermute | solution.py:29
  68.0 16.3 %collective-permute-start.5 = (f32[64,1,32,128]{3,2,1,0:T(8,128)S(1)}, f32[64,1,32,128]{3,2,1,0:T(8,128)S(1)}, u32[]{:S(2)}, u32[]{:S(2)}) collective-permute-start(f32[64,1,32,128]{3,2,1,0:T(8,128)S(1)} %get-tuple-element.6), channel_id=1, source_target_pairs={{0,4},{4,8},{8,12},{12,16},{16,20},{20,24},{24,28},{1,5},{5,9},{9,... | collective-permute-start | bytes 3145736 | tf_op jit(solution)/shard_map/ppermute | solution.py:28
  69.9 23.3 %collective-permute-start.6 = (f32[64,1,32,128]{3,2,1,0:T(8,128)S(1)}, f32[64,1,32,128]{3,2,1,0:T(8,128)S(1)}, u32[]{:S(2)}, u32[]{:S(2)}) collective-permute-start(f32[64,1,32,128]{3,2,1,0:T(8,128)S(1)} %get-tuple-element.7), channel_id=1, source_target_pairs={{4,0},{8,4},{12,8},{16,12},{20,16},{24,20},{28,24},{5,1},{9,5},{13... | collective-permute-start | bytes 3145736 | tf_op jit(solution)/shard_map/ppermute | solution.py:29
  101.1 5.0 copy-start
  101.1 408.0 %all-to-all-start = ((f32[64,3,32,128]{3,0,1,2:T(8,128)}), f32[64,3,32,128]{3,0,1,2:T(8,128)S(1)}, u32[]{:S(2)}, u32[]{:S(2)}) async-start(f32[64,3,32,128]{3,0,1,2:T(8,128)} %copy.22), calls=%async_computation | async-start | bytes 6291456 | tf_op jit(solution)/shard_map/all_to_all | solution.py:100
where the time goes:
time: 543 us
  local copies, waits for them, and re-layouts  418 us (77%)
  waiting for transfers between devices  56.1 us (10%)
  starting transfers between devices  24.3 us (4%)
  other arithmetic  19.5 us (4%)
  blocking collectives  13.6 us (3%)
  matrix products  10.5 us (2%)
    gather x2, local copies, waits for them, and re-layouts, kinetics(): kernel[jnp.clip(offsets, 0, bin_count - 1)]  401 us
    ppermute x3, waiting for transfers between devices, padded(): after = lax.ppermute(initial, axis, down)  30 us
    ppermute x3, waiting for transfers between devices, padded(): before = lax.ppermute(last, axis, up)  26.1 us
    all_gather x1, blocking collectives, body(): lax.all_gather(depletion.reshape(supersat.shape), 'bins', axis=1, tiled=T...  13.6 us
  transfers between devices with their start and end apart: 8, of which 6 were waited for; matrix products, arithmetic and copies ran while one was open for 76% of the time, Pallas kernels for 0%

commit v1 on v0

--- a/solution.py
+++ b/solution.py
@@ -61,12 +61,10 @@
 
 def kinetics(columns, supersat, kernel):
     bin_count = kernel.shape[0]
-    row_index = jnp.arange(bin_count, dtype=jnp.int32)[:, None]
-    col_index = jnp.arange(bin_count, dtype=jnp.int32)[None, :]
-    offsets = row_index - col_index
-    toeplitz = jnp.where(offsets >= 0, kernel[jnp.clip(offsets, 0, bin_count - 1)], 0.0).astype(
-        jnp.bfloat16
-    )
+    wide = jnp.concatenate([kernel, jnp.zeros_like(kernel)]).astype(jnp.bfloat16)
+    span = 2 * bin_count
+    rows = jnp.tile(wide, bin_count)[: bin_count * (span - 1)].reshape(bin_count, span - 1)
+    toeplitz = rows[:, :bin_count].T
     colsum = jnp.cumsum(kernel)[::-1][:, None]
     masses = ((jnp.arange(bin_count, dtype=jnp.float32) + 1.0) / bin_count) ** 3
     initial = columns

time: 543 us -> 207 us (0.38)
  local copies, waits for them, and re-layouts: 418 us -> 18.4 us
  waiting for transfers between devices: 56.1 us -> 120 us
    gather x2 -> x0, local copies, waits for them, and re-layouts: 401 us -> none  [kinetics(): kernel[jnp.clip(offsets, 0, bin_count - 1)]]
    all_to_all x1, waiting for transfers between devices: 0.01 us -> 63.8 us  [body(): lax.all_to_all(density, 'bins', split_axis=2, concat_axis=0, tiled=True)]
  transfers between devices with their start and end apart: 8 -> 8, of which waited for: 6 -> 7; matrix products, arithmetic and copies ran while one was open for 76% -> 5% of each run, Pallas kernels for 0% -> 0%
where the time goes in v1:
time: 207 us; the launch traced here: 206 us
  waiting for transfers between devices  120 us (58%)
  starting transfers between devices  24.3 us (12%)
  other arithmetic  18.7 us (9%)
  local copies, waits for them, and re-layouts  18.4 us (9%)
  blocking collectives  13.1 us (6%)
  matrix products  10.7 us (5%)
    all_to_all x1, waiting for transfers between devices, body(): lax.all_to_all(density, 'bins', split_axis=2, concat_axis=0, tiled=True)  63.8 us
    ppermute x3, waiting for transfers between devices, padded(): after = lax.ppermute(initial, axis, down)  30 us
    ppermute x3, waiting for transfers between devices, padded(): before = lax.ppermute(last, axis, up)  26.1 us
    all_gather x1, blocking collectives, body(): lax.all_gather(depletion.reshape(supersat.shape), 'bins', axis=1, tiled=T...  13.1 us
    dot_general x8, matrix products, kinetics(): jnp.dot(toeplitz, columns.astype(jnp.bfloat16), preferred_element_type=jn...  10.7 us
    ppermute x3, starting transfers between devices, padded(): after = lax.ppermute(initial, axis, down)  10.1 us
    ppermute x3, starting transfers between devices, padded(): before = lax.ppermute(last, axis, up)  7.14 us
    sub x3, other arithmetic, advance(): return centre - COURANT * outflow  5.7 us
  transfers between devices with their start and end apart: 8, of which 7 were waited for; matrix products, arithmetic and copies ran while one was open for 5% of the time, Pallas kernels for 0%

profile of v1, /device:TPU:2, one launch (start us, length us, event | category | flops | bytes accessed | tf_op | source)
XLA Modules:
  0.0 206.1 jit_solution(8054078403074162504)
XLA Ops:
  1.5 2.0 collective-permute-start
  3.6 1.7 fusion.60
  5.3 2.4 %collective-permute-start.1 = (f32[64,1,32,128]{3,2,1,0:T(8,128)S(1)}, f32[64,1,32,128]{3,2,1,0:T(8,128)S(1)}, u32[]{:S(2)}, u32[]{:S(2)}) collective-permute-start(f32[64,1,32,128]{3,2,1,0:T(8,128)S(1)} %get-tuple-element.10), channel_id=1, source_target_pairs={{0,4},{4,8},{8,12},{12,16},{16,20},{20,24},{24,28},{1,5},{5,9},{9,... | collective-permute-start | bytes 3145736 | tf_op jit(solution)/shard_map/ppermute | solution.py:28
  7.7 3.2 %collective-permute-start.2 = (f32[64,1,32,128]{3,2,1,0:T(8,128)S(1)}, f32[64,1,32,128]{3,2,1,0:T(8,128)S(1)}, u32[]{:S(2)}, u32[]{:S(2)}) collective-permute-start(f32[64,1,32,128]{3,2,1,0:T(8,128)S(1)} %get-tuple-element.11), channel_id=1, source_target_pairs={{4,0},{8,4},{12,8},{16,12},{20,16},{24,20},{28,24},{5,1},{9,5},{13... | collective-permute-start | bytes 3145736 | tf_op jit(solution)/shard_map/ppermute | solution.py:29
  12.8 8.6 %collective-permute-done.1 = f32[64,1,32,128]{3,2,1,0:T(8,128)S(1)} collective-permute-done((f32[64,1,32,128]{3,2,1,0:T(8,128)S(1)}, f32[64,1,32,128]{3,2,1,0:T(8,128)S(1)}, u32[]{:S(2)}, u32[]{:S(2)}) %collective-permute-start.1) | collective-permute-done | bytes 1048608 | tf_op jit(solution)/shard_map/ppermute | solution.py:28
  21.4 11.1 %collective-permute-done.2 = f32[64,1,32,128]{3,2,1,0:T(8,128)S(1)} collective-permute-done((f32[64,1,32,128]{3,2,1,0:T(8,128)S(1)}, f32[64,1,32,128]{3,2,1,0:T(8,128)S(1)}, u32[]{:S(2)}, u32[]{:S(2)}) %collective-permute-start.2) | collective-permute-done | bytes 1048608 | tf_op jit(solution)/shard_map/ppermute | solution.py:29
  35.0 1.9 fusion.37
  37.1 2.8 %collective-permute-start.3 = (f32[64,1,32,128]{3,2,1,0:T(8,128)S(1)}, f32[64,1,32,128]{3,2,1,0:T(8,128)S(1)}, u32[]{:S(2)}, u32[]{:S(2)}) collective-permute-start(f32[64,1,32,128]{3,2,1,0:T(8,128)S(1)} %get-tuple-element.8), channel_id=1, source_target_pairs={{0,4},{4,8},{8,12},{12,16},{16,20},{20,24},{24,28},{1,5},{5,9},{9,... | collective-permute-start | bytes 3145736 | tf_op jit(solution)/shard_map/ppermute | solution.py:28
  39.9 2.9 %collective-permute-start.4 = (f32[64,1,32,128]{3,2,1,0:T(8,128)S(1)}, f32[64,1,32,128]{3,2,1,0:T(8,128)S(1)}, u32[]{:S(2)}, u32[]{:S(2)}) collective-permute-start(f32[64,1,32,128]{3,2,1,0:T(8,128)S(1)} %get-tuple-element.9), channel_id=1, source_target_pairs={{4,0},{8,4},{12,8},{16,12},{20,16},{24,20},{28,24},{5,1},{9,5},{13... | collective-permute-start | bytes 3145736 | tf_op jit(solution)/shard_map/ppermute | solution.py:29
  44.6 8.8 %collective-permute-done.3 = f32[64,1,32,128]{3,2,1,0:T(8,128)S(1)} collective-permute-done((f32[64,1,32,128]{3,2,1,0:T(8,128)S(1)}, f32[64,1,32,128]{3,2,1,0:T(8,128)S(1)}, u32[]{:S(2)}, u32[]{:S(2)}) %collective-permute-start.3) | collective-permute-done | bytes 1048608 | tf_op jit(solution)/shard_map/ppermute | solution.py:28
  53.4 10.0 %collective-permute-done.4 = f32[64,1,32,128]{3,2,1,0:T(8,128)S(1)} collective-permute-done((f32[64,1,32,128]{3,2,1,0:T(8,128)S(1)}, f32[64,1,32,128]{3,2,1,0:T(8,128)S(1)}, u32[]{:S(2)}, u32[]{:S(2)}) %collective-permute-start.4) | collective-permute-done | bytes 1048608 | tf_op jit(solution)/shard_map/ppermute | solution.py:29
  65.9 1.9 fusion.35
  68.0 1.9 collective-permute-start.5
  69.9 4.0 %collective-permute-start.6 = (f32[64,1,32,128]{3,2,1,0:T(8,128)S(1)}, f32[64,1,32,128]{3,2,1,0:T(8,128)S(1)}, u32[]{:S(2)}, u32[]{:S(2)}) collective-permute-start(f32[64,1,32,128]{3,2,1,0:T(8,128)S(1)} %get-tuple-element.7), channel_id=1, source_target_pairs={{4,0},{8,4},{12,8},{16,12},{20,16},{24,20},{28,24},{5,1},{9,5},{13... | collective-permute-start | bytes 3145736 | tf_op jit(solution)/shard_map/ppermute | solution.py:29
  75.6 8.7 %collective-permute-done.5 = f32[64,1,32,128]{3,2,1,0:T(8,128)S(1)} collective-permute-done((f32[64,1,32,128]{3,2,1,0:T(8,128)S(1)}, f32[64,1,32,128]{3,2,1,0:T(8,128)S(1)}, u32[]{:S(2)}, u32[]{:S(2)}) %collective-permute-start.5) | collective-permute-done | bytes 1048608 | tf_op jit(solution)/shard_map/ppermute | solution.py:28
  84.3 8.9 %collective-permute-done.6 = f32[64,1,32,128]{3,2,1,0:T(8,128)S(1)} collective-permute-done((f32[64,1,32,128]{3,2,1,0:T(8,128)S(1)}, f32[64,1,32,128]{3,2,1,0:T(8,128)S(1)}, u32[]{:S(2)}, u32[]{:S(2)}) %collective-permute-start.6) | collective-permute-done | bytes 1048608 | tf_op jit(solution)/shard_map/ppermute | solution.py:29
  95.7 1.9 fusion.33
  97.6 3.5 %copy.22 = f32[64,3,32,128]{3,0,1,2:T(8,128)} copy(f32[64,3,32,128]{3,2,1,0:T(8,128)S(1)} %fusion.33) | data formatting | bytes 6291456 | tf_op jit(solution)/shard_map/sub | solution.py:59
  101.1 5.0 %all-to-all-start = ((f32[64,3,32,128]{3,0,1,2:T(8,128)}), f32[64,3,32,128]{3,0,1,2:T(8,128)S(1)}, u32[]{:S(2)}, u32[]{:S(2)}) async-start(f32[64,3,32,128]{3,0,1,2:T(8,128)} %copy.22), calls=%async_computation | async-start | bytes 6291456 | tf_op jit(solution)/shard_map/all_to_all | solution.py:98
  109.1 63.8 %all-to-all-done = f32[64,3,32,128]{3,0,1,2:T(8,128)S(1)} async-done(((f32[64,3,32,128]{3,0,1,2:T(8,128)}), f32[64,3,32,128]{3,0,1,2:T(8,128)S(1)}, u32[]{:S(2)}, u32[]{:S(2)}) %all-to-all-start) | async-done | bytes 3145760 | tf_op jit(solution)/shard_map/all_to_all | solution.py:98
  172.9 3.5 %copy.27 = f32[64,3,4,8,128]{4,3,1,0,2:T(8,128)} copy(f32[64,3,4,8,128]{4,0,1,3,2:T(8,128)S(1)} %bitcast.48) | data formatting | bytes 6291456 | tf_op jit(solution)/shard_map/all_to_all | solution.py:98
  176.4 3.0 %reshape.57 = f32[256,3072]{1,0:T(8,128)S(1)} reshape(f32[4,64,3,8,128]{4,3,2,1,0:T(8,128)} %bitcast.49) | data formatting | bytes 6291456 | tf_op jit(solution)/shard_map/reshape | solution.py:100
  190.2 2.2 %copy.25 = f32[32,8,24,128]{3,2,1,0:T(8,128)} copy(f32[32,8,24,128]{3,1,2,0:T(8,128)S(1)} %bitcast.50) | data formatting | bytes 6291456
  192.4 13.1 %all_gather.3 = f32[3,32,128]{2,1,0:T(8,128)S(1)} all-gather(f32[3,8,128]{2,1,0:T(8,128)S(1)} %bitcast.53), channel_id=1, replica_groups=mesh['space'=8,'bins'=4] {'bins'}, dimensions={1}, use_global_device_ids=true | all-gather | bytes 61440 | tf_op jit(solution)/shard_map/all_gather | solution.py:102
  (54 shorter events, 28.1 us)
Async XLA Ops:
  0.6 10.3 %copy-start.1 = (bf16[3,3,32,128]{3,2,1,0:T(8,128)(2,1)S(1)}, bf16[3,3,32,128]{3,2,1,0:T(8,128)(2,1)}, u32[]{:S(2)}) copy-start(bf16[3,3,32,128]{3,2,1,0:T(8,128)(2,1)} %param.5) | copy-start | bytes 221188
  0.6 10.5 %copy-start = (f32[64,3,32,128]{3,2,1,0:T(8,128)S(1)}, f32[64,3,32,128]{3,2,1,0:T(8,128)}, u32[]{:S(2)}) copy-start(f32[64,3,32,128]{3,2,1,0:T(8,128)} %param.4) | copy-start | bytes 9437188
  1.5 9.4 %collective-permute-start = (bf16[3,1,32,128]{3,2,1,0:T(8,128)(2,1)S(1)}, bf16[3,1,32,128]{3,2,1,0:T(8,128)(2,1)S(1)}, u32[]{:S(2)}, u32[]{:S(2)}) collective-permute-start(bf16[3,1,32,128]{3,2,1,0:T(8,128)(2,1)S(1)} %slice.187), channel_id=1, source_target_pairs={{4,0},{8,4},{12,8},{16,12},{20,16},{24,20},{28,24},{5,1},{9,5},{13... | collective-permute-start | bytes 73736 | tf_op jit(solution)/shard_map/ppermute | solution.py:18
  5.3 16.1 %collective-permute-start.1 = (f32[64,1,32,128]{3,2,1,0:T(8,128)S(1)}, f32[64,1,32,128]{3,2,1,0:T(8,128)S(1)}, u32[]{:S(2)}, u32[]{:S(2)}) collective-permute-start(f32[64,1,32,128]{3,2,1,0:T(8,128)S(1)} %get-tuple-element.10), channel_id=1, source_target_pairs={{0,4},{4,8},{8,12},{12,16},{16,20},{20,24},{24,28},{1,5},{5,9},{9,... | collective-permute-start | bytes 3145736 | tf_op jit(solution)/shard_map/ppermute | solution.py:28
  7.7 24.8 %collective-permute-start.2 = (f32[64,1,32,128]{3,2,1,0:T(8,128)S(1)}, f32[64,1,32,128]{3,2,1,0:T(8,128)S(1)}, u32[]{:S(2)}, u32[]{:S(2)}) collective-permute-start(f32[64,1,32,128]{3,2,1,0:T(8,128)S(1)} %get-tuple-element.11), channel_id=1, source_target_pairs={{4,0},{8,4},{12,8},{16,12},{20,16},{24,20},{28,24},{5,1},{9,5},{13... | collective-permute-start | bytes 3145736 | tf_op jit(solution)/shard_map/ppermute | solution.py:29
  37.1 16.3 %collective-permute-start.3 = (f32[64,1,32,128]{3,2,1,0:T(8,128)S(1)}, f32[64,1,32,128]{3,2,1,0:T(8,128)S(1)}, u32[]{:S(2)}, u32[]{:S(2)}) collective-permute-start(f32[64,1,32,128]{3,2,1,0:T(8,128)S(1)} %get-tuple-element.8), channel_id=1, source_target_pairs={{0,4},{4,8},{8,12},{12,16},{16,20},{20,24},{24,28},{1,5},{5,9},{9,... | collective-permute-start | bytes 3145736 | tf_op jit(solution)/shard_map/ppermute | solution.py:28
  39.9 23.5 %collective-permute-start.4 = (f32[64,1,32,128]{3,2,1,0:T(8,128)S(1)}, f32[64,1,32,128]{3,2,1,0:T(8,128)S(1)}, u32[]{:S(2)}, u32[]{:S(2)}) collective-permute-start(f32[64,1,32,128]{3,2,1,0:T(8,128)S(1)} %get-tuple-element.9), channel_id=1, source_target_pairs={{4,0},{8,4},{12,8},{16,12},{20,16},{24,20},{28,24},{5,1},{9,5},{13... | collective-permute-start | bytes 3145736 | tf_op jit(solution)/shard_map/ppermute | solution.py:29
  68.0 16.3 %collective-permute-start.5 = (f32[64,1,32,128]{3,2,1,0:T(8,128)S(1)}, f32[64,1,32,128]{3,2,1,0:T(8,128)S(1)}, u32[]{:S(2)}, u32[]{:S(2)}) collective-permute-start(f32[64,1,32,128]{3,2,1,0:T(8,128)S(1)} %get-tuple-element.6), channel_id=1, source_target_pairs={{0,4},{4,8},{8,12},{12,16},{16,20},{20,24},{24,28},{1,5},{5,9},{9,... | collective-permute-start | bytes 3145736 | tf_op jit(solution)/shard_map/ppermute | solution.py:28
  69.9 23.3 %collective-permute-start.6 = (f32[64,1,32,128]{3,2,1,0:T(8,128)S(1)}, f32[64,1,32,128]{3,2,1,0:T(8,128)S(1)}, u32[]{:S(2)}, u32[]{:S(2)}) collective-permute-start(f32[64,1,32,128]{3,2,1,0:T(8,128)S(1)} %get-tuple-element.7), channel_id=1, source_target_pairs={{4,0},{8,4},{12,8},{16,12},{20,16},{24,20},{28,24},{5,1},{9,5},{13... | collective-permute-start | bytes 3145736 | tf_op jit(solution)/shard_map/ppermute | solution.py:29
  101.0 5.0 %copy-start.3 = (f32[256]{0:T(256)S(1)}, f32[256]{0:T(256)}, u32[]{:S(2)}) copy-start(f32[256]{0:T(256)} %param.7) | copy-start | bytes 3076
  101.1 8.0 %copy-start.2 = (f32[3,8,128]{2,1,0:T(8,128)S(1)}, f32[3,8,128]{2,1,0:T(8,128)}, u32[]{:S(2)}) copy-start(f32[3,8,128]{2,1,0:T(8,128)} %param.6) | copy-start | bytes 36868
  101.1 71.8 %all-to-all-start = ((f32[64,3,32,128]{3,0,1,2:T(8,128)}), f32[64,3,32,128]{3,0,1,2:T(8,128)S(1)}, u32[]{:S(2)}, u32[]{:S(2)}) async-start(f32[64,3,32,128]{3,0,1,2:T(8,128)} %copy.22), calls=%async_computation | async-start | bytes 6291456 | tf_op jit(solution)/shard_map/all_to_all | solution.py:98

commit v2 on v1

v2 whole, which is shorter than its diff:
```python
import functools

import jax
import jax.numpy as jnp
from jax import lax
from jax.experimental import pallas as pl
from jax.experimental.pallas import tpu as pltpu
from jax.sharding import PartitionSpec as P

STEPS = 3
KSTEPS = 8

COURANT = 0.3
GROW = 0.4
BETA = 0.5

POWER = 9
SCALE = 256.0
GROUP = 16
VMEM_LIMIT = 48 * 1024 * 1024


def encode(scaled):
    square = scaled * scaled
    fourth = square * square
    return (fourth * fourth * scaled).astype(jnp.bfloat16)


def decode(code):
    wide = code.astype(jnp.float32)
    size = jnp.exp(jnp.log(jnp.abs(wide)) * (1.0 / POWER))
    return jnp.where(wide < 0.0, -size, size)


def params():
    return pltpu.CompilerParams(vmem_limit_bytes=VMEM_LIMIT)


def vmem_spec():
    return pl.BlockSpec(memory_space=pltpu.VMEM)


def cells_first(block_ref, x, y, bins, span_x, span_y):
    rows = block_ref.reshape(bins * span_x * span_y, block_ref.shape[3])
    return rows[pl.ds(x * span_y + y, bins, stride=span_x * span_y), :]


def code_kernel(pop_ref, code_ref):
    bins, span_x, span_y, _ = pop_ref.shape
    for x in range(span_x):

        def row(y, carry, x=x):
            code_ref[x, y] = encode(cells_first(pop_ref, x, y, bins, span_x, span_y) * SCALE)
            return carry

        lax.fori_loop(0, span_y, row, 0, unroll=4)


def coded_slab(population, index):
    _, span_x, span_y, span_z = population.shape
    return pl.pallas_call(
        code_kernel,
        grid=(1,),
        in_specs=[pl.BlockSpec((GROUP, span_x, span_y, span_z), lambda i: (index, 0, 0, 0))],
        out_specs=pl.BlockSpec((span_x, span_y, GROUP, span_z), lambda i: (0, 0, 0, 0)),
        out_shape=jax.ShapeDtypeStruct((span_x, span_y, GROUP, span_z), jnp.bfloat16),
        compiler_params=params(),
        name="code_slab",
    )(population)


def stencil(src_ref, coef_ref, x, y, shift):
    span_z = src_ref.shape[3]
    centre = src_ref[x + 1, y + 1]
    weight = lambda k: coef_ref[x + shift, y, pl.ds(k, 1), :]
    total = weight(0) * centre
    total += weight(1) * src_ref[x, y + 1]
    total += weight(2) * src_ref[x + 2, y + 1]
    total += weight(3) * src_ref[x + 1, y]
    total += weight(4) * src_ref[x + 1, y + 2]
    total += weight(5) * pltpu.roll(centre, 1, 1)
    total += weight(6) * pltpu.roll(centre, span_z - 1, 1)
    return total


def transport_kernel(batches, place_ref, pop_ref, below_ref, above_ref, coef_ref, *rest):
    outs, (first, second, third) = rest[:batches], rest[batches:]
    bins, span_x, span_y, span_z = pop_ref.shape
    zeros = jnp.zeros((bins, span_z), jnp.float32)
    for ref in (first, second, third):
        for x in range(ref.shape[0]):
            ref[x, 0] = zeros
            ref[x, span_y + 1] = zeros
    for x in range(span_x):

        def fill(y, carry, x=x):
            first[x, y + 1] = decode(below_ref[x, y])
            first[span_x + x, y + 1] = cells_first(pop_ref, x, y, bins, span_x, span_y) * SCALE
            first[2 * span_x + x, y + 1] = decode(above_ref[x, y])
            return carry

        lax.fori_loop(0, span_y, fill, 0, unroll=2)
    for src, dst, shift in ((first, second, 0), (second, third, 1)):

        def layer(x, carry, src=src, dst=dst, shift=shift):
            def row(y, carry):
                dst[x, y + 1] = stencil(src, coef_ref, x, y, shift)
                return carry

            return lax.fori_loop(0, span_y, row, carry, unroll=4)

        lax.fori_loop(0, dst.shape[0], layer, 0)
    span_out = span_y // batches
    for ahead in range(batches):
        begin = lax.rem(place_ref[0] + ahead, batches) * span_out

        def layer(x, carry, ahead=ahead, begin=begin):
            for y in range(span_out):
                outs[ahead][x, y] = encode(stencil(third, coef_ref, x, begin + y, 2))
            return carry

        lax.fori_loop(0, span_x, layer, 0)


def transported(place, population, below, above, coefs, index, batches):
    _, span_x, span_y, span_z = population.shape
    out = (span_x, span_y // batches, GROUP, span_z)
    whole = lambda shape: pl.BlockSpec(shape, lambda i, place_ref: (0,) * len(shape))
    grid_spec = pltpu.PrefetchScalarGridSpec(
        num_scalar_prefetch=1,
        grid=(1,),
        in_specs=[
            pl.BlockSpec(
                (GROUP, span_x, span_y, span_z), lambda i, place_ref: (index, 0, 0, 0)
            ),
            whole(below.shape),
            whole(above.shape),
            whole(coefs.shape),
        ],
        out_specs=[whole(out)] * batches,
        scratch_shapes=[
            pltpu.VMEM((layers, span_y + 2, GROUP, span_z), jnp.float32)
            for layers in (3 * span_x, 3 * span_x - 2, 3 * span_x - 4)
        ],
    )
    return pl.pallas_call(
        functools.partial(transport_kernel, batches),
        grid_spec=grid_spec,
        out_shape=[jax.ShapeDtypeStruct(out, jnp.bfloat16)] * batches,
        compiler_params=params(),
        name="transport",
    )(place, population, below, above, coefs)


def table_kernel(kernel_ref, toeplitz_ref, column_ref):
    bin_count = toeplitz_ref.shape[0]
    wide = jnp.broadcast_to(kernel_ref[...], (bin_count, 2 * bin_count))
    turned = pltpu.roll(wide, 0, 1, stride=1, stride_axis=0)[:, :bin_count]
    column_ref[...] = jnp.broadcast_to(
        jnp.sum(turned, axis=1, keepdims=True), column_ref.shape
    )
    toeplitz_ref[...] = turned.T.astype(jnp.bfloat16)


def tables(kernel):
    bin_count = kernel.shape[0]
    return pl.pallas_call(
        table_kernel,
        in_specs=[vmem_spec()],
        out_specs=[vmem_spec()] * 2,
        out_shape=[
            jax.ShapeDtypeStruct((bin_count, bin_count), jnp.bfloat16),
            jax.ShapeDtypeStruct((bin_count, 128), jnp.float32),
        ],
        compiler_params=params(),
        name="tables",
    )(jnp.concatenate([kernel, jnp.zeros_like(kernel)])[None, :])


def kinetics_kernel(
    batches, groups, native, place_ref, supersat_ref, toeplitz_ref, column_ref, *rest
):
    parts = rest[: batches * groups]
    out_ref, depletion_ref, initial, even, odd = rest[batches * groups :]
    bin_count, width = initial.shape
    span_y, span_z = supersat_ref.shape[1:]
    pad = even.shape[0] - bin_count
    block = min(width, 2 * span_z)
    for ref in (even, odd):
        ref[0:pad, :] = jnp.zeros((pad, width), jnp.float32)
    for back in range(batches):
        source = lax.rem(place_ref[0] + batches - back, batches) * (groups * GROUP)
        for index in range(groups):
            part = parts[back * groups + index]
            at = pl.multiple_of(source + index * GROUP, GROUP)
            for y in range(span_y):
                value = decode(part[0, y]) * (1.0 / SCALE)
                cells = slice(y * span_z, (y + 1) * span_z)
                initial[pl.ds(at, GROUP), cells] = value
                even[pl.ds(pad + at, GROUP), cells] = value

    def substep(src, dst):
        for begin in range(0, width, block):
            cells = slice(begin, begin + block)
            speed = jnp.concatenate(
                [
                    supersat_ref[0, pl.ds(y, 1), :]
                    for y in range(begin // span_z, (begin + block) // span_z)
                ],
                axis=1,
            )
            column = jnp.concatenate([column_ref[...]] * (block // 128), axis=1)
            now = src[pad:, cells]
            product = jnp.dot(
                toeplitz_ref[...],
                now.astype(jnp.bfloat16),
                preferred_element_type=jnp.float32,
            )
            lower = src[pad - 1 : pad - 1 + bin_count, cells]
            change = (GROW / BETA) * (lower - now) + (product - column * now)
            dst[pad:, cells] = now + (BETA * speed) * change

    def pair(index, carry):
        substep(even, odd)
        substep(odd, even)
        return carry

    lax.fori_loop(0, KSTEPS // 2, pair, 0)
    bins = lax.broadcasted_iota(jnp.int32, (bin_count, span_z), 0).astype(jnp.float32)
    ratio = (bins + 1.0) / bin_count
    masses = ratio * ratio * ratio
    for y in range(span_y):
        cells = slice(y * span_z, (y + 1) * span_z)
        final = even[pad:, cells]
        depletion_ref[0, pl.ds(y, 1), :] = jnp.sum(
            masses * (final - initial[:, cells]), axis=0, keepdims=True
        )
        if native:
            rows = out_ref.reshape(bin_count * span_y, span_z)
            rows[pl.ds(y, bin_count, stride=span_y), :] = final
        else:
            out_ref[0, y] = final


def kinetics(place, supersat, toeplitz, column, parts, batches, groups):
    span_x, span_y, span_z = supersat.shape
    bin_count = toeplitz.shape[0]
    native = span_y % 8 == 0
    whole = lambda shape: pl.BlockSpec(shape, lambda i, place_ref: (0,) * len(shape))
    layer = lambda shape: pl.BlockSpec(
        (1,) + shape[1:], lambda i, place_ref: (i,) + (0,) * (len(shape) - 1)
    )
    if native:
        out_shape = (bin_count, span_x, span_y, span_z)
        out_spec = pl.BlockSpec(
            (bin_count, 1, span_y, span_z), lambda i, place_ref: (0, i, 0, 0)
        )
    else:
        out_shape = (span_x, span_y, bin_count, span_z)
        out_spec = layer(out_shape)
    grid_spec = pltpu.PrefetchScalarGridSpec(
        num_scalar_prefetch=1,
        grid=(span_x,),
        in_specs=[layer(supersat.shape), whole(toeplitz.shape), whole(column.shape)]
        + [layer(part.shape) for part in parts],
        out_specs=[out_spec, layer(supersat.shape)],
        scratch_shapes=[
            pltpu.VMEM((bin_count + pad, span_y * span_z), jnp.float32) for pad in (0, 8, 8)
        ],
    )
    out, depletion = pl.pallas_call(
        functools.partial(kinetics_kernel, batches, groups, native),
        grid_spec=grid_spec,
        out_shape=[
            jax.ShapeDtypeStruct(out_shape, jnp.float32),
            jax.ShapeDtypeStruct(supersat.shape, jnp.float32),
        ],
        compiler_params=params(),
        name="kinetics",
    )(place, supersat, toeplitz, column, *parts)
    return (out if native else jnp.transpose(out, (2, 0, 1, 3)), depletion)


def along(array, axis, by, around=False):
    count = lax.axis_size(axis)
    pairs = [(i, (i + by) % count) for i in range(count) if around or 0 <= i + by < count]
    return lax.ppermute(array, axis, pairs)


def weights(velocity):
    below = along(velocity, "space", 1)
    above = along(velocity, "space", -1)
    span_x = velocity.shape[1]
    vel = jnp.concatenate([below, velocity, above], axis=1).astype(jnp.float32)
    rise = COURANT * jnp.maximum(vel, 0.0)
    fall = -COURANT * jnp.minimum(vel, 0.0)

    def following(values, axis):
        sides = [(0, 0)] * 3
        sides[axis] = (0, 1)
        return lax.slice_in_dim(
            jnp.pad(values, sides), 1, values.shape[axis] + 1, axis=axis
        )

    here = slice(1, -1)
    rise_next = [following(rise[axis], axis)[here] for axis in range(3)]
    fall_next = [following(fall[axis], axis)[here] for axis in range(3)]
    rise, fall = rise[:, here], fall[:, here]
    kept = 1.0 - sum(rise_next) - fall[0] - fall[1] - fall[2]
    inner = (jnp.arange(vel.shape[3]) > 0).astype(jnp.float32)
    stacked = jnp.stack(
        [
            kept,
            rise[0],
            fall_next[0],
            rise[1],
            fall_next[1],
            rise[2] * inner,
            fall_next[2],
            jnp.zeros_like(kept),
        ],
        axis=2,
    )
    layers = jnp.arange(1, 3 * span_x - 1)
    exists = (layers >= span_x) | (lax.axis_index("space") > 0)
    return jnp.where(exists[:, None, None, None], stacked, 0.0)


def body(population, velocity, supersat, kernel):
    batches = lax.axis_size("bins")
    groups = population.shape[0] // GROUP
    place = lax.axis_index("bins").astype(jnp.int32)[None]
    coefs = weights(velocity)
    toeplitz, column = tables(kernel)
    codes = [coded_slab(population, index) for index in range(groups)]
    rims = [(along(code, "space", 1), along(code, "space", -1)) for code in codes]
    parts = [[None] * groups for _ in range(batches)]
    for index in range(groups):
        below, above = rims[index]
        pieces = transported(place, population, below, above, coefs, index, batches)
        for ahead in range(batches):
            piece = pieces[ahead]
            parts[ahead][index] = along(piece, "bins", ahead, True) if ahead else piece
    flat = [part for row in parts for part in row]
    new_population, depletion = kinetics(
        place, supersat, toeplitz, column, flat, batches, groups
    )
    depletion = lax.all_gather(depletion, "bins", axis=1, tiled=True)
    return (new_population, depletion)


def solution(mesh):
    in_specs = (
        P("bins", "space", None, None),
        P(None, "space", None, None),
        P("space", "bins", None),
        P(),
    )
    out_specs = (P(None, "space", "bins", None), P("space", None, None))
    return jax.shard_map(body, mesh=mesh, in_specs=in_specs, out_specs=out_specs, check_vma=False)
```

time: 207 us -> 157 us (0.76)
  waiting for transfers between devices: 120 us -> 9.17 us
  Pallas kernels: 0 us -> 72.8 us
  starting transfers between devices: 24.3 us -> 46.4 us
  other arithmetic: 18.7 us -> 2.85 us
  matrix products: 10.7 us -> 0 us
  local copies, waits for them, and re-layouts: 18.4 us -> 9.88 us
    pallas_call x0 -> x10, Pallas kernels: none -> 72.8 us  [the longest x4 50 us: transported(): pl.pallas_call(functools.partial(transport_kernel, batches), grid_spec=gr...]
    all_to_all x1 -> x0, waiting for transfers between devices: 63.8 us -> none  [body(): lax.all_to_all(density, 'bins', split_axis=2, concat_axis=0, tiled=True)]
    ppermute x7 -> x22, waiting for transfers between devices: 56.1 us -> 9.17 us  [along(): return lax.ppermute(array, axis, pairs)]
    ppermute x7 -> x22, starting transfers between devices: 19.3 us -> 46.4 us  [along(): return lax.ppermute(array, axis, pairs)]
    dot_general x8 -> x0, matrix products: 10.7 us -> none  [kinetics(): jnp.dot(toeplitz, columns.astype(jnp.bfloat16), preferred_element_type=jn...]
    add x9 -> x0, other arithmetic: 9.59 us -> none  [the longest x3 5.07 us: advance(): jnp.maximum(vel_z, 0.0) * padded_z[..., 0:count_z + 1]]
    all_to_all x1 -> x0, starting transfers between devices: 5 us -> none  [body(): lax.all_to_all(density, 'bins', split_axis=2, concat_axis=0, tiled=True)]
    sub x3 -> x1, other arithmetic: 5.7 us -> 0.76 us  [weights(): kept = 1.0 - sum(rise_next) - fall[0] - fall[1] - fall[2]]
  transfers between devices with their start and end apart: 8 -> 22, of which waited for: 7 -> 3; matrix products, arithmetic and copies ran while one was open for 5% -> 7% of each run, Pallas kernels for 0% -> 36%
where the time goes in v2:
time: 157 us; the launch traced here: 155 us
  Pallas kernels  72.8 us (46%)
  starting transfers between devices  46.4 us (30%)
  blocking collectives  13.3 us (8%)
  local copies, waits for them, and re-layouts  9.88 us (6%)
  waiting for transfers between devices  9.17 us (6%)
  other arithmetic  2.85 us (2%)
    pallas_call x4, Pallas kernels, transported(): pl.pallas_call(functools.partial(transport_kernel, batches), grid_spec=gr...  50 us
    ppermute x22, starting transfers between devices, along(): return lax.ppermute(array, axis, pairs)  46.4 us
    pallas_call x1, Pallas kernels, kinetics(): pl.pallas_call(functools.partial(kinetics_kernel, batches, groups, native...  17.5 us
    all_gather x1, blocking collectives, body(): depletion = lax.all_gather(depletion, 'bins', axis=1, tiled=True)  13.3 us
    ppermute x22, waiting for transfers between devices, along(): return lax.ppermute(array, axis, pairs)  9.17 us
    pallas_call x4, Pallas kernels, coded_slab(): pl.pallas_call(code_kernel, grid=(1,), in_specs=[pl.BlockSpec((GROUP, spa...  5.06 us
    another operation x2, local copies, waits for them, and re-layouts, weights(): jnp.stack([kept, rise[0], fall_next[0], rise[1], fall_next[1], rise[2] *...  4.5 us
  transfers between devices with their start and end apart: 22, of which 3 were waited for; matrix products, arithmetic and copies ran while one was open for 7% of the time, Pallas kernels for 36%

profile of v2, /device:TPU:2, one launch (start us, length us, event | category | flops | bytes accessed | tf_op | source)
XLA Modules:
  0.0 155.4 jit_solution(5916395048165253241)
XLA Ops:
  0.6 1.9 %collective-permute-start.2 = (bf16[3,3,32,128]{3,2,1,0:T(8,128)(2,1)}, bf16[3,3,32,128]{3,2,1,0:T(8,128)(2,1)S(1)}, u32[]{:S(2)}, u32[]{:S(2)}) collective-permute-start(bf16[3,3,32,128]{3,2,1,0:T(8,128)(2,1)} %param.5), channel_id=1, source_target_pairs={{0,4},{4,8},{8,12},{12,16},{16,20},{20,24},{24,28},{1,5},{5,9},{9,... | collective-permute-start | bytes 221192 | tf_op jit(solution)/shard_map/ppermute | solution.py:287
  2.6 3.6 %collective-permute-start.3 = (bf16[3,3,32,128]{3,2,1,0:T(8,128)(2,1)}, bf16[3,3,32,128]{3,2,1,0:T(8,128)(2,1)S(1)}, u32[]{:S(2)}, u32[]{:S(2)}) collective-permute-start(bf16[3,3,32,128]{3,2,1,0:T(8,128)(2,1)} %param.5), channel_id=1, source_target_pairs={{4,0},{8,4},{12,8},{16,12},{20,16},{24,20},{28,24},{5,1},{9,5},{13... | collective-permute-start | bytes 221192 | tf_op jit(solution)/shard_map/ppermute | solution.py:287
  6.2 1.9 %copy-done = f32[64,3,32,128]{3,2,1,0:T(8,128)S(1)} copy-done((f32[64,3,32,128]{3,2,1,0:T(8,128)S(1)}, f32[64,3,32,128]{3,2,1,0:T(8,128)}, u32[]{:S(2)}) %copy-start) | copy-done | bytes 3145752
  9.6 1.9 %collective-permute-start.6 = (bf16[3,32,16,128]{3,2,1,0:T(8,128)(2,1)}, bf16[3,32,16,128]{3,2,1,0:T(8,128)(2,1)}, u32[]{:S(2)}, u32[]{:S(2)}) collective-permute-start(bf16[3,32,16,128]{3,2,1,0:T(8,128)(2,1)} %code_slab.6), channel_id=1, source_target_pairs={{0,4},{4,8},{8,12},{12,16},{16,20},{20,24},{24,28},{1,5},{5,9},{9,... | collective-permute-start | bytes 1179656 | tf_op jit(solution)/shard_map/ppermute | solution.py:287
  11.5 3.6 %collective-permute-start.7 = (bf16[3,32,16,128]{3,2,1,0:T(8,128)(2,1)}, bf16[3,32,16,128]{3,2,1,0:T(8,128)(2,1)}, u32[]{:S(2)}, u32[]{:S(2)}) collective-permute-start(bf16[3,32,16,128]{3,2,1,0:T(8,128)(2,1)} %code_slab.6), channel_id=1, source_target_pairs={{4,0},{8,4},{12,8},{16,12},{20,16},{24,20},{28,24},{5,1},{9,5},{13... | collective-permute-start | bytes 1179656 | tf_op jit(solution)/shard_map/ppermute | solution.py:287
  16.6 2.7 %collective-permute-start.8 = (bf16[3,32,16,128]{3,2,1,0:T(8,128)(2,1)}, bf16[3,32,16,128]{3,2,1,0:T(8,128)(2,1)}, u32[]{:S(2)}, u32[]{:S(2)}) collective-permute-start(bf16[3,32,16,128]{3,2,1,0:T(8,128)(2,1)} %code_slab.7), channel_id=1, source_target_pairs={{0,4},{4,8},{8,12},{12,16},{16,20},{20,24},{24,28},{1,5},{5,9},{9,... | collective-permute-start | bytes 1179656 | tf_op jit(solution)/shard_map/ppermute | solution.py:287
  21.5 2.9 %collective-permute-start.9 = (bf16[3,32,16,128]{3,2,1,0:T(8,128)(2,1)}, bf16[3,32,16,128]{3,2,1,0:T(8,128)(2,1)}, u32[]{:S(2)}, u32[]{:S(2)}) collective-permute-start(bf16[3,32,16,128]{3,2,1,0:T(8,128)(2,1)} %code_slab.7), channel_id=1, source_target_pairs={{4,0},{8,4},{12,8},{16,12},{20,16},{24,20},{28,24},{5,1},{9,5},{13... | collective-permute-start | bytes 1179656 | tf_op jit(solution)/shard_map/ppermute | solution.py:287
  24.4 3.6 %collective-permute-start.4 = (bf16[3,32,16,128]{3,2,1,0:T(8,128)(2,1)}, bf16[3,32,16,128]{3,2,1,0:T(8,128)(2,1)}, u32[]{:S(2)}, u32[]{:S(2)}) collective-permute-start(bf16[3,32,16,128]{3,2,1,0:T(8,128)(2,1)} %code_slab.5), channel_id=1, source_target_pairs={{0,4},{4,8},{8,12},{12,16},{16,20},{20,24},{24,28},{1,5},{5,9},{9,... | collective-permute-start | bytes 1179656 | tf_op jit(solution)/shard_map/ppermute | solution.py:287
  31.0 2.0 %collective-permute-start.5 = (bf16[3,32,16,128]{3,2,1,0:T(8,128)(2,1)}, bf16[3,32,16,128]{3,2,1,0:T(8,128)(2,1)}, u32[]{:S(2)}, u32[]{:S(2)}) collective-permute-start(bf16[3,32,16,128]{3,2,1,0:T(8,128)(2,1)} %code_slab.5), channel_id=1, source_target_pairs={{4,0},{8,4},{12,8},{16,12},{20,16},{24,20},{28,24},{5,1},{9,5},{13... | collective-permute-start | bytes 1179656 | tf_op jit(solution)/shard_map/ppermute | solution.py:287
  33.0 4.5 %collective-permute-start = (bf16[3,32,16,128]{3,2,1,0:T(8,128)(2,1)S(1)}, bf16[3,32,16,128]{3,2,1,0:T(8,128)(2,1)}, u32[]{:S(2)}, u32[]{:S(2)}) collective-permute-start(bf16[3,32,16,128]{3,2,1,0:T(8,128)(2,1)S(1)} %code_slab.4), channel_id=1, source_target_pairs={{0,4},{4,8},{8,12},{12,16},{16,20},{20,24},{24,28},{1,5},{5,9},{9,... | collective-permute-start | bytes 1179656 | tf_op jit(solution)/shard_map/ppermute | solution.py:287
  37.5 1.9 %collective-permute-start.1 = (bf16[3,32,16,128]{3,2,1,0:T(8,128)(2,1)S(1)}, bf16[3,32,16,128]{3,2,1,0:T(8,128)(2,1)}, u32[]{:S(2)}, u32[]{:S(2)}) collective-permute-start(bf16[3,32,16,128]{3,2,1,0:T(8,128)(2,1)S(1)} %code_slab.4), channel_id=1, source_target_pairs={{4,0},{8,4},{12,8},{16,12},{20,16},{24,20},{28,24},{5,1},{9,5},{13... | collective-permute-start | bytes 1179656 | tf_op jit(solution)/shard_map/ppermute | solution.py:287
  41.5 3.8 %stack.20 = f32[7,32,8,128]{3,2,1,0:T(8,128)} concatenate(f32[7,32,1,128]{3,2,1,0:T(1,128)} %bitcast.54, f32[7,32,1,128]{3,2,1,0:T(1,128)} %bitcast.49, f32[7,32,1,128]{3,2,1,0:T(1,128)} %bitcast.51, f32[7,32,1,128]{3,2,1,0:T(1,128)} %bitcast.48, f32[7,32,1,128]{3,2,1,0:T(1,128)} %bitcast.52, f32[7,32,1,128]{3,2,1,0:T(1,128)} %bitcast.50, f32[7,32,1,128]{3,2,1,0:T(1,128)} %bitcast.53, ...), dimensions={2} | concatenate | bytes 1835008 | tf_op jit(solution)/shard_map/stack | solution.py:311
  46.6 12.5 %transport.6 = (bf16[3,8,16,128]{3,2,1,0:T(8,128)(2,1)S(1)}, bf16[3,8,16,128]{3,2,1,0:T(8,128)(2,1)S(1)}, bf16[3,8,16,128]{3,2,1,0:T(8,128)(2,1)S(1)}, bf16[3,8,16,128]{3,2,1,0:T(8,128)(2,1)S(1)}) custom-call(s32[1]{0:T(128)} %bitcast.place_ref, f32[64,3,32,128]{3,2,1,0:T(8,128)S(1)} %copy-done.1, bf16[3,32,16,128]{3,2,1,0:T(8,128)(2,1)} %collective-permute-done.6.below_ref, ...), custom_call_target="tpu_custom_call" | custom-call | tf_op jit(solution)/shard_map/transport/pallas_call | solution.py:146
  60.8 12.5 %transport.7 = (bf16[3,8,16,128]{3,2,1,0:T(8,128)(2,1)S(1)}, bf16[3,8,16,128]{3,2,1,0:T(8,128)(2,1)S(1)}, bf16[3,8,16,128]{3,2,1,0:T(8,128)(2,1)S(1)}, bf16[3,8,16,128]{3,2,1,0:T(8,128)(2,1)S(1)}) custom-call(s32[1]{0:T(128)} %bitcast.place_ref, f32[64,3,32,128]{3,2,1,0:T(8,128)S(1)} %copy-done.1, bf16[3,32,16,128]{3,2,1,0:T(8,128)(2,1)} %collective-permute-done.8.below_ref, ...), custom_call_target="tpu_custom_call" | custom-call | tf_op jit(solution)/shard_map/transport/pallas_call | solution.py:146
  76.2 12.5 %transport.5 = (bf16[3,8,16,128]{3,2,1,0:T(8,128)(2,1)S(1)}, bf16[3,8,16,128]{3,2,1,0:T(8,128)(2,1)S(1)}, bf16[3,8,16,128]{3,2,1,0:T(8,128)(2,1)S(1)}, bf16[3,8,16,128]{3,2,1,0:T(8,128)(2,1)S(1)}) custom-call(s32[1]{0:T(128)} %bitcast.place_ref, f32[64,3,32,128]{3,2,1,0:T(8,128)S(1)} %copy-done.1, bf16[3,32,16,128]{3,2,1,0:T(8,128)(2,1)} %collective-permute-done.4.below_ref, ...), custom_call_target="tpu_custom_call" | custom-call | tf_op jit(solution)/shard_map/transport/pallas_call | solution.py:146
  88.7 1.8 %collective-permute-start.17 = (bf16[3,8,16,128]{3,2,1,0:T(8,128)(2,1)S(1)}, bf16[3,8,16,128]{3,2,1,0:T(8,128)(2,1)S(1)}, u32[]{:S(2)}, u32[]{:S(2)}) collective-permute-start(bf16[3,8,16,128]{3,2,1,0:T(8,128)(2,1)S(1)} %get-tuple-element.35), channel_id=1, source_target_pairs={{0,2},{1,3},{2,0},{3,1},{4,6},{5,7},{6,4},{7,5},{8,10},{9,11},{10,... | collective-permute-start | bytes 294920 | tf_op jit(solution)/shard_map/ppermute | solution.py:287
  90.5 2.2 %collective-permute-start.20 = (bf16[3,8,16,128]{3,2,1,0:T(8,128)(2,1)S(1)}, bf16[3,8,16,128]{3,2,1,0:T(8,128)(2,1)S(1)}, u32[]{:S(2)}, u32[]{:S(2)}) collective-permute-start(bf16[3,8,16,128]{3,2,1,0:T(8,128)(2,1)S(1)} %get-tuple-element.38), channel_id=1, source_target_pairs={{0,3},{1,0},{2,1},{3,2},{4,7},{5,4},{6,5},{7,6},{8,11},{9,8},{10,9... | collective-permute-start | bytes 294920 | tf_op jit(solution)/shard_map/ppermute | solution.py:287
  94.8 12.5 %transport.4 = (bf16[3,8,16,128]{3,2,1,0:T(8,128)(2,1)S(1)}, bf16[3,8,16,128]{3,2,1,0:T(8,128)(2,1)S(1)}, bf16[3,8,16,128]{3,2,1,0:T(8,128)(2,1)S(1)}, bf16[3,8,16,128]{3,2,1,0:T(8,128)(2,1)S(1)}) custom-call(s32[1]{0:T(128)} %bitcast.place_ref, f32[64,3,32,128]{3,2,1,0:T(8,128)S(1)} %copy-done.1, bf16[3,32,16,128]{3,2,1,0:T(8,128)(2,1)} %collective-permute-done.below_ref, ...), custom_call_target="tpu_custom_call" | custom-call | tf_op jit(solution)/shard_map/transport/pallas_call | solution.py:146
  110.2 2.1 %collective-permute-start.14 = (bf16[3,8,16,128]{3,2,1,0:T(8,128)(2,1)S(1)}, bf16[3,8,16,128]{3,2,1,0:T(8,128)(2,1)S(1)}, u32[]{:S(2)}, u32[]{:S(2)}) collective-permute-start(bf16[3,8,16,128]{3,2,1,0:T(8,128)(2,1)S(1)} %get-tuple-element.32), channel_id=1, source_target_pairs={{0,2},{1,3},{2,0},{3,1},{4,6},{5,7},{6,4},{7,5},{8,10},{9,11},{10,... | collective-permute-start | bytes 294920 | tf_op jit(solution)/shard_map/ppermute | solution.py:287
  112.3 2.2 %collective-permute-start.18 = (bf16[3,8,16,128]{3,2,1,0:T(8,128)(2,1)S(1)}, bf16[3,8,16,128]{3,2,1,0:T(8,128)(2,1)S(1)}, u32[]{:S(2)}, u32[]{:S(2)}) collective-permute-start(bf16[3,8,16,128]{3,2,1,0:T(8,128)(2,1)S(1)} %get-tuple-element.36), channel_id=1, source_target_pairs={{0,3},{1,0},{2,1},{3,2},{4,7},{5,4},{6,5},{7,6},{8,11},{9,8},{10,9... | collective-permute-start | bytes 294920 | tf_op jit(solution)/shard_map/ppermute | solution.py:287
  115.6 2.4 %collective-permute-done.19.rest_13_ = bf16[3,8,16,128]{3,2,1,0:T(8,128)(2,1)S(1)} collective-permute-done((bf16[3,8,16,128]{3,2,1,0:T(8,128)(2,1)S(1)}, bf16[3,8,16,128]{3,2,1,0:T(8,128)(2,1)S(1)}, u32[]{:S(2)}, u32[]{:S(2)}) %collective-permute-start.19) | collective-permute-done | bytes 98336 | tf_op jit(solution)/shard_map/ppermute | solution.py:287
  118.0 5.9 %collective-permute-done.14.rest_8_ = bf16[3,8,16,128]{3,2,1,0:T(8,128)(2,1)S(1)} collective-permute-done((bf16[3,8,16,128]{3,2,1,0:T(8,128)(2,1)S(1)}, bf16[3,8,16,128]{3,2,1,0:T(8,128)(2,1)S(1)}, u32[]{:S(2)}, u32[]{:S(2)}) %collective-permute-start.14) | collective-permute-done | bytes 98336 | tf_op jit(solution)/shard_map/ppermute | solution.py:287
  124.0 17.5 %kinetics.1 = (f32[256,3,8,128]{3,2,1,0:T(8,128)}, f32[3,8,128]{2,1,0:T(8,128)S(1)}) custom-call(s32[1]{0:T(128)} %bitcast.place_ref, f32[3,8,128]{2,1,0:T(8,128)S(1)} %copy-done.2, bf16[256,256]{1,0:T(8,128)(2,1)S(1)} %get-tuple-element.22.toeplitz_ref, f32[256,128]{1,0:T(8,128)S(1)} %get-tuple-element.23.column_ref, ...), custom_call_target="tpu_custom_call" | custom-call | tf_op jit(solution)/shard_map/kinetics/pallas_call | solution.py:271
  141.5 13.3 %all_gather.3 = f32[3,32,128]{2,1,0:T(8,128)S(1)} all-gather(f32[3,8,128]{2,1,0:T(8,128)S(1)} %get-tuple-element.41), channel_id=1, replica_groups=mesh['space'=8,'bins'=4] {'bins'}, dimensions={1}, use_global_device_ids=true | all-gather | bytes 61440 | tf_op jit(solution)/shard_map/all_gather | solution.py:348
  (56 shorter events, 22.6 us)
Async XLA Ops:
  0.6 20.8 %collective-permute-start.2 = (bf16[3,3,32,128]{3,2,1,0:T(8,128)(2,1)}, bf16[3,3,32,128]{3,2,1,0:T(8,128)(2,1)S(1)}, u32[]{:S(2)}, u32[]{:S(2)}) collective-permute-start(bf16[3,3,32,128]{3,2,1,0:T(8,128)(2,1)} %param.5), channel_id=1, source_target_pairs={{0,4},{4,8},{8,12},{12,16},{16,20},{20,24},{24,28},{1,5},{5,9},{9,... | collective-permute-start | bytes 221192 | tf_op jit(solution)/shard_map/ppermute | solution.py:287
  2.6 21.8 %collective-permute-start.3 = (bf16[3,3,32,128]{3,2,1,0:T(8,128)(2,1)}, bf16[3,3,32,128]{3,2,1,0:T(8,128)(2,1)S(1)}, u32[]{:S(2)}, u32[]{:S(2)}) collective-permute-start(bf16[3,3,32,128]{3,2,1,0:T(8,128)(2,1)} %param.5), channel_id=1, source_target_pairs={{4,0},{8,4},{12,8},{16,12},{20,16},{24,20},{28,24},{5,1},{9,5},{13... | collective-permute-start | bytes 221192 | tf_op jit(solution)/shard_map/ppermute | solution.py:287
  9.6 21.4 %collective-permute-start.6 = (bf16[3,32,16,128]{3,2,1,0:T(8,128)(2,1)}, bf16[3,32,16,128]{3,2,1,0:T(8,128)(2,1)}, u32[]{:S(2)}, u32[]{:S(2)}) collective-permute-start(bf16[3,32,16,128]{3,2,1,0:T(8,128)(2,1)} %code_slab.6), channel_id=1, source_target_pairs={{0,4},{4,8},{8,12},{12,16},{16,20},{20,24},{24,28},{1,5},{5,9},{9,... | collective-permute-start | bytes 1179656 | tf_op jit(solution)/shard_map/ppermute | solution.py:287
  11.5 21.5 %collective-permute-start.7 = (bf16[3,32,16,128]{3,2,1,0:T(8,128)(2,1)}, bf16[3,32,16,128]{3,2,1,0:T(8,128)(2,1)}, u32[]{:S(2)}, u32[]{:S(2)}) collective-permute-start(bf16[3,32,16,128]{3,2,1,0:T(8,128)(2,1)} %code_slab.6), channel_id=1, source_target_pairs={{4,0},{8,4},{12,8},{16,12},{20,16},{24,20},{28,24},{5,1},{9,5},{13... | collective-permute-start | bytes 1179656 | tf_op jit(solution)/shard_map/ppermute | solution.py:287
  16.6 20.9 %collective-permute-start.8 = (bf16[3,32,16,128]{3,2,1,0:T(8,128)(2,1)}, bf16[3,32,16,128]{3,2,1,0:T(8,128)(2,1)}, u32[]{:S(2)}, u32[]{:S(2)}) collective-permute-start(bf16[3,32,16,128]{3,2,1,0:T(8,128)(2,1)} %code_slab.7), channel_id=1, source_target_pairs={{0,4},{4,8},{8,12},{12,16},{16,20},{20,24},{24,28},{1,5},{5,9},{9,... | collective-permute-start | bytes 1179656 | tf_op jit(solution)/shard_map/ppermute | solution.py:287
  21.5 37.7 %collective-permute-start.9 = (bf16[3,32,16,128]{3,2,1,0:T(8,128)(2,1)}, bf16[3,32,16,128]{3,2,1,0:T(8,128)(2,1)}, u32[]{:S(2)}, u32[]{:S(2)}) collective-permute-start(bf16[3,32,16,128]{3,2,1,0:T(8,128)(2,1)} %code_slab.7), channel_id=1, source_target_pairs={{4,0},{8,4},{12,8},{16,12},{20,16},{24,20},{28,24},{5,1},{9,5},{13... | collective-permute-start | bytes 1179656 | tf_op jit(solution)/shard_map/ppermute | solution.py:287
  24.4 48.9 %collective-permute-start.4 = (bf16[3,32,16,128]{3,2,1,0:T(8,128)(2,1)}, bf16[3,32,16,128]{3,2,1,0:T(8,128)(2,1)}, u32[]{:S(2)}, u32[]{:S(2)}) collective-permute-start(bf16[3,32,16,128]{3,2,1,0:T(8,128)(2,1)} %code_slab.5), channel_id=1, source_target_pairs={{0,4},{4,8},{8,12},{12,16},{16,20},{20,24},{24,28},{1,5},{5,9},{9,... | collective-permute-start | bytes 1179656 | tf_op jit(solution)/shard_map/ppermute | solution.py:287
  31.0 44.0 %collective-permute-start.5 = (bf16[3,32,16,128]{3,2,1,0:T(8,128)(2,1)}, bf16[3,32,16,128]{3,2,1,0:T(8,128)(2,1)}, u32[]{:S(2)}, u32[]{:S(2)}) collective-permute-start(bf16[3,32,16,128]{3,2,1,0:T(8,128)(2,1)} %code_slab.5), channel_id=1, source_target_pairs={{4,0},{8,4},{12,8},{16,12},{20,16},{24,20},{28,24},{5,1},{9,5},{13... | collective-permute-start | bytes 1179656 | tf_op jit(solution)/shard_map/ppermute | solution.py:287
  33.0 55.8 %collective-permute-start = (bf16[3,32,16,128]{3,2,1,0:T(8,128)(2,1)S(1)}, bf16[3,32,16,128]{3,2,1,0:T(8,128)(2,1)}, u32[]{:S(2)}, u32[]{:S(2)}) collective-permute-start(bf16[3,32,16,128]{3,2,1,0:T(8,128)(2,1)S(1)} %code_slab.4), channel_id=1, source_target_pairs={{0,4},{4,8},{8,12},{12,16},{16,20},{20,24},{24,28},{1,5},{5,9},{9,... | collective-permute-start | bytes 1179656 | tf_op jit(solution)/shard_map/ppermute | solution.py:287
  37.5 53.0 %collective-permute-start.1 = (bf16[3,32,16,128]{3,2,1,0:T(8,128)(2,1)S(1)}, bf16[3,32,16,128]{3,2,1,0:T(8,128)(2,1)}, u32[]{:S(2)}, u32[]{:S(2)}) collective-permute-start(bf16[3,32,16,128]{3,2,1,0:T(8,128)(2,1)S(1)} %code_slab.4), channel_id=1, source_target_pairs={{4,0},{8,4},{12,8},{16,12},{20,16},{24,20},{28,24},{5,1},{9,5},{13... | collective-permute-start | bytes 1179656 | tf_op jit(solution)/shard_map/ppermute | solution.py:287
  59.1 33.6 %collective-permute-start.12 = (bf16[3,8,16,128]{3,2,1,0:T(8,128)(2,1)S(1)}, bf16[3,8,16,128]{3,2,1,0:T(8,128)(2,1)S(1)}, u32[]{:S(2)}, u32[]{:S(2)}) collective-permute-start(bf16[3,8,16,128]{3,2,1,0:T(8,128)(2,1)S(1)} %get-tuple-element.30), channel_id=1, source_target_pairs={{0,1},{1,2},{2,3},{3,0},{4,5},{5,6},{6,7},{7,4},{8,9},{9,10},{10,1... | collective-permute-start | bytes 294920 | tf_op jit(solution)/shard_map/ppermute | solution.py:287
  73.3 19.9 %collective-permute-start.13 = (bf16[3,8,16,128]{3,2,1,0:T(8,128)(2,1)S(1)}, bf16[3,8,16,128]{3,2,1,0:T(8,128)(2,1)S(1)}, u32[]{:S(2)}, u32[]{:S(2)}) collective-permute-start(bf16[3,8,16,128]{3,2,1,0:T(8,128)(2,1)S(1)} %get-tuple-element.31), channel_id=1, source_target_pairs={{0,1},{1,2},{2,3},{3,0},{4,5},{5,6},{6,7},{7,4},{8,9},{9,10},{10,1... | collective-permute-start | bytes 294920 | tf_op jit(solution)/shard_map/ppermute | solution.py:287
  74.9 32.3 %collective-permute-start.16 = (bf16[3,8,16,128]{3,2,1,0:T(8,128)(2,1)S(1)}, bf16[3,8,16,128]{3,2,1,0:T(8,128)(2,1)S(1)}, u32[]{:S(2)}, u32[]{:S(2)}) collective-permute-start(bf16[3,8,16,128]{3,2,1,0:T(8,128)(2,1)S(1)} %get-tuple-element.34), channel_id=1, source_target_pairs={{0,2},{1,3},{2,0},{3,1},{4,6},{5,7},{6,4},{7,5},{8,10},{9,11},{10,... | collective-permute-start | bytes 294920 | tf_op jit(solution)/shard_map/ppermute | solution.py:287
  88.7 25.9 %copy-start.4 = (f32[256]{0:T(256)S(1)}, f32[256]{0:T(256)}, u32[]{:S(2)}) copy-start(f32[256]{0:T(256)} %param.7) | copy-start | bytes 3076
  88.7 35.3 %copy-start.2 = (f32[3,8,128]{2,1,0:T(8,128)S(1)}, f32[3,8,128]{2,1,0:T(8,128)}, u32[]{:S(2)}) copy-start(f32[3,8,128]{2,1,0:T(8,128)} %supersat_ref.1) | copy-start | bytes 36868
  88.7 19.4 %collective-permute-start.17 = (bf16[3,8,16,128]{3,2,1,0:T(8,128)(2,1)S(1)}, bf16[3,8,16,128]{3,2,1,0:T(8,128)(2,1)S(1)}, u32[]{:S(2)}, u32[]{:S(2)}) collective-permute-start(bf16[3,8,16,128]{3,2,1,0:T(8,128)(2,1)S(1)} %get-tuple-element.35), channel_id=1, source_target_pairs={{0,2},{1,3},{2,0},{3,1},{4,6},{5,7},{6,4},{7,5},{8,10},{9,11},{10,... | collective-permute-start | bytes 294920 | tf_op jit(solution)/shard_map/ppermute | solution.py:287
  90.5 19.2 %collective-permute-start.20 = (bf16[3,8,16,128]{3,2,1,0:T(8,128)(2,1)S(1)}, bf16[3,8,16,128]{3,2,1,0:T(8,128)(2,1)S(1)}, u32[]{:S(2)}, u32[]{:S(2)}) collective-permute-start(bf16[3,8,16,128]{3,2,1,0:T(8,128)(2,1)S(1)} %get-tuple-element.38), channel_id=1, source_target_pairs={{0,3},{1,0},{2,1},{3,2},{4,7},{5,4},{6,5},{7,6},{8,11},{9,8},{10,9... | collective-permute-start | bytes 294920 | tf_op jit(solution)/shard_map/ppermute | solution.py:287
  92.7 17.5 %collective-permute-start.21 = (bf16[3,8,16,128]{3,2,1,0:T(8,128)(2,1)S(1)}, bf16[3,8,16,128]{3,2,1,0:T(8,128)(2,1)S(1)}, u32[]{:S(2)}, u32[]{:S(2)}) collective-permute-start(bf16[3,8,16,128]{3,2,1,0:T(8,128)(2,1)S(1)} %get-tuple-element.39), channel_id=1, source_target_pairs={{0,3},{1,0},{2,1},{3,2},{4,7},{5,4},{6,5},{7,6},{8,11},{9,8},{10,9... | collective-permute-start | bytes 294920 | tf_op jit(solution)/shard_map/ppermute | solution.py:287
  93.2 19.2 %collective-permute-start.11 = (bf16[3,8,16,128]{3,2,1,0:T(8,128)(2,1)S(1)}, bf16[3,8,16,128]{3,2,1,0:T(8,128)(2,1)S(1)}, u32[]{:S(2)}, u32[]{:S(2)}) collective-permute-start(bf16[3,8,16,128]{3,2,1,0:T(8,128)(2,1)S(1)} %get-tuple-element.29), channel_id=1, source_target_pairs={{0,1},{1,2},{2,3},{3,0},{4,5},{5,6},{6,7},{7,4},{8,9},{9,10},{10,1... | collective-permute-start | bytes 294920 | tf_op jit(solution)/shard_map/ppermute | solution.py:287
  107.3 8.3 %collective-permute-start.15 = (bf16[3,8,16,128]{3,2,1,0:T(8,128)(2,1)S(1)}, bf16[3,8,16,128]{3,2,1,0:T(8,128)(2,1)S(1)}, u32[]{:S(2)}, u32[]{:S(2)}) collective-permute-start(bf16[3,8,16,128]{3,2,1,0:T(8,128)(2,1)S(1)} %get-tuple-element.33), channel_id=1, source_target_pairs={{0,2},{1,3},{2,0},{3,1},{4,6},{5,7},{6,4},{7,5},{8,10},{9,11},{10,... | collective-permute-start | bytes 294920 | tf_op jit(solution)/shard_map/ppermute | solution.py:287
  108.1 9.9 %collective-permute-start.19 = (bf16[3,8,16,128]{3,2,1,0:T(8,128)(2,1)S(1)}, bf16[3,8,16,128]{3,2,1,0:T(8,128)(2,1)S(1)}, u32[]{:S(2)}, u32[]{:S(2)}) collective-permute-start(bf16[3,8,16,128]{3,2,1,0:T(8,128)(2,1)S(1)} %get-tuple-element.37), channel_id=1, source_target_pairs={{0,3},{1,0},{2,1},{3,2},{4,7},{5,4},{6,5},{7,6},{8,11},{9,8},{10,9... | collective-permute-start | bytes 294920 | tf_op jit(solution)/shard_map/ppermute | solution.py:287
  109.7 8.3 %collective-permute-start.10 = (bf16[3,8,16,128]{3,2,1,0:T(8,128)(2,1)S(1)}, bf16[3,8,16,128]{3,2,1,0:T(8,128)(2,1)S(1)}, u32[]{:S(2)}, u32[]{:S(2)}) collective-permute-start(bf16[3,8,16,128]{3,2,1,0:T(8,128)(2,1)S(1)} %get-tuple-element.28), channel_id=1, source_target_pairs={{0,1},{1,2},{2,3},{3,0},{4,5},{5,6},{6,7},{7,4},{8,9},{9,10},{10,1... | collective-permute-start | bytes 294920 | tf_op jit(solution)/shard_map/ppermute | solution.py:287
  110.2 13.7 %collective-permute-start.14 = (bf16[3,8,16,128]{3,2,1,0:T(8,128)(2,1)S(1)}, bf16[3,8,16,128]{3,2,1,0:T(8,128)(2,1)S(1)}, u32[]{:S(2)}, u32[]{:S(2)}) collective-permute-start(bf16[3,8,16,128]{3,2,1,0:T(8,128)(2,1)S(1)} %get-tuple-element.32), channel_id=1, source_target_pairs={{0,2},{1,3},{2,0},{3,1},{4,6},{5,7},{6,4},{7,5},{8,10},{9,11},{10,... | collective-permute-start | bytes 294920 | tf_op jit(solution)/shard_map/ppermute | solution.py:287
  112.3 11.6 %collective-permute-start.18 = (bf16[3,8,16,128]{3,2,1,0:T(8,128)(2,1)S(1)}, bf16[3,8,16,128]{3,2,1,0:T(8,128)(2,1)S(1)}, u32[]{:S(2)}, u32[]{:S(2)}) collective-permute-start(bf16[3,8,16,128]{3,2,1,0:T(8,128)(2,1)S(1)} %get-tuple-element.36), channel_id=1, source_target_pairs={{0,3},{1,0},{2,1},{3,2},{4,7},{5,4},{6,5},{7,6},{8,11},{9,8},{10,9... | collective-permute-start | bytes 294920 | tf_op jit(solution)/shard_map/ppermute | solution.py:287
  (3 other events, 28.4 us)

commit v3 on v1

v3 whole, which is shorter than its diff:
```python
import functools

import jax
import jax.numpy as jnp
from jax import lax
from jax.experimental import pallas as pl
from jax.experimental.pallas import tpu as pltpu
from jax.sharding import PartitionSpec as P

STEPS = 3
KSTEPS = 8

COURANT = 0.3
GROW = 0.4
BETA = 0.5

POWER = 9
SCALE = 256.0
GROUP = 16
VMEM_LIMIT = 32 * 1024 * 1024


def encode(scaled):
    square = scaled * scaled
    fourth = square * square
    return (fourth * fourth * scaled).astype(jnp.bfloat16)


def decode(code):
    wide = code.astype(jnp.float32)
    size = jnp.exp(jnp.log(jnp.abs(wide)) * (1.0 / POWER))
    return jnp.where(wide < 0.0, -size, size)


def params(limit=VMEM_LIMIT):
    return pltpu.CompilerParams(vmem_limit_bytes=limit)


def cost(flops, size):
    return pl.CostEstimate(flops=flops, bytes_accessed=size, transcendentals=0)


def vmem_spec():
    return pl.BlockSpec(memory_space=pltpu.VMEM)


def smem_spec():
    return pl.BlockSpec(memory_space=pltpu.SMEM)


def code_kernel(pop_ref, velocity_ref, all_ref, *group_refs):
    bins = pop_ref.shape[0]
    all_ref[pl.ds(bins, 3)] = velocity_ref[...]
    all_ref[pl.ds(bins + 3, GROUP - 3)] = jnp.zeros(
        (GROUP - 3,) + all_ref.shape[1:], jnp.bfloat16
    )
    group_refs[0][pl.ds(GROUP, 3)] = velocity_ref[...]

    for number, group_ref in enumerate(group_refs):

        def layer(x, carry, number=number, group_ref=group_ref):
            for index in range(0, GROUP, 4):
                code = encode(pop_ref[pl.ds(number * GROUP + index, 4), x] * SCALE)
                all_ref[pl.ds(number * GROUP + index, 4), x] = code
                group_ref[pl.ds(index, 4), x] = code
            return carry

        lax.fori_loop(0, pop_ref.shape[1], layer, 0)


def coded_slab(population, velocity):
    bins = population.shape[0]
    span = population.shape[1:]
    groups = bins // GROUP
    sizes = [bins + GROUP, GROUP + 3] + [GROUP] * (groups - 1)
    return pl.pallas_call(
        code_kernel,
        in_specs=[vmem_spec()] * 2,
        out_specs=[vmem_spec()] * len(sizes),
        out_shape=[jax.ShapeDtypeStruct((size,) + span, jnp.bfloat16) for size in sizes],
        compiler_params=params(),
        cost_estimate=cost(0, 6_000_000),
        name="code_slab",
    )(population, velocity)


def weight_kernel(place_ref, own_ref, inside_ref, outside_ref, coef_ref, vel_ref):
    _, span_x, span_y, span_z = own_ref.shape
    odd = lax.rem(place_ref[1], 2)
    inside = 2 * span_x * (1 - odd)
    for axis in range(3):
        for x in range(span_x):
            vel_ref[axis, inside + x] = inside_ref[axis, x].astype(jnp.float32)
            vel_ref[axis, span_x + x] = own_ref[axis, x].astype(jnp.float32)
            vel_ref[axis, 2 * span_x - inside + x] = outside_ref[GROUP + axis, x].astype(jnp.float32)
    rows = lax.broadcasted_iota(jnp.int32, (span_y, span_z), 0)
    lanes = lax.broadcasted_iota(jnp.int32, (span_y, span_z), 1)

    def layer(x, carry):
        kept_in = jnp.where((x + 1 >= span_x) | (place_ref[1] > 0), 1.0, 0.0)
        scale = COURANT * kept_in
        rise = lambda value: jnp.maximum(value, 0.0) * scale
        fall = lambda value: jnp.minimum(value, 0.0) * (-scale)
        vel_x, next_x = vel_ref[0, x + 1], vel_ref[0, x + 2]
        vel_y, vel_z = vel_ref[1, x + 1], vel_ref[2, x + 1]
        next_y = jnp.where(rows < span_y - 1, pltpu.roll(vel_y, span_y - 1, 0), 0.0)
        next_z = jnp.where(lanes < span_z - 1, pltpu.roll(vel_z, span_z - 1, 1), 0.0)
        coef_ref[0, x] = kept_in - (
            rise(next_x) + fall(vel_x) + rise(next_y) + fall(vel_y) + rise(next_z) + fall(vel_z)
        )
        coef_ref[1, x] = rise(vel_x)
        coef_ref[2, x] = fall(next_x)
        coef_ref[3, x] = rise(vel_y)
        coef_ref[4, x] = fall(next_y)
        coef_ref[5, x] = jnp.where(lanes > 0, rise(vel_z), 0.0)
        coef_ref[6, x] = fall(next_z)
        return carry

    lax.fori_loop(0, coef_ref.shape[1], layer, 0)


def weights(place, velocity, inside, outside):
    span = velocity.shape[1:]
    whole = lambda shape: pl.BlockSpec(shape, lambda i: (0, 0, 0, 0))
    tail = inside.shape[0] // GROUP - 1
    return pl.pallas_call(
        weight_kernel,
        grid=(1,),
        in_specs=[
            smem_spec(),
            whole(velocity.shape),
            pl.BlockSpec((GROUP,) + span, lambda i: (tail, 0, 0, 0)),
            whole(outside.shape),
        ],
        out_specs=whole((7, 3 * span[0] - 2) + span[1:]),
        out_shape=jax.ShapeDtypeStruct((7, 3 * span[0] - 2) + span[1:], jnp.float32),
        scratch_shapes=[pltpu.VMEM((3, 3 * span[0]) + span[1:], jnp.float32)],
        compiler_params=params(),
        cost_estimate=cost(0, 4_000_000),
        name="weights",
    )(place, velocity, inside, outside)


RIM = 8


def transport_kernel(batches, place_ref, pop_ref, inside_ref, outside_ref, coef_ref, *rest):
    *outs, first, second, third, last = rest[-batches - 4 :]
    _, span_x, span_y, span_z = pop_ref.shape
    bins = GROUP
    zeros = jnp.zeros((bins, RIM, span_z), jnp.float32)
    for ref in (first, second, third):
        for x in range(ref.shape[0]):
            ref[x, :, pl.ds(0, RIM)] = zeros
            ref[x, :, pl.ds(RIM + span_y, RIM)] = zeros
    inside = 2 * span_x * (1 - lax.rem(place_ref[1], 2))
    body = pl.ds(RIM, span_y)

    def fill(x, carry):
        for index in range(bins):
            first[inside + x, index, body] = decode(inside_ref[index, x])
            first[span_x + x, index, body] = pop_ref[index, x] * SCALE
            first[2 * span_x - inside + x, index, body] = decode(outside_ref[index, x])
        return carry

    lax.fori_loop(0, span_x, fill, 0)

    for src, dst, shift, rim in (
        (first, second, 0, RIM),
        (second, third, 1, RIM),
        (third, last, 2, 0),
    ):

        def layer(x, carry, src=src, dst=dst, shift=shift, rim=rim):
            for y in range(0, span_y, 8):
                here, down, up = (pl.ds(RIM + y + by, 8) for by in (0, -1, 1))
                weight = [coef_ref[k, x + shift, pl.ds(y, 8)] for k in range(7)]
                for index in range(bins):
                    centre = src[x + 1, index, here]
                    total = weight[0] * centre
                    total += weight[1] * src[x, index, here]
                    total += weight[2] * src[x + 2, index, here]
                    total += weight[3] * src[x + 1, index, down]
                    total += weight[4] * src[x + 1, index, up]
                    total += weight[5] * pltpu.roll(centre, 1, 1)
                    total += weight[6] * pltpu.roll(centre, span_z - 1, 1)
                    dst[x, index, pl.ds(rim + y, 8)] = total
            return carry

        lax.fori_loop(0, dst.shape[0], layer, 0)
    span_out = span_y // batches
    rows = last.reshape(span_x * bins * span_y, span_z)
    for ahead in range(batches):
        begin = lax.bitwise_xor(place_ref[0], ahead) * span_out
        for x in range(span_x):
            for y in range(span_out):
                at = x * bins * span_y + begin + y
                outs[ahead][x, y] = encode(rows[pl.ds(at, bins, stride=span_y), :])


def transported(place, population, inside, outside, coefs, group, batches, after):
    _, span_x, span_y, span_z = population.shape
    out = (span_x, span_y // batches, GROUP, span_z)
    block = (GROUP, span_x, span_y, span_z)
    at = lambda shape, start: pl.BlockSpec(shape, lambda i: (start, 0, 0, 0))
    return pl.pallas_call(
        functools.partial(transport_kernel, batches),
        grid=(1,),
        in_specs=[smem_spec(), at(block, group), at(block, group), at(block, 0), at(coefs.shape, 0)]
        + [pl.BlockSpec(memory_space=pl.ANY)] * len(after),
        out_specs=[at(out, 0)] * batches,
        out_shape=[jax.ShapeDtypeStruct(out, jnp.bfloat16)] * batches,
        scratch_shapes=[
            pltpu.VMEM((depth, GROUP, span_y + 2 * RIM, span_z), jnp.float32)
            for depth in (3 * span_x, 3 * span_x - 2, 3 * span_x - 4)
        ]
        + [pltpu.VMEM((span_x, GROUP, span_y, span_z), jnp.float32)],
        compiler_params=params(),
        cost_estimate=cost(0, 18_000_000),
        name="transport",
    )(place, population, inside, outside, coefs, *after)


def bins_of_rows(shape, dim):
    count = shape[dim]
    row = lax.broadcasted_iota(jnp.int32, shape, dim)
    return (row % 8) * (count // 8) + row // 8


def table_kernel(kernel_ref, toeplitz_ref, column_ref):
    bin_count = toeplitz_ref.shape[0]
    square = (bin_count, bin_count)
    wide = jnp.broadcast_to(kernel_ref[...], (bin_count, 2 * bin_count))
    turned = pltpu.roll(wide, 0, 1, stride=1, stride_axis=0)[:, :bin_count]
    column = jnp.broadcast_to(jnp.sum(turned, axis=1, keepdims=True), column_ref.shape)
    plain = turned.T.astype(jnp.bfloat16)
    other = lax.broadcasted_iota(jnp.int32, square, 1)
    moves = jnp.where(bins_of_rows(square, 0) == other, 1.0, 0.0)
    exact = functools.partial(
        jnp.dot, preferred_element_type=jnp.float32, precision=lax.Precision.HIGHEST
    )
    column_ref[...] = exact(moves, column) + GROW / BETA
    moves = moves.astype(jnp.bfloat16)
    half = jnp.dot(moves, plain, preferred_element_type=jnp.float32).astype(jnp.bfloat16)
    toeplitz_ref[...] = jnp.dot(half, moves.T, preferred_element_type=jnp.float32).astype(
        jnp.bfloat16
    )


def tables(kernel):
    bin_count = kernel.shape[0]
    return pl.pallas_call(
        table_kernel,
        in_specs=[vmem_spec()],
        out_specs=[vmem_spec()] * 2,
        out_shape=[
            jax.ShapeDtypeStruct((bin_count, bin_count), jnp.bfloat16),
            jax.ShapeDtypeStruct((bin_count, 128), jnp.float32),
        ],
        compiler_params=params(),
        name="tables",
    )(jnp.concatenate([kernel, jnp.zeros_like(kernel)])[None, :])


def kinetics_kernel(
    batches, groups, layer, native, chained, place_ref, supersat_ref, toeplitz_ref, column_ref, *rest
):
    parts = rest[: batches * groups]
    out_ref, depletion_ref, initial, state, product, rounded = rest[batches * groups + chained :]
    bin_count, width = state.shape
    span_y, span_z = supersat_ref.shape[1:]
    run = bin_count // 8
    block = min(width, 2 * span_z)
    for back in range(batches):
        source = lax.bitwise_xor(place_ref[0], back) * (groups * GROUP)
        for index in range(groups):
            part = parts[back * groups + index]
            begin = source + index * GROUP
            at = lax.rem(begin, run) * 8 + begin // run
            for y in range(span_y):
                value = decode(part[layer, y]) * (1.0 / SCALE)
                initial[pl.ds(y * bin_count + at, GROUP, stride=8), :] = value
    for y in range(span_y):
        cells = slice(y * span_z, (y + 1) * span_z)
        for row in range(0, bin_count, 16):
            value = initial[pl.ds(y * bin_count + row, 16), :]
            state[pl.ds(row, 16), cells] = value
            rounded[pl.ds(row, 16), cells] = value.astype(jnp.bfloat16)

    eighth = lax.broadcasted_iota(jnp.int32, (8, span_z), 0)

    def multiply(begin):
        cells = slice(begin, begin + block)
        product[:, cells] = jnp.dot(
            toeplitz_ref[...], rounded[:, cells], preferred_element_type=jnp.float32
        )

    def advance(begin):
        lanes = [slice(lane, lane + span_z) for lane in range(begin, begin + block, span_z)]
        speeds, lowers = [], []
        for cells in lanes:
            row = supersat_ref[layer, pl.ds(cells.start // span_z, 1), :]
            speeds.append(BETA * jnp.broadcast_to(row, (8, span_z)))
            last = state[pl.ds(bin_count - 8, 8), cells]
            lowers.append(jnp.where(eighth > 0, pltpu.roll(last, 1, 0), 0.0))
        for row in range(0, bin_count, 16):
            pairs = [[] for _ in lanes]
            for at in (pl.ds(row, 8), pl.ds(row + 8, 8)):
                column = column_ref[at, :]
                for index, cells in enumerate(lanes):
                    now = state[at, cells]
                    change = (GROW / BETA) * lowers[index] - column * now
                    new = now + speeds[index] * (change + product[at, cells])
                    state[at, cells] = new
                    pairs[index].append(new)
                    lowers[index] = now
            for pair, cells in zip(pairs, lanes):
                rounded[pl.ds(row, 16), cells] = jnp.concatenate(pair, axis=0).astype(
                    jnp.bfloat16
                )

    def substep(index, carry):
        begins = list(range(0, width, block))
        multiply(begins[0])
        for begin, following in zip(begins, begins[1:] + [None]):
            if following is not None:
                multiply(following)
            advance(begin)
        return carry

    lax.fori_loop(0, KSTEPS, substep, 0)
    ratio = (bins_of_rows((bin_count, span_z), 0).astype(jnp.float32) + 1.0) / bin_count
    masses = ratio * ratio * ratio
    for y in range(span_y):
        cells = slice(y * span_z, (y + 1) * span_z)
        final = state[:, cells]
        depletion_ref[0, pl.ds(y, 1), :] = jnp.sum(
            masses * (final - initial[pl.ds(y * bin_count, bin_count), :]), axis=0, keepdims=True
        )
        if native:
            rows = out_ref.reshape(bin_count * span_y, span_z)
        for row in range(run):
            value = state[pl.ds(8 * row, 8), cells]
            if native:
                rows[pl.ds(row * span_y + y, 8, stride=run * span_y), :] = value
            else:
                out_ref[0, y, pl.ds(row, 8, stride=run), :] = value


def kinetics(place, supersat, toeplitz, column, parts, layer, batches, chain):
    span_x, span_y, span_z = supersat.shape
    bin_count = toeplitz.shape[0]
    native = span_y % 8 == 0
    whole = pl.BlockSpec(memory_space=pltpu.VMEM)
    if native:
        out_shape = (bin_count, span_x, span_y, span_z)
        out_spec = pl.BlockSpec((bin_count, 1, span_y, span_z), lambda i: (0, layer, 0, 0))
    else:
        out_shape = (span_x, span_y, bin_count, span_z)
        out_spec = pl.BlockSpec((1,) + out_shape[1:], lambda i: (layer, 0, 0, 0))
    chained = 0 if chain is None else 1
    return pl.pallas_call(
        functools.partial(kinetics_kernel, batches, len(parts) // batches, layer, native, chained),
        grid=(1,),
        in_specs=[smem_spec()]
        + [whole] * (3 + len(parts))
        + [pl.BlockSpec(memory_space=pl.ANY)] * chained,
        out_specs=[out_spec, whole],
        out_shape=[
            jax.ShapeDtypeStruct(out_shape, jnp.float32),
            jax.ShapeDtypeStruct((1, span_y, span_z), jnp.float32),
        ],
        scratch_shapes=[
            pltpu.VMEM((bin_count * span_y, span_z), jnp.float32),
            pltpu.VMEM((bin_count, span_y * span_z), jnp.float32),
            pltpu.VMEM((bin_count, span_y * span_z), jnp.float32),
            pltpu.VMEM((bin_count, span_y * span_z), jnp.bfloat16),
        ],
        input_output_aliases={4 + len(parts): 0} if chained else {},
        compiler_params=params(),
        cost_estimate=cost(0, 22_000_000),
        name="kinetics",
    )(place, supersat, toeplitz, column, *parts, *([chain] if chained else []))


def assemble_kernel(batches, place_ref, *refs):
    *parts, out_ref = refs
    for back in range(batches):
        source = lax.bitwise_xor(place_ref[0], back)
        for layer in range(out_ref.shape[0]):
            out_ref[layer, source] = parts[back][layer]


def assembled(place, parts, batches):
    span_x, span_y, span_z = parts[0].shape
    out = pl.pallas_call(
        functools.partial(assemble_kernel, batches),
        in_specs=[pl.BlockSpec(memory_space=pltpu.SMEM)] + [vmem_spec()] * batches,
        out_specs=vmem_spec(),
        out_shape=jax.ShapeDtypeStruct((span_x, batches, span_y, span_z), jnp.float32),
        compiler_params=params(),
        name="assemble",
    )(place, *parts)
    return out.reshape(span_x, batches * span_y, span_z)


def swapped(array, axis, partner):
    count = lax.axis_size(axis)
    pairs = [(i, partner(i)) for i in range(count) if 0 <= partner(i) < count]
    return lax.ppermute(array, axis, pairs)


def with_partner(array):
    return swapped(array, "space", lambda i: i ^ 1)


def with_other(array):
    return swapped(array, "space", lambda i: ((i + 1) ^ 1) - 1)


def body(population, velocity, supersat, kernel):
    batches = lax.axis_size("bins")
    span_x = population.shape[1]
    place = jnp.stack([lax.axis_index("bins"), lax.axis_index("space")]).astype(jnp.int32)
    toeplitz, column = tables(kernel)
    codes, *groups = coded_slab(population, velocity)
    inside = with_partner(codes)
    outside = [with_other(group) for group in groups]
    coefs = weights(place, velocity, inside, outside[0])
    parts = [[] for _ in range(batches)]
    moved = []
    for group in range(len(groups)):
        after = list(moved[:1]) + ([row[group - 2] for row in parts[1:]] if group > 1 else [])
        moved = transported(
            place, population, inside, outside[group], coefs, group, batches, after
        )
        for ahead, array in enumerate(moved):
            if ahead:
                array = swapped(array, "bins", lambda i: i ^ ahead)
            parts[ahead].append(array)
    flat = [part for row in parts for part in row]
    out, depletions = None, []
    for layer in range(span_x):
        out, depletion = kinetics(
            place, supersat, toeplitz, column, flat, layer, batches, out
        )
        depletions.append(depletion)
    if not supersat.shape[1] % 8 == 0:
        out = jnp.transpose(out, (2, 0, 1, 3))
    own = jnp.concatenate(depletions, axis=0)
    others = [own] + [swapped(own, "bins", lambda i: i ^ ahead) for ahead in range(1, batches)]
    return (out, assembled(place, others, batches))


def solution(mesh):
    in_specs = (
        P("bins", "space", None, None),
        P(None, "space", None, None),
        P("space", "bins", None),
        P(),
    )
    out_specs = (P(None, "space", "bins", None), P("space", None, None))
    return jax.shard_map(body, mesh=mesh, in_specs=in_specs, out_specs=out_specs, check_vma=False)
```

time: 207 us -> 96.8 us (0.47)
  waiting for transfers between devices: 120 us -> 11.2 us
  Pallas kernels: 0 us -> 46.1 us
  other arithmetic: 18.7 us -> 0.08 us
  local copies, waits for them, and re-layouts: 18.4 us -> 3.68 us
  blocking collectives: 13.1 us -> 0 us
  matrix products: 10.7 us -> 0 us
  starting transfers between devices: 24.3 us -> 34.4 us
    all_to_all x1 -> x0, waiting for transfers between devices: 63.8 us -> none  [body(): lax.all_to_all(density, 'bins', split_axis=2, concat_axis=0, tiled=True)]
    pallas_call x0 -> x11, Pallas kernels: none -> 46.1 us  [the longest x4 21.8 us: transported(): pl.pallas_call(functools.partial(transport_kernel, batches), grid=(1,), i...]
    ppermute x7 -> x20, waiting for transfers between devices: 56.1 us -> 11.2 us  [swapped(): return lax.ppermute(array, axis, pairs)]
    ppermute x7 -> x20, starting transfers between devices: 19.3 us -> 34.4 us  [swapped(): return lax.ppermute(array, axis, pairs)]
    all_gather x1 -> x0, blocking collectives: 13.1 us -> none  [body(): lax.all_gather(depletion.reshape(supersat.shape), 'bins', axis=1, tiled=T...]
    dot_general x8 -> x0, matrix products: 10.7 us -> none  [kinetics(): jnp.dot(toeplitz, columns.astype(jnp.bfloat16), preferred_element_type=jn...]
    add x9 -> x0, other arithmetic: 9.59 us -> none  [the longest x3 5.07 us: advance(): jnp.maximum(vel_z, 0.0) * padded_z[..., 0:count_z + 1]]
    sub x3 -> x0, other arithmetic: 5.7 us -> none  [advance(): return centre - COURANT * outflow]
  transfers between devices with their start and end apart: 8 -> 20, of which waited for: 7 -> 6; matrix products, arithmetic and copies ran while one was open for 5% -> 0% of each run, Pallas kernels for 0% -> 25%
where the time goes in v3:
time: 96.8 us; the launch traced here: 96.1 us
  Pallas kernels  46.1 us (48%)
  starting transfers between devices  34.4 us (36%)
  waiting for transfers between devices  11.2 us (12%)
  local copies, waits for them, and re-layouts  3.68 us (4%)
    ppermute x20, starting transfers between devices, swapped(): return lax.ppermute(array, axis, pairs)  34.4 us
    pallas_call x4, Pallas kernels, transported(): pl.pallas_call(functools.partial(transport_kernel, batches), grid=(1,), i...  21.8 us
    pallas_call x3, Pallas kernels, kinetics(): pl.pallas_call(functools.partial(kinetics_kernel, batches, len(parts) //...  18.2 us
    ppermute x20, waiting for transfers between devices, swapped(): return lax.ppermute(array, axis, pairs)  11.2 us
    unnamed x14, local copies, waits for them, and re-layouts  3.67 us
    pallas_call x1, Pallas kernels, coded_slab(): pl.pallas_call(code_kernel, in_specs=[vmem_spec()] * 2, out_specs=[vmem_s...  2.48 us
  transfers between devices with their start and end apart: 20, of which 6 were waited for; matrix products, arithmetic and copies ran while one was open for 0% of the time, Pallas kernels for 25%

profile of v3, /device:TPU:2, one launch (start us, length us, event | category | flops | bytes accessed | tf_op | source)
XLA Modules:
  0.0 96.1 jit_solution(3163819906084292041)
XLA Ops:
  0.6 1.9 %copy-done = f32[64,3,32,128]{3,2,1,0:T(8,128)S(1)} copy-done((f32[64,3,32,128]{3,2,1,0:T(8,128)S(1)}, f32[64,3,32,128]{3,2,1,0:T(8,128)}, u32[]{:S(2)}) %copy-start) | copy-done | bytes 3145752
  3.4 2.5 %code_slab.1 = (bf16[80,3,32,128]{3,2,1,0:T(8,128)(2,1)}, bf16[19,3,32,128]{3,2,1,0:T(8,128)(2,1)}, bf16[16,3,32,128]{3,2,1,0:T(8,128)(2,1)}, bf16[16,3,32,128]{3,2,1,0:T(8,128)(2,1)}, bf16[16,3,32,128]{3,2,1,0:T(8,128)(2,1)}) custom-call(f32[64,3,32,128]{3,2,1,0:T(8,128)S(1)} %copy-done, bf16[3,3,32,128]{3,2,1,0:T(8,128)(2,1)S(1)} %copy-done.2), custom_call_target="tpu_custom_call" | custom-call | bytes 6000000 | tf_op jit(solution)/shard_map/code_slab/pallas_call | solution.py:76
  5.9 1.9 %collective-permute-start.1 = (bf16[19,3,32,128]{3,2,1,0:T(8,128)(2,1)}, bf16[19,3,32,128]{3,2,1,0:T(8,128)(2,1)}, u32[]{:S(2)}, u32[]{:S(2)}) collective-permute-start(bf16[19,3,32,128]{3,2,1,0:T(8,128)(2,1)} %get-tuple-element.34), channel_id=1, source_target_pairs={{4,8},{8,4},{12,16},{16,12},{20,24},{24,20},{5,9},{9,5},{13,17},{1... | collective-permute-start | bytes 1400840 | tf_op jit(solution)/shard_map/ppermute | solution.py:410
  7.8 3.6 %collective-permute-start.2 = (bf16[16,3,32,128]{3,2,1,0:T(8,128)(2,1)}, bf16[16,3,32,128]{3,2,1,0:T(8,128)(2,1)S(1)}, u32[]{:S(2)}, u32[]{:S(2)}) collective-permute-start(bf16[16,3,32,128]{3,2,1,0:T(8,128)(2,1)} %get-tuple-element.36), channel_id=1, source_target_pairs={{4,8},{8,4},{12,16},{16,12},{20,24},{24,20},{5,9},{9,5},{13,17},{1... | collective-permute-start | bytes 1179656 | tf_op jit(solution)/shard_map/ppermute | solution.py:410
  11.5 1.9 %collective-permute-start.3 = (bf16[16,3,32,128]{3,2,1,0:T(8,128)(2,1)}, bf16[16,3,32,128]{3,2,1,0:T(8,128)(2,1)}, u32[]{:S(2)}, u32[]{:S(2)}) collective-permute-start(bf16[16,3,32,128]{3,2,1,0:T(8,128)(2,1)} %get-tuple-element.38), channel_id=1, source_target_pairs={{4,8},{8,4},{12,16},{16,12},{20,24},{24,20},{5,9},{9,5},{13,17},{1... | collective-permute-start | bytes 1179656 | tf_op jit(solution)/shard_map/ppermute | solution.py:410
  13.4 3.6 %collective-permute-start.7 = (bf16[16,3,32,128]{3,2,1,0:T(8,128)(2,1)}, bf16[16,3,32,128]{3,2,1,0:T(8,128)(2,1)}, u32[]{:S(2)}, u32[]{:S(2)}) collective-permute-start(bf16[16,3,32,128]{3,2,1,0:T(8,128)(2,1)} %get-tuple-element.43), channel_id=1, source_target_pairs={{4,8},{8,4},{12,16},{16,12},{20,24},{24,20},{5,9},{9,5},{13,17},{1... | collective-permute-start | bytes 1179656 | tf_op jit(solution)/shard_map/ppermute | solution.py:410
  17.1 1.2 %collective-permute-done.1.outside_ref = bf16[19,3,32,128]{3,2,1,0:T(8,128)(2,1)} collective-permute-done((bf16[19,3,32,128]{3,2,1,0:T(8,128)(2,1)}, bf16[19,3,32,128]{3,2,1,0:T(8,128)(2,1)}, u32[]{:S(2)}, u32[]{:S(2)}) %collective-permute-start.1) | collective-permute-done | bytes 466976 | tf_op jit(solution)/shard_map/ppermute | solution.py:410
  19.2 1.7 %weights.1.coef_ref = f32[7,7,32,128]{3,2,1,0:T(8,128)S(1)} custom-call(s32[2]{0:T(128)S(1)} %pad_add_fusion.place_ref, bf16[3,3,32,128]{3,2,1,0:T(8,128)(2,1)S(1)} %copy-done.3, bf16[80,3,32,128]{3,2,1,0:T(8,128)(2,1)} %collective-permute-done.inside_ref, bf16[19,3,32,128]{3,2,1,0:T(8,128)(2,1)} %collective-permute-done.1.outside_ref), custom_call_target="tpu_custom_call" | custom-call | bytes 4000000 | tf_op jit(solution)/shard_map/weights/pallas_call | solution.py:126
  20.9 5.5 %transport.4 = (bf16[3,8,16,128]{3,2,1,0:T(8,128)(2,1)S(1)}, bf16[3,8,16,128]{3,2,1,0:T(8,128)(2,1)S(1)}, bf16[3,8,16,128]{3,2,1,0:T(8,128)(2,1)S(1)}, bf16[3,8,16,128]{3,2,1,0:T(8,128)(2,1)S(1)}) custom-call(s32[2]{0:T(128)S(1)} %pad_add_fusion.place_ref, f32[64,3,32,128]{3,2,1,0:T(8,128)S(1)} %copy-done.1, ...), custom_call_target="tpu_custom_call" | custom-call | bytes 18000000 | tf_op jit(solution)/shard_map/transport/pallas_call | solution.py:206
  26.4 2.9 %collective-permute-start.4 = (bf16[3,8,16,128]{3,2,1,0:T(8,128)(2,1)S(1)}, bf16[3,8,16,128]{3,2,1,0:T(8,128)(2,1)S(1)}, u32[]{:S(2)}, u32[]{:S(2)}) collective-permute-start(bf16[3,8,16,128]{3,2,1,0:T(8,128)(2,1)S(1)} %get-tuple-element.39), channel_id=1, source_target_pairs={{0,1},{1,0},{2,3},{3,2},{4,5},{5,4},{6,7},{7,6},{8,9},{9,8},{10,11... | collective-permute-start | bytes 294920 | tf_op jit(solution)/shard_map/ppermute | solution.py:410
  29.3 2.6 %collective-permute-start.5 = (bf16[3,8,16,128]{3,2,1,0:T(8,128)(2,1)S(1)}, bf16[3,8,16,128]{3,2,1,0:T(8,128)(2,1)S(1)}, u32[]{:S(2)}, u32[]{:S(2)}) collective-permute-start(bf16[3,8,16,128]{3,2,1,0:T(8,128)(2,1)S(1)} %get-tuple-element.40), channel_id=1, source_target_pairs={{0,2},{1,3},{2,0},{3,1},{4,6},{5,7},{6,4},{7,5},{8,10},{9,11},{10,... | collective-permute-start | bytes 294920 | tf_op jit(solution)/shard_map/ppermute | solution.py:410
  31.9 5.4 %transport.5 = (bf16[3,8,16,128]{3,2,1,0:T(8,128)(2,1)S(1)}, bf16[3,8,16,128]{3,2,1,0:T(8,128)(2,1)S(1)}, bf16[3,8,16,128]{3,2,1,0:T(8,128)(2,1)S(1)}, bf16[3,8,16,128]{3,2,1,0:T(8,128)(2,1)S(1)}) custom-call(s32[2]{0:T(128)S(1)} %pad_add_fusion.place_ref, f32[64,3,32,128]{3,2,1,0:T(8,128)S(1)} %copy-done.1, ...), custom_call_target="tpu_custom_call" | custom-call | bytes 18000000 | tf_op jit(solution)/shard_map/transport/pallas_call | solution.py:206
  38.2 3.5 %collective-permute-start.9 = (bf16[3,8,16,128]{3,2,1,0:T(8,128)(2,1)S(1)}, bf16[3,8,16,128]{3,2,1,0:T(8,128)(2,1)S(1)}, u32[]{:S(2)}, u32[]{:S(2)}) collective-permute-start(bf16[3,8,16,128]{3,2,1,0:T(8,128)(2,1)S(1)} %get-tuple-element.45), channel_id=1, source_target_pairs={{0,2},{1,3},{2,0},{3,1},{4,6},{5,7},{6,4},{7,5},{8,10},{9,11},{10,... | collective-permute-start | bytes 294920 | tf_op jit(solution)/shard_map/ppermute | solution.py:410
  41.7 5.5 %transport.6 = (bf16[3,8,16,128]{3,2,1,0:T(8,128)(2,1)S(1)}, bf16[3,8,16,128]{3,2,1,0:T(8,128)(2,1)S(1)}, bf16[3,8,16,128]{3,2,1,0:T(8,128)(2,1)S(1)}, bf16[3,8,16,128]{3,2,1,0:T(8,128)(2,1)S(1)}) custom-call(s32[2]{0:T(128)S(1)} %pad_add_fusion.place_ref, f32[64,3,32,128]{3,2,1,0:T(8,128)S(1)} %copy-done.1, ...), custom_call_target="tpu_custom_call" | custom-call | bytes 18000000 | tf_op jit(solution)/shard_map/transport/pallas_call | solution.py:206
  47.9 3.8 %collective-permute-start.13 = (bf16[3,8,16,128]{3,2,1,0:T(8,128)(2,1)S(1)}, bf16[3,8,16,128]{3,2,1,0:T(8,128)(2,1)S(1)}, u32[]{:S(2)}, u32[]{:S(2)}) collective-permute-start(bf16[3,8,16,128]{3,2,1,0:T(8,128)(2,1)S(1)} %get-tuple-element.50), channel_id=1, source_target_pairs={{0,2},{1,3},{2,0},{3,1},{4,6},{5,7},{6,4},{7,5},{8,10},{9,11},{10,... | collective-permute-start | bytes 294920 | tf_op jit(solution)/shard_map/ppermute | solution.py:410
  51.7 5.5 %transport.7 = (bf16[3,8,16,128]{3,2,1,0:T(8,128)(2,1)S(1)}, bf16[3,8,16,128]{3,2,1,0:T(8,128)(2,1)S(1)}, bf16[3,8,16,128]{3,2,1,0:T(8,128)(2,1)S(1)}, bf16[3,8,16,128]{3,2,1,0:T(8,128)(2,1)S(1)}) custom-call(s32[2]{0:T(128)S(1)} %pad_add_fusion.place_ref, f32[64,3,32,128]{3,2,1,0:T(8,128)S(1)} %copy-done.1, ...), custom_call_target="tpu_custom_call" | custom-call | bytes 18000000 | tf_op jit(solution)/shard_map/transport/pallas_call | solution.py:206
  57.9 3.8 %collective-permute-start.14 = (bf16[3,8,16,128]{3,2,1,0:T(8,128)(2,1)S(1)}, bf16[3,8,16,128]{3,2,1,0:T(8,128)(2,1)S(1)}, u32[]{:S(2)}, u32[]{:S(2)}) collective-permute-start(bf16[3,8,16,128]{3,2,1,0:T(8,128)(2,1)S(1)} %get-tuple-element.51), channel_id=1, source_target_pairs={{0,2},{1,3},{2,0},{3,1},{4,6},{5,7},{6,4},{7,5},{8,10},{9,11},{10,... | collective-permute-start | bytes 294920 | tf_op jit(solution)/shard_map/ppermute | solution.py:410
  62.6 6.8 %collective-permute-done.14.rest_11_ = bf16[3,8,16,128]{3,2,1,0:T(8,128)(2,1)S(1)} collective-permute-done((bf16[3,8,16,128]{3,2,1,0:T(8,128)(2,1)S(1)}, bf16[3,8,16,128]{3,2,1,0:T(8,128)(2,1)S(1)}, u32[]{:S(2)}, u32[]{:S(2)}) %collective-permute-start.14) | collective-permute-done | bytes 98336 | tf_op jit(solution)/shard_map/ppermute | solution.py:410
  69.4 6.1 %kinetics.3 = (f32[256,3,8,128]{3,2,1,0:T(8,128)}, f32[1,8,128]{2,1,0:T(8,128)S(1)}) custom-call(s32[2]{0:T(128)S(1)} %pad_add_fusion.place_ref, f32[3,8,128]{2,1,0:T(8,128)S(1)} %copy-done.4, bf16[256,256]{1,0:T(8,128)(2,1)S(1)} %get-tuple-element.31.toeplitz_ref, f32[256,128]{1,0:T(8,128)S(1)} %get-tuple-element.32.column_ref, ...), custom_call_target="tpu_custom_call" | custom-call | bytes 22000000 | tf_op jit(solution)/shard_map/kinetics/pallas_call | solution.py:362
  75.5 6.1 %kinetics.4 = (f32[256,3,8,128]{3,2,1,0:T(8,128)}, f32[1,8,128]{2,1,0:T(8,128)S(1)}) custom-call(s32[2]{0:T(128)S(1)} %pad_add_fusion.place_ref, f32[3,8,128]{2,1,0:T(8,128)S(1)} %copy-done.4, bf16[256,256]{1,0:T(8,128)(2,1)S(1)} %get-tuple-element.31.toeplitz_ref, f32[256,128]{1,0:T(8,128)S(1)} %get-tuple-element.32.column_ref, ...), custom_call_target="tpu_custom_call", output_to_operand_aliasing={{0}: (20, {})} | custom-call | bytes 22000000 | tf_op jit(solution)/shard_map/kinetics/pallas_call | solution.py:362
  81.6 6.1 %kinetics.5 = (f32[256,3,8,128]{3,2,1,0:T(8,128)}, f32[1,8,128]{2,1,0:T(8,128)S(1)}) custom-call(s32[2]{0:T(128)S(1)} %pad_add_fusion.place_ref, f32[3,8,128]{2,1,0:T(8,128)S(1)} %copy-done.4, bf16[256,256]{1,0:T(8,128)(2,1)S(1)} %get-tuple-element.31.toeplitz_ref, f32[256,128]{1,0:T(8,128)S(1)} %get-tuple-element.32.column_ref, ...), custom_call_target="tpu_custom_call", output_to_operand_aliasing={{0}: (20, {})} | custom-call | bytes 22000000 | tf_op jit(solution)/shard_map/kinetics/pallas_call | solution.py:362
  87.7 2.5 %collective-permute-start.19 = (f32[3,8,128]{2,1,0:T(8,128)S(1)}, f32[3,8,128]{2,1,0:T(8,128)S(1)}, u32[]{:S(2)}, u32[]{:S(2)}) collective-permute-start(f32[3,8,128]{2,1,0:T(8,128)S(1)} %constant_dynamic-update-slice_fusion.refs_0_), channel_id=1, source_target_pairs={{0,3},{1,2},{2,1},{3,0},{4,7},{5,6},{6,5},{7,4},{8,11},{9,10},{10,... | collective-permute-start | bytes 36872 | tf_op jit(solution)/shard_map/ppermute | solution.py:410
  93.2 1.6 %collective-permute-done.18.refs_2_ = f32[3,8,128]{2,1,0:T(8,128)S(1)} collective-permute-done((f32[3,8,128]{2,1,0:T(8,128)S(1)}, f32[3,8,128]{2,1,0:T(8,128)S(1)}, u32[]{:S(2)}, u32[]{:S(2)}) %collective-permute-start.18) | collective-permute-done | bytes 12320 | tf_op jit(solution)/shard_map/ppermute | solution.py:410
  94.9 1.2 %assemble.1 = f32[3,4,8,128]{3,2,1,0:T(8,128)} custom-call(s32[2]{0:T(128)S(1)} %pad_add_fusion.place_ref, f32[3,8,128]{2,1,0:T(8,128)S(1)} %constant_dynamic-update-slice_fusion.refs_0_, f32[3,8,128]{2,1,0:T(8,128)S(1)} %collective-permute-done.17.refs_1_, f32[3,8,128]{2,1,0:T(8,128)S(1)} %collective-permute-done.18.refs_2_, ...), custom_call_target="tpu_custom_call" | custom-call | tf_op jit(solution)/shard_map/assemble/pallas_call | solution.py:396
  (44 shorter events, 8.4 us)
Async XLA Ops:
  0.6 1.9 %copy-start = (f32[64,3,32,128]{3,2,1,0:T(8,128)S(1)}, f32[64,3,32,128]{3,2,1,0:T(8,128)}, u32[]{:S(2)}) copy-start(f32[64,3,32,128]{3,2,1,0:T(8,128)} %pop_ref.9) | copy-start | bytes 9437188
  3.4 17.5 %copy-start.1 = (f32[64,3,32,128]{3,2,1,0:T(8,128)S(1)}, f32[64,3,32,128]{3,2,1,0:T(8,128)}, u32[]{:S(2)}) copy-start(f32[64,3,32,128]{3,2,1,0:T(8,128)} %pop_ref.9) | copy-start | bytes 9437188
  5.9 12.4 %collective-permute-start = (bf16[80,3,32,128]{3,2,1,0:T(8,128)(2,1)}, bf16[80,3,32,128]{3,2,1,0:T(8,128)(2,1)}, u32[]{:S(2)}, u32[]{:S(2)}) collective-permute-start(bf16[80,3,32,128]{3,2,1,0:T(8,128)(2,1)} %get-tuple-element.33), channel_id=1, source_target_pairs={{0,4},{4,0},{8,12},{12,8},{16,20},{20,16},{24,28},{28,24},{1,5},{5... | collective-permute-start | bytes 5898248 | tf_op jit(solution)/shard_map/ppermute | solution.py:410
  5.9 12.4 %collective-permute-start.1 = (bf16[19,3,32,128]{3,2,1,0:T(8,128)(2,1)}, bf16[19,3,32,128]{3,2,1,0:T(8,128)(2,1)}, u32[]{:S(2)}, u32[]{:S(2)}) collective-permute-start(bf16[19,3,32,128]{3,2,1,0:T(8,128)(2,1)} %get-tuple-element.34), channel_id=1, source_target_pairs={{4,8},{8,4},{12,16},{16,12},{20,24},{24,20},{5,9},{9,5},{13,17},{1... | collective-permute-start | bytes 1400840 | tf_op jit(solution)/shard_map/ppermute | solution.py:410
  7.8 24.1 %collective-permute-start.2 = (bf16[16,3,32,128]{3,2,1,0:T(8,128)(2,1)}, bf16[16,3,32,128]{3,2,1,0:T(8,128)(2,1)S(1)}, u32[]{:S(2)}, u32[]{:S(2)}) collective-permute-start(bf16[16,3,32,128]{3,2,1,0:T(8,128)(2,1)} %get-tuple-element.36), channel_id=1, source_target_pairs={{4,8},{8,4},{12,16},{16,12},{20,24},{24,20},{5,9},{9,5},{13,17},{1... | collective-permute-start | bytes 1179656 | tf_op jit(solution)/shard_map/ppermute | solution.py:410
  11.5 25.8 %collective-permute-start.3 = (bf16[16,3,32,128]{3,2,1,0:T(8,128)(2,1)}, bf16[16,3,32,128]{3,2,1,0:T(8,128)(2,1)}, u32[]{:S(2)}, u32[]{:S(2)}) collective-permute-start(bf16[16,3,32,128]{3,2,1,0:T(8,128)(2,1)} %get-tuple-element.38), channel_id=1, source_target_pairs={{4,8},{8,4},{12,16},{16,12},{20,24},{24,20},{5,9},{9,5},{13,17},{1... | collective-permute-start | bytes 1179656 | tf_op jit(solution)/shard_map/ppermute | solution.py:410
  13.4 34.5 %collective-permute-start.7 = (bf16[16,3,32,128]{3,2,1,0:T(8,128)(2,1)}, bf16[16,3,32,128]{3,2,1,0:T(8,128)(2,1)}, u32[]{:S(2)}, u32[]{:S(2)}) collective-permute-start(bf16[16,3,32,128]{3,2,1,0:T(8,128)(2,1)} %get-tuple-element.43), channel_id=1, source_target_pairs={{4,8},{8,4},{12,16},{16,12},{20,24},{24,20},{5,9},{9,5},{13,17},{1... | collective-permute-start | bytes 1179656 | tf_op jit(solution)/shard_map/ppermute | solution.py:410
  26.4 11.8 %collective-permute-start.4 = (bf16[3,8,16,128]{3,2,1,0:T(8,128)(2,1)S(1)}, bf16[3,8,16,128]{3,2,1,0:T(8,128)(2,1)S(1)}, u32[]{:S(2)}, u32[]{:S(2)}) collective-permute-start(bf16[3,8,16,128]{3,2,1,0:T(8,128)(2,1)S(1)} %get-tuple-element.39), channel_id=1, source_target_pairs={{0,1},{1,0},{2,3},{3,2},{4,5},{5,4},{6,7},{7,6},{8,9},{9,8},{10,11... | collective-permute-start | bytes 294920 | tf_op jit(solution)/shard_map/ppermute | solution.py:410
  29.3 12.4 %collective-permute-start.5 = (bf16[3,8,16,128]{3,2,1,0:T(8,128)(2,1)S(1)}, bf16[3,8,16,128]{3,2,1,0:T(8,128)(2,1)S(1)}, u32[]{:S(2)}, u32[]{:S(2)}) collective-permute-start(bf16[3,8,16,128]{3,2,1,0:T(8,128)(2,1)S(1)} %get-tuple-element.40), channel_id=1, source_target_pairs={{0,2},{1,3},{2,0},{3,1},{4,6},{5,7},{6,4},{7,5},{8,10},{9,11},{10,... | collective-permute-start | bytes 294920 | tf_op jit(solution)/shard_map/ppermute | solution.py:410
  31.9 9.8 %collective-permute-start.6 = (bf16[3,8,16,128]{3,2,1,0:T(8,128)(2,1)S(1)}, bf16[3,8,16,128]{3,2,1,0:T(8,128)(2,1)S(1)}, u32[]{:S(2)}, u32[]{:S(2)}) collective-permute-start(bf16[3,8,16,128]{3,2,1,0:T(8,128)(2,1)S(1)} %get-tuple-element.41), channel_id=1, source_target_pairs={{0,3},{1,2},{2,1},{3,0},{4,7},{5,6},{6,5},{7,4},{8,11},{9,10},{10,... | collective-permute-start | bytes 294920 | tf_op jit(solution)/shard_map/ppermute | solution.py:410
  37.3 14.4 %collective-permute-start.8 = (bf16[3,8,16,128]{3,2,1,0:T(8,128)(2,1)S(1)}, bf16[3,8,16,128]{3,2,1,0:T(8,128)(2,1)S(1)}, u32[]{:S(2)}, u32[]{:S(2)}) collective-permute-start(bf16[3,8,16,128]{3,2,1,0:T(8,128)(2,1)S(1)} %get-tuple-element.44), channel_id=1, source_target_pairs={{0,1},{1,0},{2,3},{3,2},{4,5},{5,4},{6,7},{7,6},{8,9},{9,8},{10,11... | collective-permute-start | bytes 294920 | tf_op jit(solution)/shard_map/ppermute | solution.py:410
  38.2 13.4 %collective-permute-start.9 = (bf16[3,8,16,128]{3,2,1,0:T(8,128)(2,1)S(1)}, bf16[3,8,16,128]{3,2,1,0:T(8,128)(2,1)S(1)}, u32[]{:S(2)}, u32[]{:S(2)}) collective-permute-start(bf16[3,8,16,128]{3,2,1,0:T(8,128)(2,1)S(1)} %get-tuple-element.45), channel_id=1, source_target_pairs={{0,2},{1,3},{2,0},{3,1},{4,6},{5,7},{6,4},{7,5},{8,10},{9,11},{10,... | collective-permute-start | bytes 294920 | tf_op jit(solution)/shard_map/ppermute | solution.py:410
  41.7 10.0 %collective-permute-start.10 = (bf16[3,8,16,128]{3,2,1,0:T(8,128)(2,1)S(1)}, bf16[3,8,16,128]{3,2,1,0:T(8,128)(2,1)S(1)}, u32[]{:S(2)}, u32[]{:S(2)}) collective-permute-start(bf16[3,8,16,128]{3,2,1,0:T(8,128)(2,1)S(1)} %get-tuple-element.46), channel_id=1, source_target_pairs={{0,3},{1,2},{2,1},{3,0},{4,7},{5,6},{6,5},{7,4},{8,11},{9,10},{10,... | collective-permute-start | bytes 294920 | tf_op jit(solution)/shard_map/ppermute | solution.py:410
  47.2 14.4 %collective-permute-start.11 = (bf16[3,8,16,128]{3,2,1,0:T(8,128)(2,1)S(1)}, bf16[3,8,16,128]{3,2,1,0:T(8,128)(2,1)S(1)}, u32[]{:S(2)}, u32[]{:S(2)}) collective-permute-start(bf16[3,8,16,128]{3,2,1,0:T(8,128)(2,1)S(1)} %get-tuple-element.48), channel_id=1, source_target_pairs={{0,1},{1,0},{2,3},{3,2},{4,5},{5,4},{6,7},{7,6},{8,9},{9,8},{10,11... | collective-permute-start | bytes 294920 | tf_op jit(solution)/shard_map/ppermute | solution.py:410
  47.9 14.5 %collective-permute-start.13 = (bf16[3,8,16,128]{3,2,1,0:T(8,128)(2,1)S(1)}, bf16[3,8,16,128]{3,2,1,0:T(8,128)(2,1)S(1)}, u32[]{:S(2)}, u32[]{:S(2)}) collective-permute-start(bf16[3,8,16,128]{3,2,1,0:T(8,128)(2,1)S(1)} %get-tuple-element.50), channel_id=1, source_target_pairs={{0,2},{1,3},{2,0},{3,1},{4,6},{5,7},{6,4},{7,5},{8,10},{9,11},{10,... | collective-permute-start | bytes 294920 | tf_op jit(solution)/shard_map/ppermute | solution.py:410
  51.7 10.7 %collective-permute-start.15 = (bf16[3,8,16,128]{3,2,1,0:T(8,128)(2,1)S(1)}, bf16[3,8,16,128]{3,2,1,0:T(8,128)(2,1)S(1)}, u32[]{:S(2)}, u32[]{:S(2)}) collective-permute-start(bf16[3,8,16,128]{3,2,1,0:T(8,128)(2,1)S(1)} %get-tuple-element.52), channel_id=1, source_target_pairs={{0,3},{1,2},{2,1},{3,0},{4,7},{5,6},{6,5},{7,4},{8,11},{9,10},{10,... | collective-permute-start | bytes 294920 | tf_op jit(solution)/shard_map/ppermute | solution.py:410
  51.7 10.0 %copy-start.5 = (f32[256]{0:T(256)S(1)}, f32[256]{0:T(256)}, u32[]{:S(2)}) copy-start(f32[256]{0:T(256)} %param.7) | copy-start | bytes 3076
  51.7 17.8 %copy-start.4 = (f32[3,8,128]{2,1,0:T(8,128)S(1)}, f32[3,8,128]{2,1,0:T(8,128)}, u32[]{:S(2)}) copy-start(f32[3,8,128]{2,1,0:T(8,128)} %supersat_ref.5) | copy-start | bytes 36868
  57.2 5.4 %collective-permute-start.12 = (bf16[3,8,16,128]{3,2,1,0:T(8,128)(2,1)S(1)}, bf16[3,8,16,128]{3,2,1,0:T(8,128)(2,1)S(1)}, u32[]{:S(2)}, u32[]{:S(2)}) collective-permute-start(bf16[3,8,16,128]{3,2,1,0:T(8,128)(2,1)S(1)} %get-tuple-element.49), channel_id=1, source_target_pairs={{0,1},{1,0},{2,3},{3,2},{4,5},{5,4},{6,7},{7,6},{8,9},{9,8},{10,11... | collective-permute-start | bytes 294920 | tf_op jit(solution)/shard_map/ppermute | solution.py:410
  57.9 11.6 %collective-permute-start.14 = (bf16[3,8,16,128]{3,2,1,0:T(8,128)(2,1)S(1)}, bf16[3,8,16,128]{3,2,1,0:T(8,128)(2,1)S(1)}, u32[]{:S(2)}, u32[]{:S(2)}) collective-permute-start(bf16[3,8,16,128]{3,2,1,0:T(8,128)(2,1)S(1)} %get-tuple-element.51), channel_id=1, source_target_pairs={{0,2},{1,3},{2,0},{3,1},{4,6},{5,7},{6,4},{7,5},{8,10},{9,11},{10,... | collective-permute-start | bytes 294920 | tf_op jit(solution)/shard_map/ppermute | solution.py:410
  61.6 7.8 %collective-permute-start.16 = (bf16[3,8,16,128]{3,2,1,0:T(8,128)(2,1)S(1)}, bf16[3,8,16,128]{3,2,1,0:T(8,128)(2,1)S(1)}, u32[]{:S(2)}, u32[]{:S(2)}) collective-permute-start(bf16[3,8,16,128]{3,2,1,0:T(8,128)(2,1)S(1)} %get-tuple-element.53), channel_id=1, source_target_pairs={{0,3},{1,2},{2,1},{3,0},{4,7},{5,6},{6,5},{7,4},{8,11},{9,10},{10,... | collective-permute-start | bytes 294920 | tf_op jit(solution)/shard_map/ppermute | solution.py:410
  87.7 5.5 %collective-permute-start.19 = (f32[3,8,128]{2,1,0:T(8,128)S(1)}, f32[3,8,128]{2,1,0:T(8,128)S(1)}, u32[]{:S(2)}, u32[]{:S(2)}) collective-permute-start(f32[3,8,128]{2,1,0:T(8,128)S(1)} %constant_dynamic-update-slice_fusion.refs_0_), channel_id=1, source_target_pairs={{0,3},{1,2},{2,1},{3,0},{4,7},{5,6},{6,5},{7,4},{8,11},{9,10},{10,... | collective-permute-start | bytes 36872 | tf_op jit(solution)/shard_map/ppermute | solution.py:410
  90.2 4.6 %collective-permute-start.18 = (f32[3,8,128]{2,1,0:T(8,128)S(1)}, f32[3,8,128]{2,1,0:T(8,128)S(1)}, u32[]{:S(2)}, u32[]{:S(2)}) collective-permute-start(f32[3,8,128]{2,1,0:T(8,128)S(1)} %constant_dynamic-update-slice_fusion.refs_0_), channel_id=1, source_target_pairs={{0,2},{1,3},{2,0},{3,1},{4,6},{5,7},{6,4},{7,5},{8,10},{9,11},{10,... | collective-permute-start | bytes 36872 | tf_op jit(solution)/shard_map/ppermute | solution.py:410
  91.3 3.7 %collective-permute-start.17 = (f32[3,8,128]{2,1,0:T(8,128)S(1)}, f32[3,8,128]{2,1,0:T(8,128)S(1)}, u32[]{:S(2)}, u32[]{:S(2)}) collective-permute-start(f32[3,8,128]{2,1,0:T(8,128)S(1)} %constant_dynamic-update-slice_fusion.refs_0_), channel_id=1, source_target_pairs={{0,1},{1,0},{2,3},{3,2},{4,5},{5,4},{6,7},{7,6},{8,9},{9,8},{10,11... | collective-permute-start | bytes 36872 | tf_op jit(solution)/shard_map/ppermute | solution.py:410
  (2 other events, 1.8 us)

commit v4 on v3

--- a/solution.py
+++ b/solution.py
@@ -142,6 +142,7 @@
 
 
 RIM = 8
+PIECE = 32
 
 
 def transport_kernel(batches, place_ref, pop_ref, inside_ref, outside_ref, coef_ref, *rest):
@@ -262,125 +263,186 @@
     )(jnp.concatenate([kernel, jnp.zeros_like(kernel)])[None, :])
 
 
-def kinetics_kernel(
-    batches, groups, layer, native, chained, place_ref, supersat_ref, toeplitz_ref, column_ref, *rest
-):
-    parts = rest[: batches * groups]
-    out_ref, depletion_ref, initial, state, product, rounded = rest[batches * groups + chained :]
-    bin_count, width = state.shape
+def unpack(place_ref, parts, first, groups, batches, bin_count, store):
+    run = bin_count // 8
+    count = len(parts) // batches
+    for back in range(batches):
+        source = lax.bitwise_xor(place_ref[0], back) * (groups * GROUP)
+        for index in range(count):
+            part = parts[back * count + index]
+            begin = source + (first + index) * GROUP
+            at = lax.rem(begin, run) * 8 + begin // run
+            for y in range(part.shape[1]):
+                value = decode(part[0, y]) * (1.0 / SCALE)
+                store(pl.ds(y * bin_count + at, GROUP, stride=8), value)
+
+
+def unpack_kernel(batches, groups, place_ref, *refs):
+    *parts, out_ref = refs
+    _, rows, span_z = out_ref.shape
+    layer = out_ref.reshape(rows, span_z)
+
+    def store(where, value):
+        layer[where, :] = value
+
+    unpack(place_ref, parts, 0, groups, batches, groups * GROUP * batches, store)
+
+
+def layer_spec(shape):
+    return pl.BlockSpec((1,) + shape[1:], lambda i: (i,) + (0,) * (len(shape) - 1))
+
+
+def unpacked(place, parts, groups, batches):
+    span_x, span_y, _, span_z = parts[0].shape
+    shape = (span_x, span_y * groups * GROUP * batches, span_z)
+    return pl.pallas_call(
+        functools.partial(unpack_kernel, batches, groups),
+        grid=(span_x,),
+        in_specs=[smem_spec()] + [layer_spec(part.shape) for part in parts],
+        out_specs=layer_spec(shape),
+        out_shape=jax.ShapeDtypeStruct(shape, jnp.float32),
+        compiler_params=params(),
+        cost_estimate=cost(0, 12_000_000),
+        name="unpack",
+    )(place, *parts)
+
+
+def kinetics_kernel(batches, groups, native, place_ref, supersat_ref, toeplitz_ref, column_ref, *rest):
+    *parts, out_ref, depletion_ref, state = rest
+    bin_count = toeplitz_ref.shape[0]
     span_y, span_z = supersat_ref.shape[1:]
     run = bin_count // 8
-    block = min(width, 2 * span_z)
-    for back in range(batches):
-        source = lax.bitwise_xor(place_ref[0], back) * (groups * GROUP)
-        for index in range(groups):
-            part = parts[back * groups + index]
-            begin = source + index * GROUP
-            at = lax.rem(begin, run) * 8 + begin // run
-            for y in range(span_y):
-                value = decode(part[layer, y]) * (1.0 / SCALE)
-                initial[pl.ds(y * bin_count + at, GROUP, stride=8), :] = value
-    for y in range(span_y):
-        cells = slice(y * span_z, (y + 1) * span_z)
-        for row in range(0, bin_count, 16):
-            value = initial[pl.ds(y * bin_count + row, 16), :]
-            state[pl.ds(row, 16), cells] = value
-            rounded[pl.ds(row, 16), cells] = value.astype(jnp.bfloat16)
-
-    eighth = lax.broadcasted_iota(jnp.int32, (8, span_z), 0)
-
-    def multiply(begin):
-        cells = slice(begin, begin + block)
-        product[:, cells] = jnp.dot(
-            toeplitz_ref[...], rounded[:, cells], preferred_element_type=jnp.float32
-        )
-
-    def advance(begin):
-        lanes = [slice(lane, lane + span_z) for lane in range(begin, begin + block, span_z)]
-        speeds, lowers = [], []
-        for cells in lanes:
-            row = supersat_ref[layer, pl.ds(cells.start // span_z, 1), :]
-            speeds.append(BETA * jnp.broadcast_to(row, (8, span_z)))
-            last = state[pl.ds(bin_count - 8, 8), cells]
-            lowers.append(jnp.where(eighth > 0, pltpu.roll(last, 1, 0), 0.0))
-        for row in range(0, bin_count, 16):
-            pairs = [[] for _ in lanes]
-            for at in (pl.ds(row, 8), pl.ds(row + 8, 8)):
-                column = column_ref[at, :]
-                for index, cells in enumerate(lanes):
-                    now = state[at, cells]
-                    change = (GROW / BETA) * lowers[index] - column * now
-                    new = now + speeds[index] * (change + product[at, cells])
-                    state[at, cells] = new
-                    pairs[index].append(new)
-                    lowers[index] = now
-            for pair, cells in zip(pairs, lanes):
-                rounded[pl.ds(row, 16), cells] = jnp.concatenate(pair, axis=0).astype(
-                    jnp.bfloat16
-                )
-
-    def substep(index, carry):
-        begins = list(range(0, width, block))
-        multiply(begins[0])
-        for begin, following in zip(begins, begins[1:] + [None]):
-            if following is not None:
-                multiply(following)
-            advance(begin)
-        return carry
-
-    lax.fori_loop(0, KSTEPS, substep, 0)
+    tiles = bin_count // span_z
+    count = span_y // tiles
+    if groups > 1:
+        *parts, early_ref = parts
+        state[...] = early_ref[0]
+
+    def store(where, value):
+        state[where, :] = value
+
+    unpack(place_ref, parts, groups - 1, groups, batches, bin_count, store)
     ratio = (bins_of_rows((bin_count, span_z), 0).astype(jnp.float32) + 1.0) / bin_count
     masses = ratio * ratio * ratio
+
+    def mass(y):
+        return jnp.sum(
+            masses * state[pl.ds(y * bin_count, bin_count), :], axis=0, keepdims=True
+        )
+
     for y in range(span_y):
-        cells = slice(y * span_z, (y + 1) * span_z)
-        final = state[:, cells]
-        depletion_ref[0, pl.ds(y, 1), :] = jnp.sum(
-            masses * (final - initial[pl.ds(y * bin_count, bin_count), :]), axis=0, keepdims=True
-        )
+        depletion_ref[0, pl.ds(y, 1), :] = mass(y)
+
+    def steps(*sums):
+        eighth = lax.broadcasted_iota(jnp.int32, (8, span_z), 0)
+        pieces = bin_count // PIECE
+
+        def multiply(number, rounded):
+            stage = number // 2 % 2
+            pltpu.matmul_push_rhs(rounded, stage, number % 2)
+            for piece in range(pieces):
+                pltpu.matmul_acc_lhs(
+                    sums[number * pieces + piece],
+                    toeplitz_ref[pl.ds(piece * PIECE, PIECE), :],
+                    load_staged_rhs=None if piece else stage,
+                )
+
+        def advance(number):
+            speeds, lowers = [], []
+            for tile in range(tiles):
+                y = number * tiles + tile
+                row = supersat_ref[0, pl.ds(y, 1), :]
+                speeds.append(BETA * jnp.broadcast_to(row, (8, span_z)))
+                last = state[pl.ds((y + 1) * bin_count - 8, 8), :]
+                lowers.append(jnp.where(eighth > 0, pltpu.roll(last, 1, 0), 0.0))
+            rounded = []
+            for row in range(0, bin_count, 16):
+                if row % PIECE == 0:
+                    product = pltpu.matmul_pop(sums[number * pieces + row // PIECE])
+                pairs = [[] for _ in range(tiles)]
+                for at in (row, row + 8):
+                    column = column_ref[pl.ds(at, 8), :]
+                    for tile in range(tiles):
+                        where = pl.ds((number * tiles + tile) * bin_count + at, 8)
+                        now = state[where, :]
+                        change = (GROW / BETA) * lowers[tile] - column * now
+                        change += product[
+                            at % PIECE : at % PIECE + 8, tile * span_z : (tile + 1) * span_z
+                        ]
+                        new = now + speeds[tile] * change
+                        state[where, :] = new
+                        pairs[tile].append(new)
+                        lowers[tile] = now
+                rounded.append(
+                    jnp.concatenate(
+                        [jnp.concatenate(pair, axis=0) for pair in pairs], axis=1
+                    ).astype(jnp.bfloat16)
+                )
+            return jnp.concatenate(rounded, axis=0)
+
+        for number in range(count):
+            values = [
+                state[pl.ds((number * tiles + tile) * bin_count, bin_count), :]
+                for tile in range(tiles)
+            ]
+            multiply(number, jnp.concatenate(values, axis=1).astype(jnp.bfloat16))
+
+        def substep(index, carry):
+            for number in range(count):
+                multiply(number, advance(number))
+            return carry
+
+        lax.fori_loop(0, KSTEPS - 1, substep, 0)
+        for number in range(count):
+            advance(number)
+
+    pl.run_scoped(
+        steps,
+        *(
+            pltpu.ACC(mxu_id=number % 2)((PIECE, bin_count), jnp.float32)
+            for number in range(count)
+            for piece in range(bin_count // PIECE)
+        ),
+    )
+    for y in range(span_y):
+        depletion_ref[0, pl.ds(y, 1), :] = mass(y) - depletion_ref[0, pl.ds(y, 1), :]
         if native:
             rows = out_ref.reshape(bin_count * span_y, span_z)
         for row in range(run):
-            value = state[pl.ds(8 * row, 8), cells]
+            value = state[pl.ds(y * bin_count + 8 * row, 8), :]
             if native:
                 rows[pl.ds(row * span_y + y, 8, stride=run * span_y), :] = value
             else:
                 out_ref[0, y, pl.ds(row, 8, stride=run), :] = value
 
 
-def kinetics(place, supersat, toeplitz, column, parts, layer, batches, chain):
+def kinetics(place, supersat, toeplitz, column, parts, early, groups, batches):
     span_x, span_y, span_z = supersat.shape
     bin_count = toeplitz.shape[0]
     native = span_y % 8 == 0
-    whole = pl.BlockSpec(memory_space=pltpu.VMEM)
     if native:
         out_shape = (bin_count, span_x, span_y, span_z)
-        out_spec = pl.BlockSpec((bin_count, 1, span_y, span_z), lambda i: (0, layer, 0, 0))
+        out_spec = pl.BlockSpec((bin_count, 1, span_y, span_z), lambda i: (0, i, 0, 0))
     else:
         out_shape = (span_x, span_y, bin_count, span_z)
-        out_spec = pl.BlockSpec((1,) + out_shape[1:], lambda i: (layer, 0, 0, 0))
-    chained = 0 if chain is None else 1
-    return pl.pallas_call(
-        functools.partial(kinetics_kernel, batches, len(parts) // batches, layer, native, chained),
-        grid=(1,),
-        in_specs=[smem_spec()]
-        + [whole] * (3 + len(parts))
-        + [pl.BlockSpec(memory_space=pl.ANY)] * chained,
-        out_specs=[out_spec, whole],
+        out_spec = layer_spec(out_shape)
+    out, depletion = pl.pallas_call(
+        functools.partial(kinetics_kernel, batches, groups, native),
+        grid=(span_x,),
+        in_specs=[smem_spec(), layer_spec(supersat.shape)]
+        + [vmem_spec()] * 2
+        + [layer_spec(array.shape) for array in parts + early],
+        out_specs=[out_spec, layer_spec(supersat.shape)],
         out_shape=[
             jax.ShapeDtypeStruct(out_shape, jnp.float32),
-            jax.ShapeDtypeStruct((1, span_y, span_z), jnp.float32),
+            jax.ShapeDtypeStruct(supersat.shape, jnp.float32),
         ],
-        scratch_shapes=[
-            pltpu.VMEM((bin_count * span_y, span_z), jnp.float32),
-            pltpu.VMEM((bin_count, span_y * span_z), jnp.float32),
-            pltpu.VMEM((bin_count, span_y * span_z), jnp.float32),
-            pltpu.VMEM((bin_count, span_y * span_z), jnp.bfloat16),
-        ],
-        input_output_aliases={4 + len(parts): 0} if chained else {},
-        compiler_params=params(),
-        cost_estimate=cost(0, 22_000_000),
+        scratch_shapes=[pltpu.VMEM((bin_count * span_y, span_z), jnp.float32)],
+        compiler_params=params(),
+        cost_estimate=cost(0, 50_000_000),
         name="kinetics",
-    )(place, supersat, toeplitz, column, *parts, *([chain] if chained else []))
+    )(place, supersat, toeplitz, column, *parts, *early)
+    return (out if native else jnp.transpose(out, (2, 0, 1, 3)), depletion)
 
 
 def assemble_kernel(batches, place_ref, *refs):
@@ -420,16 +482,16 @@
 
 def body(population, velocity, supersat, kernel):
     batches = lax.axis_size("bins")
-    span_x = population.shape[1]
     place = jnp.stack([lax.axis_index("bins"), lax.axis_index("space")]).astype(jnp.int32)
     toeplitz, column = tables(kernel)
-    codes, *groups = coded_slab(population, velocity)
+    codes, *slabs = coded_slab(population, velocity)
+    groups = len(slabs)
     inside = with_partner(codes)
-    outside = [with_other(group) for group in groups]
+    outside = [with_other(slab) for slab in slabs]
     coefs = weights(place, velocity, inside, outside[0])
     parts = [[] for _ in range(batches)]
     moved = []
-    for group in range(len(groups)):
+    for group in range(groups):
         after = list(moved[:1]) + ([row[group - 2] for row in parts[1:]] if group > 1 else [])
         moved = transported(
             place, population, inside, outside[group], coefs, group, batches, after
@@ -438,16 +500,12 @@
             if ahead:
                 array = swapped(array, "bins", lambda i: i ^ ahead)
             parts[ahead].append(array)
-    flat = [part for row in parts for part in row]
-    out, depletions = None, []
-    for layer in range(span_x):
-        out, depletion = kinetics(
-            place, supersat, toeplitz, column, flat, layer, batches, out
-        )
-        depletions.append(depletion)
-    if not supersat.shape[1] % 8 == 0:
-        out = jnp.transpose(out, (2, 0, 1, 3))
-    own = jnp.concatenate(depletions, axis=0)
+    early = []
+    if groups > 1:
+        flat = [part for row in parts for part in row[:-1]]
+        early = [unpacked(place, flat, groups, batches)]
+    last = [row[-1] for row in parts]
+    out, own = kinetics(place, supersat, toeplitz, column, last, early, groups, batches)
     others = [own] + [swapped(own, "bins", lambda i: i ^ ahead) for ahead in range(1, batches)]
     return (out, assembled(place, others, batches))
 

time: 96.8 us -> 92.9 us (0.960)
  waiting for transfers between devices: 11.2 us -> 9.09 us
  Pallas kernels: 46.1 us -> 44.2 us
    ppermute x20, waiting for transfers between devices: 11.2 us -> 9.09 us  [swapped(): return lax.ppermute(array, axis, pairs)]
    pallas_call x3 -> x2, Pallas kernels: 18.2 us -> 16.4 us  [the longest x1 14.4 us: kinetics(): pl.pallas_call(functools.partial(kinetics_kernel, batches, groups, native...]
    unnamed x14 -> x12, local copies, waits for them, and re-layouts: 3.67 us -> 3.67 us
  transfers between devices with their start and end apart: 20 -> 20, of which waited for: 6 -> 5; matrix products, arithmetic and copies ran while one was open for 0% -> 0% of each run, Pallas kernels for 25% -> 28%
where the time goes in v4:
time: 92.9 us; the launch traced here: 92.2 us
  Pallas kernels  44.2 us (48%)
  starting transfers between devices  34.4 us (37%)
  waiting for transfers between devices  9.09 us (10%)
  local copies, waits for them, and re-layouts  3.67 us (4%)
    ppermute x20, starting transfers between devices, swapped(): return lax.ppermute(array, axis, pairs)  34.4 us
    pallas_call x4, Pallas kernels, transported(): pl.pallas_call(functools.partial(transport_kernel, batches), grid=(1,), i...  21.8 us
    pallas_call x1, Pallas kernels, kinetics(): pl.pallas_call(functools.partial(kinetics_kernel, batches, groups, native...  14.4 us
    ppermute x20, waiting for transfers between devices, swapped(): return lax.ppermute(array, axis, pairs)  9.09 us
    unnamed x12, local copies, waits for them, and re-layouts  3.67 us
    pallas_call x1, Pallas kernels, coded_slab(): pl.pallas_call(code_kernel, in_specs=[vmem_spec()] * 2, out_specs=[vmem_s...  2.47 us
    pallas_call x1, Pallas kernels, unpacked(): pl.pallas_call(functools.partial(unpack_kernel, batches, groups), grid=(s...  2.03 us
  transfers between devices with their start and end apart: 20, of which 5 were waited for; matrix products, arithmetic and copies ran while one was open for 0% of the time, Pallas kernels for 28%

profile of v4, /device:TPU:2, one launch (start us, length us, event | category | flops | bytes accessed | tf_op | source)
XLA Modules:
  0.0 92.2 jit_solution(5406668240431626797)
XLA Ops:
  0.6 1.9 %copy-done = f32[64,3,32,128]{3,2,1,0:T(8,128)S(1)} copy-done((f32[64,3,32,128]{3,2,1,0:T(8,128)S(1)}, f32[64,3,32,128]{3,2,1,0:T(8,128)}, u32[]{:S(2)}) %copy-start) | copy-done | bytes 3145752
  3.4 2.5 %code_slab.1 = (bf16[80,3,32,128]{3,2,1,0:T(8,128)(2,1)}, bf16[19,3,32,128]{3,2,1,0:T(8,128)(2,1)}, bf16[16,3,32,128]{3,2,1,0:T(8,128)(2,1)}, bf16[16,3,32,128]{3,2,1,0:T(8,128)(2,1)}, bf16[16,3,32,128]{3,2,1,0:T(8,128)(2,1)}) custom-call(f32[64,3,32,128]{3,2,1,0:T(8,128)S(1)} %copy-done, bf16[3,3,32,128]{3,2,1,0:T(8,128)(2,1)S(1)} %copy-done.2), custom_call_target="tpu_custom_call" | custom-call | bytes 6000000 | tf_op jit(solution)/shard_map/code_slab/pallas_call | solution.py:76
  5.9 1.9 %collective-permute-start.2 = (bf16[19,3,32,128]{3,2,1,0:T(8,128)(2,1)}, bf16[19,3,32,128]{3,2,1,0:T(8,128)(2,1)}, u32[]{:S(2)}, u32[]{:S(2)}) collective-permute-start(bf16[19,3,32,128]{3,2,1,0:T(8,128)(2,1)} %get-tuple-element.31), channel_id=1, source_target_pairs={{4,8},{8,4},{12,16},{16,12},{20,24},{24,20},{5,9},{9,5},{13,17},{1... | collective-permute-start | bytes 1400840 | tf_op jit(solution)/shard_map/ppermute | solution.py:472
  7.8 3.6 %collective-permute-start.4 = (bf16[16,3,32,128]{3,2,1,0:T(8,128)(2,1)}, bf16[16,3,32,128]{3,2,1,0:T(8,128)(2,1)S(1)}, u32[]{:S(2)}, u32[]{:S(2)}) collective-permute-start(bf16[16,3,32,128]{3,2,1,0:T(8,128)(2,1)} %get-tuple-element.33), channel_id=1, source_target_pairs={{4,8},{8,4},{12,16},{16,12},{20,24},{24,20},{5,9},{9,5},{13,17},{1... | collective-permute-start | bytes 1179656 | tf_op jit(solution)/shard_map/ppermute | solution.py:472
  11.5 1.9 %collective-permute-start.3 = (bf16[16,3,32,128]{3,2,1,0:T(8,128)(2,1)}, bf16[16,3,32,128]{3,2,1,0:T(8,128)(2,1)}, u32[]{:S(2)}, u32[]{:S(2)}) collective-permute-start(bf16[16,3,32,128]{3,2,1,0:T(8,128)(2,1)} %get-tuple-element.32), channel_id=1, source_target_pairs={{4,8},{8,4},{12,16},{16,12},{20,24},{24,20},{5,9},{9,5},{13,17},{1... | collective-permute-start | bytes 1179656 | tf_op jit(solution)/shard_map/ppermute | solution.py:472
  13.4 3.6 %collective-permute-start.1 = (bf16[16,3,32,128]{3,2,1,0:T(8,128)(2,1)}, bf16[16,3,32,128]{3,2,1,0:T(8,128)(2,1)}, u32[]{:S(2)}, u32[]{:S(2)}) collective-permute-start(bf16[16,3,32,128]{3,2,1,0:T(8,128)(2,1)} %get-tuple-element.30), channel_id=1, source_target_pairs={{4,8},{8,4},{12,16},{16,12},{20,24},{24,20},{5,9},{9,5},{13,17},{1... | collective-permute-start | bytes 1179656 | tf_op jit(solution)/shard_map/ppermute | solution.py:472
  17.1 1.2 %collective-permute-done.2.outside_ref = bf16[19,3,32,128]{3,2,1,0:T(8,128)(2,1)} collective-permute-done((bf16[19,3,32,128]{3,2,1,0:T(8,128)(2,1)}, bf16[19,3,32,128]{3,2,1,0:T(8,128)(2,1)}, u32[]{:S(2)}, u32[]{:S(2)}) %collective-permute-start.2) | collective-permute-done | bytes 466976 | tf_op jit(solution)/shard_map/ppermute | solution.py:472
  19.2 1.7 %weights.1.coef_ref = f32[7,7,32,128]{3,2,1,0:T(8,128)S(1)} custom-call(s32[2]{0:T(128)S(1)} %pad_add_fusion.place_ref, bf16[3,3,32,128]{3,2,1,0:T(8,128)(2,1)S(1)} %copy-done.3, bf16[80,3,32,128]{3,2,1,0:T(8,128)(2,1)} %collective-permute-done.inside_ref, bf16[19,3,32,128]{3,2,1,0:T(8,128)(2,1)} %collective-permute-done.2.outside_ref), custom_call_target="tpu_custom_call" | custom-call | bytes 4000000 | tf_op jit(solution)/shard_map/weights/pallas_call | solution.py:126
  20.9 5.5 %transport.4 = (bf16[3,8,16,128]{3,2,1,0:T(8,128)(2,1)S(1)}, bf16[3,8,16,128]{3,2,1,0:T(8,128)(2,1)S(1)}, bf16[3,8,16,128]{3,2,1,0:T(8,128)(2,1)S(1)}, bf16[3,8,16,128]{3,2,1,0:T(8,128)(2,1)S(1)}) custom-call(s32[2]{0:T(128)S(1)} %pad_add_fusion.place_ref, f32[64,3,32,128]{3,2,1,0:T(8,128)S(1)} %copy-done.1, ...), custom_call_target="tpu_custom_call" | custom-call | bytes 18000000 | tf_op jit(solution)/shard_map/transport/pallas_call | solution.py:207
  26.4 2.9 %collective-permute-start.5 = (bf16[3,8,16,128]{3,2,1,0:T(8,128)(2,1)S(1)}, bf16[3,8,16,128]{3,2,1,0:T(8,128)(2,1)S(1)}, u32[]{:S(2)}, u32[]{:S(2)}) collective-permute-start(bf16[3,8,16,128]{3,2,1,0:T(8,128)(2,1)S(1)} %get-tuple-element.36), channel_id=1, source_target_pairs={{0,1},{1,0},{2,3},{3,2},{4,5},{5,4},{6,7},{7,6},{8,9},{9,8},{10,11... | collective-permute-start | bytes 294920 | tf_op jit(solution)/shard_map/ppermute | solution.py:472
  29.3 2.6 %collective-permute-start.6 = (bf16[3,8,16,128]{3,2,1,0:T(8,128)(2,1)S(1)}, bf16[3,8,16,128]{3,2,1,0:T(8,128)(2,1)S(1)}, u32[]{:S(2)}, u32[]{:S(2)}) collective-permute-start(bf16[3,8,16,128]{3,2,1,0:T(8,128)(2,1)S(1)} %get-tuple-element.37), channel_id=1, source_target_pairs={{0,2},{1,3},{2,0},{3,1},{4,6},{5,7},{6,4},{7,5},{8,10},{9,11},{10,... | collective-permute-start | bytes 294920 | tf_op jit(solution)/shard_map/ppermute | solution.py:472
  31.9 5.4 %transport.5 = (bf16[3,8,16,128]{3,2,1,0:T(8,128)(2,1)S(1)}, bf16[3,8,16,128]{3,2,1,0:T(8,128)(2,1)S(1)}, bf16[3,8,16,128]{3,2,1,0:T(8,128)(2,1)S(1)}, bf16[3,8,16,128]{3,2,1,0:T(8,128)(2,1)S(1)}) custom-call(s32[2]{0:T(128)S(1)} %pad_add_fusion.place_ref, f32[64,3,32,128]{3,2,1,0:T(8,128)S(1)} %copy-done.1, ...), custom_call_target="tpu_custom_call" | custom-call | bytes 18000000 | tf_op jit(solution)/shard_map/transport/pallas_call | solution.py:207
  38.2 3.5 %collective-permute-start.9 = (bf16[3,8,16,128]{3,2,1,0:T(8,128)(2,1)S(1)}, bf16[3,8,16,128]{3,2,1,0:T(8,128)(2,1)S(1)}, u32[]{:S(2)}, u32[]{:S(2)}) collective-permute-start(bf16[3,8,16,128]{3,2,1,0:T(8,128)(2,1)S(1)} %get-tuple-element.41), channel_id=1, source_target_pairs={{0,2},{1,3},{2,0},{3,1},{4,6},{5,7},{6,4},{7,5},{8,10},{9,11},{10,... | collective-permute-start | bytes 294920 | tf_op jit(solution)/shard_map/ppermute | solution.py:472
  41.7 5.5 %transport.6 = (bf16[3,8,16,128]{3,2,1,0:T(8,128)(2,1)S(1)}, bf16[3,8,16,128]{3,2,1,0:T(8,128)(2,1)S(1)}, bf16[3,8,16,128]{3,2,1,0:T(8,128)(2,1)S(1)}, bf16[3,8,16,128]{3,2,1,0:T(8,128)(2,1)S(1)}) custom-call(s32[2]{0:T(128)S(1)} %pad_add_fusion.place_ref, f32[64,3,32,128]{3,2,1,0:T(8,128)S(1)} %copy-done.1, ...), custom_call_target="tpu_custom_call" | custom-call | bytes 18000000 | tf_op jit(solution)/shard_map/transport/pallas_call | solution.py:207
  47.9 3.8 %collective-permute-start.15 = (bf16[3,8,16,128]{3,2,1,0:T(8,128)(2,1)S(1)}, bf16[3,8,16,128]{3,2,1,0:T(8,128)(2,1)S(1)}, u32[]{:S(2)}, u32[]{:S(2)}) collective-permute-start(bf16[3,8,16,128]{3,2,1,0:T(8,128)(2,1)S(1)} %get-tuple-element.48), channel_id=1, source_target_pairs={{0,2},{1,3},{2,0},{3,1},{4,6},{5,7},{6,4},{7,5},{8,10},{9,11},{10,... | collective-permute-start | bytes 294920 | tf_op jit(solution)/shard_map/ppermute | solution.py:472
  51.7 5.5 %transport.7 = (bf16[3,8,16,128]{3,2,1,0:T(8,128)(2,1)S(1)}, bf16[3,8,16,128]{3,2,1,0:T(8,128)(2,1)S(1)}, bf16[3,8,16,128]{3,2,1,0:T(8,128)(2,1)S(1)}, bf16[3,8,16,128]{3,2,1,0:T(8,128)(2,1)S(1)}) custom-call(s32[2]{0:T(128)S(1)} %pad_add_fusion.place_ref, f32[64,3,32,128]{3,2,1,0:T(8,128)S(1)} %copy-done.1, ...), custom_call_target="tpu_custom_call" | custom-call | bytes 18000000 | tf_op jit(solution)/shard_map/transport/pallas_call | solution.py:207
  57.9 3.8 %collective-permute-start.12 = (bf16[3,8,16,128]{3,2,1,0:T(8,128)(2,1)S(1)}, bf16[3,8,16,128]{3,2,1,0:T(8,128)(2,1)S(1)}, u32[]{:S(2)}, u32[]{:S(2)}) collective-permute-start(bf16[3,8,16,128]{3,2,1,0:T(8,128)(2,1)S(1)} %get-tuple-element.45), channel_id=1, source_target_pairs={{0,2},{1,3},{2,0},{3,1},{4,6},{5,7},{6,4},{7,5},{8,10},{9,11},{10,... | collective-permute-start | bytes 294920 | tf_op jit(solution)/shard_map/ppermute | solution.py:472
  62.4 2.0 %unpack.1.rest_4_ = f32[3,2048,128]{2,1,0:T(8,128)S(1)} custom-call(s32[2]{0:T(128)S(1)} %pad_add_fusion.place_ref, bf16[3,8,16,128]{3,2,1,0:T(8,128)(2,1)S(1)} %get-tuple-element.34.rest_0_.refs_0_, bf16[3,8,16,128]{3,2,1,0:T(8,128)(2,1)S(1)} %get-tuple-element.35.rest_0_.refs_1_, bf16[3,8,16,128]{3,2,1,0:T(8,128)(2,1)S(1)} %get-tuple-element.39.rest_0_.refs_2_, ...), custom_call_target="tpu_custom_call" | custom-call | bytes 12000000 | tf_op jit(solution)/shard_map/unpack/pallas_call | solution.py:298
  64.4 5.0 %collective-permute-done.12.rest_2_ = bf16[3,8,16,128]{3,2,1,0:T(8,128)(2,1)S(1)} collective-permute-done((bf16[3,8,16,128]{3,2,1,0:T(8,128)(2,1)S(1)}, bf16[3,8,16,128]{3,2,1,0:T(8,128)(2,1)S(1)}, u32[]{:S(2)}, u32[]{:S(2)}) %collective-permute-start.12) | collective-permute-done | bytes 98336 | tf_op jit(solution)/shard_map/ppermute | solution.py:472
  69.4 14.4 %kinetics.1 = (f32[256,3,8,128]{3,2,1,0:T(8,128)}, f32[3,8,128]{2,1,0:T(8,128)S(1)}) custom-call(s32[2]{0:T(128)S(1)} %pad_add_fusion.place_ref, f32[3,8,128]{2,1,0:T(8,128)S(1)} %copy-done.4, bf16[256,256]{1,0:T(8,128)(2,1)S(1)} %get-tuple-element.27.toeplitz_ref, f32[256,128]{1,0:T(8,128)S(1)} %get-tuple-element.28.column_ref, ...), custom_call_target="tpu_custom_call" | custom-call | bytes 50000000 | tf_op jit(solution)/shard_map/kinetics/pallas_call | solution.py:429
  83.8 2.5 %collective-permute-start.19 = (f32[3,8,128]{2,1,0:T(8,128)S(1)}, f32[3,8,128]{2,1,0:T(8,128)S(1)}, u32[]{:S(2)}, u32[]{:S(2)}) collective-permute-start(f32[3,8,128]{2,1,0:T(8,128)S(1)} %get-tuple-element.51.refs_0_), channel_id=1, source_target_pairs={{0,3},{1,2},{2,1},{3,0},{4,7},{5,6},{6,5},{7,4},{8,11},{9,10},{10,... | collective-permute-start | bytes 36872 | tf_op jit(solution)/shard_map/ppermute | solution.py:472
  88.2 1.1 %collective-permute-done.19.refs_3_ = f32[3,8,128]{2,1,0:T(8,128)S(1)} collective-permute-done((f32[3,8,128]{2,1,0:T(8,128)S(1)}, f32[3,8,128]{2,1,0:T(8,128)S(1)}, u32[]{:S(2)}, u32[]{:S(2)}) %collective-permute-start.19) | collective-permute-done | bytes 12320 | tf_op jit(solution)/shard_map/ppermute | solution.py:472
  89.3 1.6 %collective-permute-done.18.refs_2_ = f32[3,8,128]{2,1,0:T(8,128)S(1)} collective-permute-done((f32[3,8,128]{2,1,0:T(8,128)S(1)}, f32[3,8,128]{2,1,0:T(8,128)S(1)}, u32[]{:S(2)}, u32[]{:S(2)}) %collective-permute-start.18) | collective-permute-done | bytes 12320 | tf_op jit(solution)/shard_map/ppermute | solution.py:472
  91.1 1.2 %assemble.1 = f32[3,4,8,128]{3,2,1,0:T(8,128)} custom-call(s32[2]{0:T(128)S(1)} %pad_add_fusion.place_ref, f32[3,8,128]{2,1,0:T(8,128)S(1)} %get-tuple-element.51.refs_0_, f32[3,8,128]{2,1,0:T(8,128)S(1)} %collective-permute-done.17.refs_1_, f32[3,8,128]{2,1,0:T(8,128)S(1)} %collective-permute-done.18.refs_2_, f32[3,8,128]{2,1,0:T(8,128)S(1)} %collective-permute-done.19.refs_3_), custom_call_target="tpu_custom_call" | custom-call | tf_op jit(solution)/shard_map/assemble/pallas_call | solution.py:458
  (40 shorter events, 7.0 us)
Async XLA Ops:
  0.6 1.9 %copy-start = (f32[64,3,32,128]{3,2,1,0:T(8,128)S(1)}, f32[64,3,32,128]{3,2,1,0:T(8,128)}, u32[]{:S(2)}) copy-start(f32[64,3,32,128]{3,2,1,0:T(8,128)} %pop_ref.9) | copy-start | bytes 9437188
  3.4 17.5 %copy-start.1 = (f32[64,3,32,128]{3,2,1,0:T(8,128)S(1)}, f32[64,3,32,128]{3,2,1,0:T(8,128)}, u32[]{:S(2)}) copy-start(f32[64,3,32,128]{3,2,1,0:T(8,128)} %pop_ref.9) | copy-start | bytes 9437188
  5.9 12.4 %collective-permute-start = (bf16[80,3,32,128]{3,2,1,0:T(8,128)(2,1)}, bf16[80,3,32,128]{3,2,1,0:T(8,128)(2,1)}, u32[]{:S(2)}, u32[]{:S(2)}) collective-permute-start(bf16[80,3,32,128]{3,2,1,0:T(8,128)(2,1)} %get-tuple-element.29), channel_id=1, source_target_pairs={{0,4},{4,0},{8,12},{12,8},{16,20},{20,16},{24,28},{28,24},{1,5},{5... | collective-permute-start | bytes 5898248 | tf_op jit(solution)/shard_map/ppermute | solution.py:472
  5.9 12.4 %collective-permute-start.2 = (bf16[19,3,32,128]{3,2,1,0:T(8,128)(2,1)}, bf16[19,3,32,128]{3,2,1,0:T(8,128)(2,1)}, u32[]{:S(2)}, u32[]{:S(2)}) collective-permute-start(bf16[19,3,32,128]{3,2,1,0:T(8,128)(2,1)} %get-tuple-element.31), channel_id=1, source_target_pairs={{4,8},{8,4},{12,16},{16,12},{20,24},{24,20},{5,9},{9,5},{13,17},{1... | collective-permute-start | bytes 1400840 | tf_op jit(solution)/shard_map/ppermute | solution.py:472
  7.8 24.1 %collective-permute-start.4 = (bf16[16,3,32,128]{3,2,1,0:T(8,128)(2,1)}, bf16[16,3,32,128]{3,2,1,0:T(8,128)(2,1)S(1)}, u32[]{:S(2)}, u32[]{:S(2)}) collective-permute-start(bf16[16,3,32,128]{3,2,1,0:T(8,128)(2,1)} %get-tuple-element.33), channel_id=1, source_target_pairs={{4,8},{8,4},{12,16},{16,12},{20,24},{24,20},{5,9},{9,5},{13,17},{1... | collective-permute-start | bytes 1179656 | tf_op jit(solution)/shard_map/ppermute | solution.py:472
  11.5 25.8 %collective-permute-start.3 = (bf16[16,3,32,128]{3,2,1,0:T(8,128)(2,1)}, bf16[16,3,32,128]{3,2,1,0:T(8,128)(2,1)}, u32[]{:S(2)}, u32[]{:S(2)}) collective-permute-start(bf16[16,3,32,128]{3,2,1,0:T(8,128)(2,1)} %get-tuple-element.32), channel_id=1, source_target_pairs={{4,8},{8,4},{12,16},{16,12},{20,24},{24,20},{5,9},{9,5},{13,17},{1... | collective-permute-start | bytes 1179656 | tf_op jit(solution)/shard_map/ppermute | solution.py:472
  13.4 34.5 %collective-permute-start.1 = (bf16[16,3,32,128]{3,2,1,0:T(8,128)(2,1)}, bf16[16,3,32,128]{3,2,1,0:T(8,128)(2,1)}, u32[]{:S(2)}, u32[]{:S(2)}) collective-permute-start(bf16[16,3,32,128]{3,2,1,0:T(8,128)(2,1)} %get-tuple-element.30), channel_id=1, source_target_pairs={{4,8},{8,4},{12,16},{16,12},{20,24},{24,20},{5,9},{9,5},{13,17},{1... | collective-permute-start | bytes 1179656 | tf_op jit(solution)/shard_map/ppermute | solution.py:472
  26.4 11.8 %collective-permute-start.5 = (bf16[3,8,16,128]{3,2,1,0:T(8,128)(2,1)S(1)}, bf16[3,8,16,128]{3,2,1,0:T(8,128)(2,1)S(1)}, u32[]{:S(2)}, u32[]{:S(2)}) collective-permute-start(bf16[3,8,16,128]{3,2,1,0:T(8,128)(2,1)S(1)} %get-tuple-element.36), channel_id=1, source_target_pairs={{0,1},{1,0},{2,3},{3,2},{4,5},{5,4},{6,7},{7,6},{8,9},{9,8},{10,11... | collective-permute-start | bytes 294920 | tf_op jit(solution)/shard_map/ppermute | solution.py:472
  29.3 12.4 %collective-permute-start.6 = (bf16[3,8,16,128]{3,2,1,0:T(8,128)(2,1)S(1)}, bf16[3,8,16,128]{3,2,1,0:T(8,128)(2,1)S(1)}, u32[]{:S(2)}, u32[]{:S(2)}) collective-permute-start(bf16[3,8,16,128]{3,2,1,0:T(8,128)(2,1)S(1)} %get-tuple-element.37), channel_id=1, source_target_pairs={{0,2},{1,3},{2,0},{3,1},{4,6},{5,7},{6,4},{7,5},{8,10},{9,11},{10,... | collective-permute-start | bytes 294920 | tf_op jit(solution)/shard_map/ppermute | solution.py:472
  31.9 9.8 %collective-permute-start.7 = (bf16[3,8,16,128]{3,2,1,0:T(8,128)(2,1)S(1)}, bf16[3,8,16,128]{3,2,1,0:T(8,128)(2,1)S(1)}, u32[]{:S(2)}, u32[]{:S(2)}) collective-permute-start(bf16[3,8,16,128]{3,2,1,0:T(8,128)(2,1)S(1)} %get-tuple-element.38), channel_id=1, source_target_pairs={{0,3},{1,2},{2,1},{3,0},{4,7},{5,6},{6,5},{7,4},{8,11},{9,10},{10,... | collective-permute-start | bytes 294920 | tf_op jit(solution)/shard_map/ppermute | solution.py:472
  37.3 14.4 %collective-permute-start.8 = (bf16[3,8,16,128]{3,2,1,0:T(8,128)(2,1)S(1)}, bf16[3,8,16,128]{3,2,1,0:T(8,128)(2,1)S(1)}, u32[]{:S(2)}, u32[]{:S(2)}) collective-permute-start(bf16[3,8,16,128]{3,2,1,0:T(8,128)(2,1)S(1)} %get-tuple-element.40), channel_id=1, source_target_pairs={{0,1},{1,0},{2,3},{3,2},{4,5},{5,4},{6,7},{7,6},{8,9},{9,8},{10,11... | collective-permute-start | bytes 294920 | tf_op jit(solution)/shard_map/ppermute | solution.py:472
  38.2 13.4 %collective-permute-start.9 = (bf16[3,8,16,128]{3,2,1,0:T(8,128)(2,1)S(1)}, bf16[3,8,16,128]{3,2,1,0:T(8,128)(2,1)S(1)}, u32[]{:S(2)}, u32[]{:S(2)}) collective-permute-start(bf16[3,8,16,128]{3,2,1,0:T(8,128)(2,1)S(1)} %get-tuple-element.41), channel_id=1, source_target_pairs={{0,2},{1,3},{2,0},{3,1},{4,6},{5,7},{6,4},{7,5},{8,10},{9,11},{10,... | collective-permute-start | bytes 294920 | tf_op jit(solution)/shard_map/ppermute | solution.py:472
  41.7 10.0 %collective-permute-start.10 = (bf16[3,8,16,128]{3,2,1,0:T(8,128)(2,1)S(1)}, bf16[3,8,16,128]{3,2,1,0:T(8,128)(2,1)S(1)}, u32[]{:S(2)}, u32[]{:S(2)}) collective-permute-start(bf16[3,8,16,128]{3,2,1,0:T(8,128)(2,1)S(1)} %get-tuple-element.42), channel_id=1, source_target_pairs={{0,3},{1,2},{2,1},{3,0},{4,7},{5,6},{6,5},{7,4},{8,11},{9,10},{10,... | collective-permute-start | bytes 294920 | tf_op jit(solution)/shard_map/ppermute | solution.py:472
  47.2 14.4 %collective-permute-start.14 = (bf16[3,8,16,128]{3,2,1,0:T(8,128)(2,1)S(1)}, bf16[3,8,16,128]{3,2,1,0:T(8,128)(2,1)S(1)}, u32[]{:S(2)}, u32[]{:S(2)}) collective-permute-start(bf16[3,8,16,128]{3,2,1,0:T(8,128)(2,1)S(1)} %get-tuple-element.47), channel_id=1, source_target_pairs={{0,1},{1,0},{2,3},{3,2},{4,5},{5,4},{6,7},{7,6},{8,9},{9,8},{10,11... | collective-permute-start | bytes 294920 | tf_op jit(solution)/shard_map/ppermute | solution.py:472
  47.9 14.5 %collective-permute-start.15 = (bf16[3,8,16,128]{3,2,1,0:T(8,128)(2,1)S(1)}, bf16[3,8,16,128]{3,2,1,0:T(8,128)(2,1)S(1)}, u32[]{:S(2)}, u32[]{:S(2)}) collective-permute-start(bf16[3,8,16,128]{3,2,1,0:T(8,128)(2,1)S(1)} %get-tuple-element.48), channel_id=1, source_target_pairs={{0,2},{1,3},{2,0},{3,1},{4,6},{5,7},{6,4},{7,5},{8,10},{9,11},{10,... | collective-permute-start | bytes 294920 | tf_op jit(solution)/shard_map/ppermute | solution.py:472
  51.7 10.7 %collective-permute-start.16 = (bf16[3,8,16,128]{3,2,1,0:T(8,128)(2,1)S(1)}, bf16[3,8,16,128]{3,2,1,0:T(8,128)(2,1)S(1)}, u32[]{:S(2)}, u32[]{:S(2)}) collective-permute-start(bf16[3,8,16,128]{3,2,1,0:T(8,128)(2,1)S(1)} %get-tuple-element.49), channel_id=1, source_target_pairs={{0,3},{1,2},{2,1},{3,0},{4,7},{5,6},{6,5},{7,4},{8,11},{9,10},{10,... | collective-permute-start | bytes 294920 | tf_op jit(solution)/shard_map/ppermute | solution.py:472
  51.7 10.0 %copy-start.5 = (f32[256]{0:T(256)S(1)}, f32[256]{0:T(256)}, u32[]{:S(2)}) copy-start(f32[256]{0:T(256)} %param.7) | copy-start | bytes 3076
  57.2 12.3 %copy-start.4 = (f32[3,8,128]{2,1,0:T(8,128)S(1)}, f32[3,8,128]{2,1,0:T(8,128)}, u32[]{:S(2)}) copy-start(f32[3,8,128]{2,1,0:T(8,128)} %supersat_ref.1) | copy-start | bytes 36868
  57.2 7.2 %collective-permute-start.11 = (bf16[3,8,16,128]{3,2,1,0:T(8,128)(2,1)S(1)}, bf16[3,8,16,128]{3,2,1,0:T(8,128)(2,1)S(1)}, u32[]{:S(2)}, u32[]{:S(2)}) collective-permute-start(bf16[3,8,16,128]{3,2,1,0:T(8,128)(2,1)S(1)} %get-tuple-element.44), channel_id=1, source_target_pairs={{0,1},{1,0},{2,3},{3,2},{4,5},{5,4},{6,7},{7,6},{8,9},{9,8},{10,11... | collective-permute-start | bytes 294920 | tf_op jit(solution)/shard_map/ppermute | solution.py:472
  57.9 11.6 %collective-permute-start.12 = (bf16[3,8,16,128]{3,2,1,0:T(8,128)(2,1)S(1)}, bf16[3,8,16,128]{3,2,1,0:T(8,128)(2,1)S(1)}, u32[]{:S(2)}, u32[]{:S(2)}) collective-permute-start(bf16[3,8,16,128]{3,2,1,0:T(8,128)(2,1)S(1)} %get-tuple-element.45), channel_id=1, source_target_pairs={{0,2},{1,3},{2,0},{3,1},{4,6},{5,7},{6,4},{7,5},{8,10},{9,11},{10,... | collective-permute-start | bytes 294920 | tf_op jit(solution)/shard_map/ppermute | solution.py:472
  61.6 7.8 %collective-permute-start.13 = (bf16[3,8,16,128]{3,2,1,0:T(8,128)(2,1)S(1)}, bf16[3,8,16,128]{3,2,1,0:T(8,128)(2,1)S(1)}, u32[]{:S(2)}, u32[]{:S(2)}) collective-permute-start(bf16[3,8,16,128]{3,2,1,0:T(8,128)(2,1)S(1)} %get-tuple-element.46), channel_id=1, source_target_pairs={{0,3},{1,2},{2,1},{3,0},{4,7},{5,6},{6,5},{7,4},{8,11},{9,10},{10,... | collective-permute-start | bytes 294920 | tf_op jit(solution)/shard_map/ppermute | solution.py:472
  83.8 5.5 %collective-permute-start.19 = (f32[3,8,128]{2,1,0:T(8,128)S(1)}, f32[3,8,128]{2,1,0:T(8,128)S(1)}, u32[]{:S(2)}, u32[]{:S(2)}) collective-permute-start(f32[3,8,128]{2,1,0:T(8,128)S(1)} %get-tuple-element.51.refs_0_), channel_id=1, source_target_pairs={{0,3},{1,2},{2,1},{3,0},{4,7},{5,6},{6,5},{7,4},{8,11},{9,10},{10,... | collective-permute-start | bytes 36872 | tf_op jit(solution)/shard_map/ppermute | solution.py:472
  86.3 4.6 %collective-permute-start.18 = (f32[3,8,128]{2,1,0:T(8,128)S(1)}, f32[3,8,128]{2,1,0:T(8,128)S(1)}, u32[]{:S(2)}, u32[]{:S(2)}) collective-permute-start(f32[3,8,128]{2,1,0:T(8,128)S(1)} %get-tuple-element.51.refs_0_), channel_id=1, source_target_pairs={{0,2},{1,3},{2,0},{3,1},{4,6},{5,7},{6,4},{7,5},{8,10},{9,11},{10,... | collective-permute-start | bytes 36872 | tf_op jit(solution)/shard_map/ppermute | solution.py:472
  87.4 3.7 %collective-permute-start.17 = (f32[3,8,128]{2,1,0:T(8,128)S(1)}, f32[3,8,128]{2,1,0:T(8,128)S(1)}, u32[]{:S(2)}, u32[]{:S(2)}) collective-permute-start(f32[3,8,128]{2,1,0:T(8,128)S(1)} %get-tuple-element.51.refs_0_), channel_id=1, source_target_pairs={{0,1},{1,0},{2,3},{3,2},{4,5},{5,4},{6,7},{7,6},{8,9},{9,8},{10,11... | collective-permute-start | bytes 36872 | tf_op jit(solution)/shard_map/ppermute | solution.py:472
  (2 other events, 1.8 us)

commit v5 on v4

--- a/solution.py
+++ b/solution.py
@@ -18,6 +18,7 @@
 SCALE = 256.0
 GROUP = 16
 VMEM_LIMIT = 32 * 1024 * 1024
+CODE_LIMIT = 56 * 1024 * 1024
 
 
 def encode(scaled):
@@ -48,15 +49,25 @@
     return pl.BlockSpec(memory_space=pltpu.SMEM)
 
 
-def code_kernel(pop_ref, velocity_ref, all_ref, *group_refs):
-    bins = pop_ref.shape[0]
-    all_ref[pl.ds(bins, 3)] = velocity_ref[...]
+def code_kernel(pop_any, velocity_any, all_ref, *rest):
+    *group_refs, pop_ref, velocity_ref, sems = rest
+    bins, span_x = pop_ref.shape[:2]
+    copies = [
+        pltpu.make_async_copy(
+            pop_any.at[pl.ds(number * GROUP, GROUP)],
+            pop_ref.at[pl.ds(number * GROUP, GROUP)],
+            sems.at[number],
+        )
+        for number in range(len(group_refs))
+    ]
+    copies.append(pltpu.make_async_copy(velocity_any, velocity_ref, sems.at[len(group_refs)]))
+    for copy in copies:
+        copy.start()
     all_ref[pl.ds(bins + 3, GROUP - 3)] = jnp.zeros(
         (GROUP - 3,) + all_ref.shape[1:], jnp.bfloat16
     )
-    group_refs[0][pl.ds(GROUP, 3)] = velocity_ref[...]
-
     for number, group_ref in enumerate(group_refs):
+        copies[number].wait()
 
         def layer(x, carry, number=number, group_ref=group_ref):
             for index in range(0, GROUP, 4):
@@ -65,7 +76,10 @@
                 group_ref[pl.ds(index, 4), x] = code
             return carry
 
-        lax.fori_loop(0, pop_ref.shape[1], layer, 0)
+        lax.fori_loop(0, span_x, layer, 0)
+    copies[-1].wait()
+    group_refs[0][pl.ds(GROUP, 3)] = velocity_ref[...]
+    all_ref[pl.ds(bins, 3)] = velocity_ref[...]
 
 
 def coded_slab(population, velocity):
@@ -75,10 +89,15 @@
     sizes = [bins + GROUP, GROUP + 3] + [GROUP] * (groups - 1)
     return pl.pallas_call(
         code_kernel,
-        in_specs=[vmem_spec()] * 2,
+        in_specs=[pl.BlockSpec(memory_space=pltpu.HBM)] * 2,
         out_specs=[vmem_spec()] * len(sizes),
         out_shape=[jax.ShapeDtypeStruct((size,) + span, jnp.bfloat16) for size in sizes],
-        compiler_params=params(),
+        scratch_shapes=[
+            pltpu.VMEM(population.shape, jnp.float32),
+            pltpu.VMEM(velocity.shape, jnp.bfloat16),
+            pltpu.SemaphoreType.DMA((groups + 1,)),
+        ],
+        compiler_params=params(CODE_LIMIT),
         cost_estimate=cost(0, 6_000_000),
         name="code_slab",
     )(population, velocity)

time: 92.9 us -> 91.7 us (0.987)
  local copies, waits for them, and re-layouts: 3.67 us -> 0.9 us
  Pallas kernels: 44.2 us -> 45.8 us
    unnamed x12 -> x8, local copies, waits for them, and re-layouts: 3.67 us -> 0.9 us
    pallas_call x1, Pallas kernels: 2.47 us -> 4.01 us  [coded_slab(): pl.pallas_call(code_kernel, in_specs=[pl.BlockSpec(memory_space=pltpu.HBM...]
  transfers between devices with their start and end apart: 20 -> 20, of which waited for: 5 -> 5; matrix products, arithmetic and copies ran while one was open for 0% -> 0% of each run, Pallas kernels for 28% -> 29%
where the time goes in v5:
time: 91.7 us; the launch traced here: 91.1 us
  Pallas kernels  45.8 us (50%)
  starting transfers between devices  34.4 us (38%)
  waiting for transfers between devices  9.1 us (10%)
    ppermute x20, starting transfers between devices, swapped(): return lax.ppermute(array, axis, pairs)  34.4 us
    pallas_call x4, Pallas kernels, transported(): pl.pallas_call(functools.partial(transport_kernel, batches), grid=(1,), i...  21.8 us
    pallas_call x1, Pallas kernels, kinetics(): pl.pallas_call(functools.partial(kinetics_kernel, batches, groups, native...  14.4 us
    ppermute x20, waiting for transfers between devices, swapped(): return lax.ppermute(array, axis, pairs)  9.1 us
    pallas_call x1, Pallas kernels, coded_slab(): pl.pallas_call(code_kernel, in_specs=[pl.BlockSpec(memory_space=pltpu.HBM...  4.01 us
    pallas_call x1, Pallas kernels, unpacked(): pl.pallas_call(functools.partial(unpack_kernel, batches, groups), grid=(s...  2.03 us
  transfers between devices with their start and end apart: 20, of which 5 were waited for; matrix products, arithmetic and copies ran while one was open for 0% of the time, Pallas kernels for 29%

profile of v5, /device:TPU:2, one launch (start us, length us, event | category | flops | bytes accessed | tf_op | source)
XLA Modules:
  0.0 91.1 jit_solution(681548765288271823)
XLA Ops:
  0.6 4.0 %code_slab.1 = (bf16[80,3,32,128]{3,2,1,0:T(8,128)(2,1)}, bf16[19,3,32,128]{3,2,1,0:T(8,128)(2,1)}, bf16[16,3,32,128]{3,2,1,0:T(8,128)(2,1)}, bf16[16,3,32,128]{3,2,1,0:T(8,128)(2,1)}, bf16[16,3,32,128]{3,2,1,0:T(8,128)(2,1)}) custom-call(f32[64,3,32,128]{3,2,1,0:T(8,128)} %pop_ref.7, bf16[3,3,32,128]{3,2,1,0:T(8,128)(2,1)} %own_ref.1), custom_call_target="tpu_custom_call" | custom-call | bytes 6000000 | tf_op jit(solution)/shard_map/code_slab/pallas_call | solution.py:90
  4.7 1.9 %collective-permute-start.2 = (bf16[19,3,32,128]{3,2,1,0:T(8,128)(2,1)}, bf16[19,3,32,128]{3,2,1,0:T(8,128)(2,1)}, u32[]{:S(2)}, u32[]{:S(2)}) collective-permute-start(bf16[19,3,32,128]{3,2,1,0:T(8,128)(2,1)} %get-tuple-element.31), channel_id=1, source_target_pairs={{4,8},{8,4},{12,16},{16,12},{20,24},{24,20},{5,9},{9,5},{13,17},{1... | collective-permute-start | bytes 1400840 | tf_op jit(solution)/shard_map/ppermute | solution.py:491
  6.7 3.6 %collective-permute-start.4 = (bf16[16,3,32,128]{3,2,1,0:T(8,128)(2,1)}, bf16[16,3,32,128]{3,2,1,0:T(8,128)(2,1)S(1)}, u32[]{:S(2)}, u32[]{:S(2)}) collective-permute-start(bf16[16,3,32,128]{3,2,1,0:T(8,128)(2,1)} %get-tuple-element.33), channel_id=1, source_target_pairs={{4,8},{8,4},{12,16},{16,12},{20,24},{24,20},{5,9},{9,5},{13,17},{1... | collective-permute-start | bytes 1179656 | tf_op jit(solution)/shard_map/ppermute | solution.py:491
  10.3 1.9 %collective-permute-start.3 = (bf16[16,3,32,128]{3,2,1,0:T(8,128)(2,1)}, bf16[16,3,32,128]{3,2,1,0:T(8,128)(2,1)}, u32[]{:S(2)}, u32[]{:S(2)}) collective-permute-start(bf16[16,3,32,128]{3,2,1,0:T(8,128)(2,1)} %get-tuple-element.32), channel_id=1, source_target_pairs={{4,8},{8,4},{12,16},{16,12},{20,24},{24,20},{5,9},{9,5},{13,17},{1... | collective-permute-start | bytes 1179656 | tf_op jit(solution)/shard_map/ppermute | solution.py:491
  12.2 3.6 %collective-permute-start.1 = (bf16[16,3,32,128]{3,2,1,0:T(8,128)(2,1)}, bf16[16,3,32,128]{3,2,1,0:T(8,128)(2,1)}, u32[]{:S(2)}, u32[]{:S(2)}) collective-permute-start(bf16[16,3,32,128]{3,2,1,0:T(8,128)(2,1)} %get-tuple-element.30), channel_id=1, source_target_pairs={{4,8},{8,4},{12,16},{16,12},{20,24},{24,20},{5,9},{9,5},{13,17},{1... | collective-permute-start | bytes 1179656 | tf_op jit(solution)/shard_map/ppermute | solution.py:491
  16.0 1.2 %collective-permute-done.2.outside_ref = bf16[19,3,32,128]{3,2,1,0:T(8,128)(2,1)} collective-permute-done((bf16[19,3,32,128]{3,2,1,0:T(8,128)(2,1)}, bf16[19,3,32,128]{3,2,1,0:T(8,128)(2,1)}, u32[]{:S(2)}, u32[]{:S(2)}) %collective-permute-start.2) | collective-permute-done | bytes 466976 | tf_op jit(solution)/shard_map/ppermute | solution.py:491
  18.1 1.7 %weights.1.coef_ref = f32[7,7,32,128]{3,2,1,0:T(8,128)S(1)} custom-call(s32[2]{0:T(128)S(1)} %pad_add_fusion.place_ref, bf16[3,3,32,128]{3,2,1,0:T(8,128)(2,1)S(1)} %copy-done.1, bf16[80,3,32,128]{3,2,1,0:T(8,128)(2,1)} %collective-permute-done.inside_ref, bf16[19,3,32,128]{3,2,1,0:T(8,128)(2,1)} %collective-permute-done.2.outside_ref), custom_call_target="tpu_custom_call" | custom-call | bytes 4000000 | tf_op jit(solution)/shard_map/weights/pallas_call | solution.py:145
  19.8 5.5 %transport.4 = (bf16[3,8,16,128]{3,2,1,0:T(8,128)(2,1)S(1)}, bf16[3,8,16,128]{3,2,1,0:T(8,128)(2,1)S(1)}, bf16[3,8,16,128]{3,2,1,0:T(8,128)(2,1)S(1)}, bf16[3,8,16,128]{3,2,1,0:T(8,128)(2,1)S(1)}) custom-call(s32[2]{0:T(128)S(1)} %pad_add_fusion.place_ref, f32[64,3,32,128]{3,2,1,0:T(8,128)S(1)} %copy-done, ...), custom_call_target="tpu_custom_call" | custom-call | bytes 18000000 | tf_op jit(solution)/shard_map/transport/pallas_call | solution.py:226
  25.3 2.8 %collective-permute-start.5 = (bf16[3,8,16,128]{3,2,1,0:T(8,128)(2,1)S(1)}, bf16[3,8,16,128]{3,2,1,0:T(8,128)(2,1)S(1)}, u32[]{:S(2)}, u32[]{:S(2)}) collective-permute-start(bf16[3,8,16,128]{3,2,1,0:T(8,128)(2,1)S(1)} %get-tuple-element.36), channel_id=1, source_target_pairs={{0,1},{1,0},{2,3},{3,2},{4,5},{5,4},{6,7},{7,6},{8,9},{9,8},{10,11... | collective-permute-start | bytes 294920 | tf_op jit(solution)/shard_map/ppermute | solution.py:491
  28.1 2.6 %collective-permute-start.6 = (bf16[3,8,16,128]{3,2,1,0:T(8,128)(2,1)S(1)}, bf16[3,8,16,128]{3,2,1,0:T(8,128)(2,1)S(1)}, u32[]{:S(2)}, u32[]{:S(2)}) collective-permute-start(bf16[3,8,16,128]{3,2,1,0:T(8,128)(2,1)S(1)} %get-tuple-element.37), channel_id=1, source_target_pairs={{0,2},{1,3},{2,0},{3,1},{4,6},{5,7},{6,4},{7,5},{8,10},{9,11},{10,... | collective-permute-start | bytes 294920 | tf_op jit(solution)/shard_map/ppermute | solution.py:491
  30.7 5.4 %transport.5 = (bf16[3,8,16,128]{3,2,1,0:T(8,128)(2,1)S(1)}, bf16[3,8,16,128]{3,2,1,0:T(8,128)(2,1)S(1)}, bf16[3,8,16,128]{3,2,1,0:T(8,128)(2,1)S(1)}, bf16[3,8,16,128]{3,2,1,0:T(8,128)(2,1)S(1)}) custom-call(s32[2]{0:T(128)S(1)} %pad_add_fusion.place_ref, f32[64,3,32,128]{3,2,1,0:T(8,128)S(1)} %copy-done, ...), custom_call_target="tpu_custom_call" | custom-call | bytes 18000000 | tf_op jit(solution)/shard_map/transport/pallas_call | solution.py:226
  37.0 3.5 %collective-permute-start.9 = (bf16[3,8,16,128]{3,2,1,0:T(8,128)(2,1)S(1)}, bf16[3,8,16,128]{3,2,1,0:T(8,128)(2,1)S(1)}, u32[]{:S(2)}, u32[]{:S(2)}) collective-permute-start(bf16[3,8,16,128]{3,2,1,0:T(8,128)(2,1)S(1)} %get-tuple-element.41), channel_id=1, source_target_pairs={{0,2},{1,3},{2,0},{3,1},{4,6},{5,7},{6,4},{7,5},{8,10},{9,11},{10,... | collective-permute-start | bytes 294920 | tf_op jit(solution)/shard_map/ppermute | solution.py:491
  40.5 5.5 %transport.6 = (bf16[3,8,16,128]{3,2,1,0:T(8,128)(2,1)S(1)}, bf16[3,8,16,128]{3,2,1,0:T(8,128)(2,1)S(1)}, bf16[3,8,16,128]{3,2,1,0:T(8,128)(2,1)S(1)}, bf16[3,8,16,128]{3,2,1,0:T(8,128)(2,1)S(1)}) custom-call(s32[2]{0:T(128)S(1)} %pad_add_fusion.place_ref, f32[64,3,32,128]{3,2,1,0:T(8,128)S(1)} %copy-done, ...), custom_call_target="tpu_custom_call" | custom-call | bytes 18000000 | tf_op jit(solution)/shard_map/transport/pallas_call | solution.py:226
  46.7 3.8 %collective-permute-start.15 = (bf16[3,8,16,128]{3,2,1,0:T(8,128)(2,1)S(1)}, bf16[3,8,16,128]{3,2,1,0:T(8,128)(2,1)S(1)}, u32[]{:S(2)}, u32[]{:S(2)}) collective-permute-start(bf16[3,8,16,128]{3,2,1,0:T(8,128)(2,1)S(1)} %get-tuple-element.48), channel_id=1, source_target_pairs={{0,2},{1,3},{2,0},{3,1},{4,6},{5,7},{6,4},{7,5},{8,10},{9,11},{10,... | collective-permute-start | bytes 294920 | tf_op jit(solution)/shard_map/ppermute | solution.py:491
  50.5 5.5 %transport.7 = (bf16[3,8,16,128]{3,2,1,0:T(8,128)(2,1)S(1)}, bf16[3,8,16,128]{3,2,1,0:T(8,128)(2,1)S(1)}, bf16[3,8,16,128]{3,2,1,0:T(8,128)(2,1)S(1)}, bf16[3,8,16,128]{3,2,1,0:T(8,128)(2,1)S(1)}) custom-call(s32[2]{0:T(128)S(1)} %pad_add_fusion.place_ref, f32[64,3,32,128]{3,2,1,0:T(8,128)S(1)} %copy-done, ...), custom_call_target="tpu_custom_call" | custom-call | bytes 18000000 | tf_op jit(solution)/shard_map/transport/pallas_call | solution.py:226
  56.7 3.8 %collective-permute-start.12 = (bf16[3,8,16,128]{3,2,1,0:T(8,128)(2,1)S(1)}, bf16[3,8,16,128]{3,2,1,0:T(8,128)(2,1)S(1)}, u32[]{:S(2)}, u32[]{:S(2)}) collective-permute-start(bf16[3,8,16,128]{3,2,1,0:T(8,128)(2,1)S(1)} %get-tuple-element.45), channel_id=1, source_target_pairs={{0,2},{1,3},{2,0},{3,1},{4,6},{5,7},{6,4},{7,5},{8,10},{9,11},{10,... | collective-permute-start | bytes 294920 | tf_op jit(solution)/shard_map/ppermute | solution.py:491
  61.2 2.0 %unpack.1.rest_4_ = f32[3,2048,128]{2,1,0:T(8,128)S(1)} custom-call(s32[2]{0:T(128)S(1)} %pad_add_fusion.place_ref, bf16[3,8,16,128]{3,2,1,0:T(8,128)(2,1)S(1)} %get-tuple-element.34.rest_0_.refs_0_, bf16[3,8,16,128]{3,2,1,0:T(8,128)(2,1)S(1)} %get-tuple-element.35.rest_0_.refs_1_, bf16[3,8,16,128]{3,2,1,0:T(8,128)(2,1)S(1)} %get-tuple-element.39.rest_0_.refs_2_, ...), custom_call_target="tpu_custom_call" | custom-call | bytes 12000000 | tf_op jit(solution)/shard_map/unpack/pallas_call | solution.py:317
  63.3 5.0 %collective-permute-done.12.rest_2_ = bf16[3,8,16,128]{3,2,1,0:T(8,128)(2,1)S(1)} collective-permute-done((bf16[3,8,16,128]{3,2,1,0:T(8,128)(2,1)S(1)}, bf16[3,8,16,128]{3,2,1,0:T(8,128)(2,1)S(1)}, u32[]{:S(2)}, u32[]{:S(2)}) %collective-permute-start.12) | collective-permute-done | bytes 98336 | tf_op jit(solution)/shard_map/ppermute | solution.py:491
  68.3 14.4 %kinetics.1 = (f32[256,3,8,128]{3,2,1,0:T(8,128)}, f32[3,8,128]{2,1,0:T(8,128)S(1)}) custom-call(s32[2]{0:T(128)S(1)} %pad_add_fusion.place_ref, f32[3,8,128]{2,1,0:T(8,128)S(1)} %copy-done.2, bf16[256,256]{1,0:T(8,128)(2,1)S(1)} %get-tuple-element.27.toeplitz_ref, f32[256,128]{1,0:T(8,128)S(1)} %get-tuple-element.28.column_ref, ...), custom_call_target="tpu_custom_call" | custom-call | bytes 50000000 | tf_op jit(solution)/shard_map/kinetics/pallas_call | solution.py:448
  82.7 2.5 %collective-permute-start.19 = (f32[3,8,128]{2,1,0:T(8,128)S(1)}, f32[3,8,128]{2,1,0:T(8,128)S(1)}, u32[]{:S(2)}, u32[]{:S(2)}) collective-permute-start(f32[3,8,128]{2,1,0:T(8,128)S(1)} %get-tuple-element.51.refs_0_), channel_id=1, source_target_pairs={{0,3},{1,2},{2,1},{3,0},{4,7},{5,6},{6,5},{7,4},{8,11},{9,10},{10,... | collective-permute-start | bytes 36872 | tf_op jit(solution)/shard_map/ppermute | solution.py:491
  85.1 1.1 %collective-permute-start.18 = (f32[3,8,128]{2,1,0:T(8,128)S(1)}, f32[3,8,128]{2,1,0:T(8,128)S(1)}, u32[]{:S(2)}, u32[]{:S(2)}) collective-permute-start(f32[3,8,128]{2,1,0:T(8,128)S(1)} %get-tuple-element.51.refs_0_), channel_id=1, source_target_pairs={{0,2},{1,3},{2,0},{3,1},{4,6},{5,7},{6,4},{7,5},{8,10},{9,11},{10,... | collective-permute-start | bytes 36872 | tf_op jit(solution)/shard_map/ppermute | solution.py:491
  87.0 1.1 %collective-permute-done.19.refs_3_ = f32[3,8,128]{2,1,0:T(8,128)S(1)} collective-permute-done((f32[3,8,128]{2,1,0:T(8,128)S(1)}, f32[3,8,128]{2,1,0:T(8,128)S(1)}, u32[]{:S(2)}, u32[]{:S(2)}) %collective-permute-start.19) | collective-permute-done | bytes 12320 | tf_op jit(solution)/shard_map/ppermute | solution.py:491
  88.1 1.6 %collective-permute-done.18.refs_2_ = f32[3,8,128]{2,1,0:T(8,128)S(1)} collective-permute-done((f32[3,8,128]{2,1,0:T(8,128)S(1)}, f32[3,8,128]{2,1,0:T(8,128)S(1)}, u32[]{:S(2)}, u32[]{:S(2)}) %collective-permute-start.18) | collective-permute-done | bytes 12320 | tf_op jit(solution)/shard_map/ppermute | solution.py:491
  89.9 1.2 %assemble.1 = f32[3,4,8,128]{3,2,1,0:T(8,128)} custom-call(s32[2]{0:T(128)S(1)} %pad_add_fusion.place_ref, f32[3,8,128]{2,1,0:T(8,128)S(1)} %get-tuple-element.51.refs_0_, f32[3,8,128]{2,1,0:T(8,128)S(1)} %collective-permute-done.17.refs_1_, f32[3,8,128]{2,1,0:T(8,128)S(1)} %collective-permute-done.18.refs_2_, f32[3,8,128]{2,1,0:T(8,128)S(1)} %collective-permute-done.19.refs_3_), custom_call_target="tpu_custom_call" | custom-call | tf_op jit(solution)/shard_map/assemble/pallas_call | solution.py:477
  (36 shorter events, 5.1 us)
Async XLA Ops:
  0.6 19.2 %copy-start = (f32[64,3,32,128]{3,2,1,0:T(8,128)S(1)}, f32[64,3,32,128]{3,2,1,0:T(8,128)}, u32[]{:S(2)}) copy-start(f32[64,3,32,128]{3,2,1,0:T(8,128)} %pop_ref.7) | copy-start | bytes 9437188
  4.7 12.5 %collective-permute-start = (bf16[80,3,32,128]{3,2,1,0:T(8,128)(2,1)}, bf16[80,3,32,128]{3,2,1,0:T(8,128)(2,1)}, u32[]{:S(2)}, u32[]{:S(2)}) collective-permute-start(bf16[80,3,32,128]{3,2,1,0:T(8,128)(2,1)} %get-tuple-element.29), channel_id=1, source_target_pairs={{0,4},{4,0},{8,12},{12,8},{16,20},{20,16},{24,28},{28,24},{1,5},{5... | collective-permute-start | bytes 5898248 | tf_op jit(solution)/shard_map/ppermute | solution.py:491
  4.7 12.4 %collective-permute-start.2 = (bf16[19,3,32,128]{3,2,1,0:T(8,128)(2,1)}, bf16[19,3,32,128]{3,2,1,0:T(8,128)(2,1)}, u32[]{:S(2)}, u32[]{:S(2)}) collective-permute-start(bf16[19,3,32,128]{3,2,1,0:T(8,128)(2,1)} %get-tuple-element.31), channel_id=1, source_target_pairs={{4,8},{8,4},{12,16},{16,12},{20,24},{24,20},{5,9},{9,5},{13,17},{1... | collective-permute-start | bytes 1400840 | tf_op jit(solution)/shard_map/ppermute | solution.py:491
  6.7 24.0 %collective-permute-start.4 = (bf16[16,3,32,128]{3,2,1,0:T(8,128)(2,1)}, bf16[16,3,32,128]{3,2,1,0:T(8,128)(2,1)S(1)}, u32[]{:S(2)}, u32[]{:S(2)}) collective-permute-start(bf16[16,3,32,128]{3,2,1,0:T(8,128)(2,1)} %get-tuple-element.33), channel_id=1, source_target_pairs={{4,8},{8,4},{12,16},{16,12},{20,24},{24,20},{5,9},{9,5},{13,17},{1... | collective-permute-start | bytes 1179656 | tf_op jit(solution)/shard_map/ppermute | solution.py:491
  10.3 25.8 %collective-permute-start.3 = (bf16[16,3,32,128]{3,2,1,0:T(8,128)(2,1)}, bf16[16,3,32,128]{3,2,1,0:T(8,128)(2,1)}, u32[]{:S(2)}, u32[]{:S(2)}) collective-permute-start(bf16[16,3,32,128]{3,2,1,0:T(8,128)(2,1)} %get-tuple-element.32), channel_id=1, source_target_pairs={{4,8},{8,4},{12,16},{16,12},{20,24},{24,20},{5,9},{9,5},{13,17},{1... | collective-permute-start | bytes 1179656 | tf_op jit(solution)/shard_map/ppermute | solution.py:491
  12.2 34.5 %collective-permute-start.1 = (bf16[16,3,32,128]{3,2,1,0:T(8,128)(2,1)}, bf16[16,3,32,128]{3,2,1,0:T(8,128)(2,1)}, u32[]{:S(2)}, u32[]{:S(2)}) collective-permute-start(bf16[16,3,32,128]{3,2,1,0:T(8,128)(2,1)} %get-tuple-element.30), channel_id=1, source_target_pairs={{4,8},{8,4},{12,16},{16,12},{20,24},{24,20},{5,9},{9,5},{13,17},{1... | collective-permute-start | bytes 1179656 | tf_op jit(solution)/shard_map/ppermute | solution.py:491
  17.2 0.9 copy-start.1
  25.3 11.8 %collective-permute-start.5 = (bf16[3,8,16,128]{3,2,1,0:T(8,128)(2,1)S(1)}, bf16[3,8,16,128]{3,2,1,0:T(8,128)(2,1)S(1)}, u32[]{:S(2)}, u32[]{:S(2)}) collective-permute-start(bf16[3,8,16,128]{3,2,1,0:T(8,128)(2,1)S(1)} %get-tuple-element.36), channel_id=1, source_target_pairs={{0,1},{1,0},{2,3},{3,2},{4,5},{5,4},{6,7},{7,6},{8,9},{9,8},{10,11... | collective-permute-start | bytes 294920 | tf_op jit(solution)/shard_map/ppermute | solution.py:491
  28.1 12.4 %collective-permute-start.6 = (bf16[3,8,16,128]{3,2,1,0:T(8,128)(2,1)S(1)}, bf16[3,8,16,128]{3,2,1,0:T(8,128)(2,1)S(1)}, u32[]{:S(2)}, u32[]{:S(2)}) collective-permute-start(bf16[3,8,16,128]{3,2,1,0:T(8,128)(2,1)S(1)} %get-tuple-element.37), channel_id=1, source_target_pairs={{0,2},{1,3},{2,0},{3,1},{4,6},{5,7},{6,4},{7,5},{8,10},{9,11},{10,... | collective-permute-start | bytes 294920 | tf_op jit(solution)/shard_map/ppermute | solution.py:491
  30.7 9.8 %collective-permute-start.7 = (bf16[3,8,16,128]{3,2,1,0:T(8,128)(2,1)S(1)}, bf16[3,8,16,128]{3,2,1,0:T(8,128)(2,1)S(1)}, u32[]{:S(2)}, u32[]{:S(2)}) collective-permute-start(bf16[3,8,16,128]{3,2,1,0:T(8,128)(2,1)S(1)} %get-tuple-element.38), channel_id=1, source_target_pairs={{0,3},{1,2},{2,1},{3,0},{4,7},{5,6},{6,5},{7,4},{8,11},{9,10},{10,... | collective-permute-start | bytes 294920 | tf_op jit(solution)/shard_map/ppermute | solution.py:491
  36.1 14.4 %collective-permute-start.8 = (bf16[3,8,16,128]{3,2,1,0:T(8,128)(2,1)S(1)}, bf16[3,8,16,128]{3,2,1,0:T(8,128)(2,1)S(1)}, u32[]{:S(2)}, u32[]{:S(2)}) collective-permute-start(bf16[3,8,16,128]{3,2,1,0:T(8,128)(2,1)S(1)} %get-tuple-element.40), channel_id=1, source_target_pairs={{0,1},{1,0},{2,3},{3,2},{4,5},{5,4},{6,7},{7,6},{8,9},{9,8},{10,11... | collective-permute-start | bytes 294920 | tf_op jit(solution)/shard_map/ppermute | solution.py:491
  37.0 13.4 %collective-permute-start.9 = (bf16[3,8,16,128]{3,2,1,0:T(8,128)(2,1)S(1)}, bf16[3,8,16,128]{3,2,1,0:T(8,128)(2,1)S(1)}, u32[]{:S(2)}, u32[]{:S(2)}) collective-permute-start(bf16[3,8,16,128]{3,2,1,0:T(8,128)(2,1)S(1)} %get-tuple-element.41), channel_id=1, source_target_pairs={{0,2},{1,3},{2,0},{3,1},{4,6},{5,7},{6,4},{7,5},{8,10},{9,11},{10,... | collective-permute-start | bytes 294920 | tf_op jit(solution)/shard_map/ppermute | solution.py:491
  40.5 10.0 %collective-permute-start.10 = (bf16[3,8,16,128]{3,2,1,0:T(8,128)(2,1)S(1)}, bf16[3,8,16,128]{3,2,1,0:T(8,128)(2,1)S(1)}, u32[]{:S(2)}, u32[]{:S(2)}) collective-permute-start(bf16[3,8,16,128]{3,2,1,0:T(8,128)(2,1)S(1)} %get-tuple-element.42), channel_id=1, source_target_pairs={{0,3},{1,2},{2,1},{3,0},{4,7},{5,6},{6,5},{7,4},{8,11},{9,10},{10,... | collective-permute-start | bytes 294920 | tf_op jit(solution)/shard_map/ppermute | solution.py:491
  46.0 14.4 %collective-permute-start.14 = (bf16[3,8,16,128]{3,2,1,0:T(8,128)(2,1)S(1)}, bf16[3,8,16,128]{3,2,1,0:T(8,128)(2,1)S(1)}, u32[]{:S(2)}, u32[]{:S(2)}) collective-permute-start(bf16[3,8,16,128]{3,2,1,0:T(8,128)(2,1)S(1)} %get-tuple-element.47), channel_id=1, source_target_pairs={{0,1},{1,0},{2,3},{3,2},{4,5},{5,4},{6,7},{7,6},{8,9},{9,8},{10,11... | collective-permute-start | bytes 294920 | tf_op jit(solution)/shard_map/ppermute | solution.py:491
  46.7 14.5 %collective-permute-start.15 = (bf16[3,8,16,128]{3,2,1,0:T(8,128)(2,1)S(1)}, bf16[3,8,16,128]{3,2,1,0:T(8,128)(2,1)S(1)}, u32[]{:S(2)}, u32[]{:S(2)}) collective-permute-start(bf16[3,8,16,128]{3,2,1,0:T(8,128)(2,1)S(1)} %get-tuple-element.48), channel_id=1, source_target_pairs={{0,2},{1,3},{2,0},{3,1},{4,6},{5,7},{6,4},{7,5},{8,10},{9,11},{10,... | collective-permute-start | bytes 294920 | tf_op jit(solution)/shard_map/ppermute | solution.py:491
  50.5 10.7 %collective-permute-start.16 = (bf16[3,8,16,128]{3,2,1,0:T(8,128)(2,1)S(1)}, bf16[3,8,16,128]{3,2,1,0:T(8,128)(2,1)S(1)}, u32[]{:S(2)}, u32[]{:S(2)}) collective-permute-start(bf16[3,8,16,128]{3,2,1,0:T(8,128)(2,1)S(1)} %get-tuple-element.49), channel_id=1, source_target_pairs={{0,3},{1,2},{2,1},{3,0},{4,7},{5,6},{6,5},{7,4},{8,11},{9,10},{10,... | collective-permute-start | bytes 294920 | tf_op jit(solution)/shard_map/ppermute | solution.py:491
  50.5 10.0 %copy-start.3 = (f32[256]{0:T(256)S(1)}, f32[256]{0:T(256)}, u32[]{:S(2)}) copy-start(f32[256]{0:T(256)} %param.7) | copy-start | bytes 3076
  56.0 12.3 %copy-start.2 = (f32[3,8,128]{2,1,0:T(8,128)S(1)}, f32[3,8,128]{2,1,0:T(8,128)}, u32[]{:S(2)}) copy-start(f32[3,8,128]{2,1,0:T(8,128)} %supersat_ref.1) | copy-start | bytes 36868
  56.0 7.2 %collective-permute-start.11 = (bf16[3,8,16,128]{3,2,1,0:T(8,128)(2,1)S(1)}, bf16[3,8,16,128]{3,2,1,0:T(8,128)(2,1)S(1)}, u32[]{:S(2)}, u32[]{:S(2)}) collective-permute-start(bf16[3,8,16,128]{3,2,1,0:T(8,128)(2,1)S(1)} %get-tuple-element.44), channel_id=1, source_target_pairs={{0,1},{1,0},{2,3},{3,2},{4,5},{5,4},{6,7},{7,6},{8,9},{9,8},{10,11... | collective-permute-start | bytes 294920 | tf_op jit(solution)/shard_map/ppermute | solution.py:491
  56.7 11.6 %collective-permute-start.12 = (bf16[3,8,16,128]{3,2,1,0:T(8,128)(2,1)S(1)}, bf16[3,8,16,128]{3,2,1,0:T(8,128)(2,1)S(1)}, u32[]{:S(2)}, u32[]{:S(2)}) collective-permute-start(bf16[3,8,16,128]{3,2,1,0:T(8,128)(2,1)S(1)} %get-tuple-element.45), channel_id=1, source_target_pairs={{0,2},{1,3},{2,0},{3,1},{4,6},{5,7},{6,4},{7,5},{8,10},{9,11},{10,... | collective-permute-start | bytes 294920 | tf_op jit(solution)/shard_map/ppermute | solution.py:491
  60.5 7.8 %collective-permute-start.13 = (bf16[3,8,16,128]{3,2,1,0:T(8,128)(2,1)S(1)}, bf16[3,8,16,128]{3,2,1,0:T(8,128)(2,1)S(1)}, u32[]{:S(2)}, u32[]{:S(2)}) collective-permute-start(bf16[3,8,16,128]{3,2,1,0:T(8,128)(2,1)S(1)} %get-tuple-element.46), channel_id=1, source_target_pairs={{0,3},{1,2},{2,1},{3,0},{4,7},{5,6},{6,5},{7,4},{8,11},{9,10},{10,... | collective-permute-start | bytes 294920 | tf_op jit(solution)/shard_map/ppermute | solution.py:491
  82.7 5.5 %collective-permute-start.19 = (f32[3,8,128]{2,1,0:T(8,128)S(1)}, f32[3,8,128]{2,1,0:T(8,128)S(1)}, u32[]{:S(2)}, u32[]{:S(2)}) collective-permute-start(f32[3,8,128]{2,1,0:T(8,128)S(1)} %get-tuple-element.51.refs_0_), channel_id=1, source_target_pairs={{0,3},{1,2},{2,1},{3,0},{4,7},{5,6},{6,5},{7,4},{8,11},{9,10},{10,... | collective-permute-start | bytes 36872 | tf_op jit(solution)/shard_map/ppermute | solution.py:491
  85.1 4.6 %collective-permute-start.18 = (f32[3,8,128]{2,1,0:T(8,128)S(1)}, f32[3,8,128]{2,1,0:T(8,128)S(1)}, u32[]{:S(2)}, u32[]{:S(2)}) collective-permute-start(f32[3,8,128]{2,1,0:T(8,128)S(1)} %get-tuple-element.51.refs_0_), channel_id=1, source_target_pairs={{0,2},{1,3},{2,0},{3,1},{4,6},{5,7},{6,4},{7,5},{8,10},{9,11},{10,... | collective-permute-start | bytes 36872 | tf_op jit(solution)/shard_map/ppermute | solution.py:491
  86.2 3.7 %collective-permute-start.17 = (f32[3,8,128]{2,1,0:T(8,128)S(1)}, f32[3,8,128]{2,1,0:T(8,128)S(1)}, u32[]{:S(2)}, u32[]{:S(2)}) collective-permute-start(f32[3,8,128]{2,1,0:T(8,128)S(1)} %get-tuple-element.51.refs_0_), channel_id=1, source_target_pairs={{0,1},{1,0},{2,3},{3,2},{4,5},{5,4},{6,7},{7,6},{8,9},{9,8},{10,11... | collective-permute-start | bytes 36872 | tf_op jit(solution)/shard_map/ppermute | solution.py:491

commit v6 on v5

--- a/solution.py
+++ b/solution.py
@@ -213,6 +213,12 @@
     for ahead in range(batches):
         begin = lax.bitwise_xor(place_ref[0], ahead) * span_out
         for x in range(span_x):
+            if span_out == 8:
+                begin = pl.multiple_of(begin, 8)
+                turned = jnp.swapaxes(last[x, :, pl.ds(begin, span_out)], 0, 1)
+                for y in range(span_out):
+                    outs[ahead][x, y] = encode(turned[y])
+                continue
             for y in range(span_out):
                 at = x * bins * span_y + begin + y
                 outs[ahead][x, y] = encode(rows[pl.ds(at, bins, stride=span_y), :])
@@ -425,13 +431,14 @@
     )
     for y in range(span_y):
         depletion_ref[0, pl.ds(y, 1), :] = mass(y) - depletion_ref[0, pl.ds(y, 1), :]
+    for row in range(run):
+        values = [state[pl.ds(y * bin_count + 8 * row, 8), :] for y in range(span_y)]
         if native:
-            rows = out_ref.reshape(bin_count * span_y, span_z)
-        for row in range(run):
-            value = state[pl.ds(y * bin_count + 8 * row, 8), :]
-            if native:
-                rows[pl.ds(row * span_y + y, 8, stride=run * span_y), :] = value
-            else:
+            turned = jnp.swapaxes(jnp.stack(values), 0, 1)
+            for index in range(8):
+                out_ref[index * run + row, 0] = turned[index]
+        else:
+            for y, value in enumerate(values):
                 out_ref[0, y, pl.ds(row, 8, stride=run), :] = value
 
 

time: 91.7 us -> 89.8 us (0.979)
  Pallas kernels: 45.8 us -> 43.9 us
    pallas_call x1, Pallas kernels: 14.4 us -> 13.2 us  [kinetics(): pl.pallas_call(functools.partial(kinetics_kernel, batches, groups, native...]
where the time goes in v6:
time: 89.8 us; the launch traced here: 89.3 us
  Pallas kernels  43.9 us (49%)
  starting transfers between devices  34.4 us (38%)
  waiting for transfers between devices  9.2 us (10%)
  local copies, waits for them, and re-layouts  0.9 us (1%)
    ppermute x20, starting transfers between devices, swapped(): return lax.ppermute(array, axis, pairs)  34.4 us
    pallas_call x4, Pallas kernels, transported(): pl.pallas_call(functools.partial(transport_kernel, batches), grid=(1,), i...  21 us
    pallas_call x1, Pallas kernels, kinetics(): pl.pallas_call(functools.partial(kinetics_kernel, batches, groups, native...  13.2 us
    ppermute x20, waiting for transfers between devices, swapped(): return lax.ppermute(array, axis, pairs)  9.2 us
    pallas_call x1, Pallas kernels, coded_slab(): pl.pallas_call(code_kernel, in_specs=[pl.BlockSpec(memory_space=pltpu.HBM...  4.01 us
    pallas_call x1, Pallas kernels, unpacked(): pl.pallas_call(functools.partial(unpack_kernel, batches, groups), grid=(s...  2.03 us
  transfers between devices with their start and end apart: 20, of which 5 were waited for; matrix products, arithmetic and copies ran while one was open for 0% of the time, Pallas kernels for 29%

profile of v6, /device:TPU:2, one launch (start us, length us, event | category | flops | bytes accessed | tf_op | source)
XLA Modules:
  0.0 89.3 jit_solution(14118533104576704099)
XLA Ops:
  0.6 4.0 %code_slab.1 = (bf16[80,3,32,128]{3,2,1,0:T(8,128)(2,1)}, bf16[19,3,32,128]{3,2,1,0:T(8,128)(2,1)}, bf16[16,3,32,128]{3,2,1,0:T(8,128)(2,1)}, bf16[16,3,32,128]{3,2,1,0:T(8,128)(2,1)}, bf16[16,3,32,128]{3,2,1,0:T(8,128)(2,1)}) custom-call(f32[64,3,32,128]{3,2,1,0:T(8,128)} %pop_ref.7, bf16[3,3,32,128]{3,2,1,0:T(8,128)(2,1)} %own_ref.1), custom_call_target="tpu_custom_call" | custom-call | bytes 6000000 | tf_op jit(solution)/shard_map/code_slab/pallas_call | solution.py:90
  4.7 1.9 %collective-permute-start.2 = (bf16[19,3,32,128]{3,2,1,0:T(8,128)(2,1)}, bf16[19,3,32,128]{3,2,1,0:T(8,128)(2,1)}, u32[]{:S(2)}, u32[]{:S(2)}) collective-permute-start(bf16[19,3,32,128]{3,2,1,0:T(8,128)(2,1)} %get-tuple-element.31), channel_id=1, source_target_pairs={{4,8},{8,4},{12,16},{16,12},{20,24},{24,20},{5,9},{9,5},{13,17},{1... | collective-permute-start | bytes 1400840 | tf_op jit(solution)/shard_map/ppermute | solution.py:498
  6.7 3.6 %collective-permute-start.4 = (bf16[16,3,32,128]{3,2,1,0:T(8,128)(2,1)}, bf16[16,3,32,128]{3,2,1,0:T(8,128)(2,1)S(1)}, u32[]{:S(2)}, u32[]{:S(2)}) collective-permute-start(bf16[16,3,32,128]{3,2,1,0:T(8,128)(2,1)} %get-tuple-element.33), channel_id=1, source_target_pairs={{4,8},{8,4},{12,16},{16,12},{20,24},{24,20},{5,9},{9,5},{13,17},{1... | collective-permute-start | bytes 1179656 | tf_op jit(solution)/shard_map/ppermute | solution.py:498
  10.3 1.9 %collective-permute-start.3 = (bf16[16,3,32,128]{3,2,1,0:T(8,128)(2,1)}, bf16[16,3,32,128]{3,2,1,0:T(8,128)(2,1)}, u32[]{:S(2)}, u32[]{:S(2)}) collective-permute-start(bf16[16,3,32,128]{3,2,1,0:T(8,128)(2,1)} %get-tuple-element.32), channel_id=1, source_target_pairs={{4,8},{8,4},{12,16},{16,12},{20,24},{24,20},{5,9},{9,5},{13,17},{1... | collective-permute-start | bytes 1179656 | tf_op jit(solution)/shard_map/ppermute | solution.py:498
  12.2 3.6 %collective-permute-start.1 = (bf16[16,3,32,128]{3,2,1,0:T(8,128)(2,1)}, bf16[16,3,32,128]{3,2,1,0:T(8,128)(2,1)}, u32[]{:S(2)}, u32[]{:S(2)}) collective-permute-start(bf16[16,3,32,128]{3,2,1,0:T(8,128)(2,1)} %get-tuple-element.30), channel_id=1, source_target_pairs={{4,8},{8,4},{12,16},{16,12},{20,24},{24,20},{5,9},{9,5},{13,17},{1... | collective-permute-start | bytes 1179656 | tf_op jit(solution)/shard_map/ppermute | solution.py:498
  16.0 1.2 %collective-permute-done.2.outside_ref = bf16[19,3,32,128]{3,2,1,0:T(8,128)(2,1)} collective-permute-done((bf16[19,3,32,128]{3,2,1,0:T(8,128)(2,1)}, bf16[19,3,32,128]{3,2,1,0:T(8,128)(2,1)}, u32[]{:S(2)}, u32[]{:S(2)}) %collective-permute-start.2) | collective-permute-done | bytes 466976 | tf_op jit(solution)/shard_map/ppermute | solution.py:498
  18.1 1.7 %weights.1.coef_ref = f32[7,7,32,128]{3,2,1,0:T(8,128)S(1)} custom-call(s32[2]{0:T(128)S(1)} %pad_add_fusion.place_ref, bf16[3,3,32,128]{3,2,1,0:T(8,128)(2,1)S(1)} %copy-done.1, bf16[80,3,32,128]{3,2,1,0:T(8,128)(2,1)} %collective-permute-done.inside_ref, bf16[19,3,32,128]{3,2,1,0:T(8,128)(2,1)} %collective-permute-done.2.outside_ref), custom_call_target="tpu_custom_call" | custom-call | bytes 4000000 | tf_op jit(solution)/shard_map/weights/pallas_call | solution.py:145
  19.8 5.3 %transport.4 = (bf16[3,8,16,128]{3,2,1,0:T(8,128)(2,1)S(1)}, bf16[3,8,16,128]{3,2,1,0:T(8,128)(2,1)S(1)}, bf16[3,8,16,128]{3,2,1,0:T(8,128)(2,1)S(1)}, bf16[3,8,16,128]{3,2,1,0:T(8,128)(2,1)S(1)}) custom-call(s32[2]{0:T(128)S(1)} %pad_add_fusion.place_ref, f32[64,3,32,128]{3,2,1,0:T(8,128)S(1)} %copy-done, ...), custom_call_target="tpu_custom_call" | custom-call | bytes 18000000 | tf_op jit(solution)/shard_map/transport/pallas_call | solution.py:232
  25.1 2.8 %collective-permute-start.5 = (bf16[3,8,16,128]{3,2,1,0:T(8,128)(2,1)S(1)}, bf16[3,8,16,128]{3,2,1,0:T(8,128)(2,1)S(1)}, u32[]{:S(2)}, u32[]{:S(2)}) collective-permute-start(bf16[3,8,16,128]{3,2,1,0:T(8,128)(2,1)S(1)} %get-tuple-element.36), channel_id=1, source_target_pairs={{0,1},{1,0},{2,3},{3,2},{4,5},{5,4},{6,7},{7,6},{8,9},{9,8},{10,11... | collective-permute-start | bytes 294920 | tf_op jit(solution)/shard_map/ppermute | solution.py:498
  27.9 2.6 %collective-permute-start.6 = (bf16[3,8,16,128]{3,2,1,0:T(8,128)(2,1)S(1)}, bf16[3,8,16,128]{3,2,1,0:T(8,128)(2,1)S(1)}, u32[]{:S(2)}, u32[]{:S(2)}) collective-permute-start(bf16[3,8,16,128]{3,2,1,0:T(8,128)(2,1)S(1)} %get-tuple-element.37), channel_id=1, source_target_pairs={{0,2},{1,3},{2,0},{3,1},{4,6},{5,7},{6,4},{7,5},{8,10},{9,11},{10,... | collective-permute-start | bytes 294920 | tf_op jit(solution)/shard_map/ppermute | solution.py:498
  30.5 5.2 %transport.5 = (bf16[3,8,16,128]{3,2,1,0:T(8,128)(2,1)S(1)}, bf16[3,8,16,128]{3,2,1,0:T(8,128)(2,1)S(1)}, bf16[3,8,16,128]{3,2,1,0:T(8,128)(2,1)S(1)}, bf16[3,8,16,128]{3,2,1,0:T(8,128)(2,1)S(1)}) custom-call(s32[2]{0:T(128)S(1)} %pad_add_fusion.place_ref, f32[64,3,32,128]{3,2,1,0:T(8,128)S(1)} %copy-done, ...), custom_call_target="tpu_custom_call" | custom-call | bytes 18000000 | tf_op jit(solution)/shard_map/transport/pallas_call | solution.py:232
  36.8 3.4 %collective-permute-start.9 = (bf16[3,8,16,128]{3,2,1,0:T(8,128)(2,1)S(1)}, bf16[3,8,16,128]{3,2,1,0:T(8,128)(2,1)S(1)}, u32[]{:S(2)}, u32[]{:S(2)}) collective-permute-start(bf16[3,8,16,128]{3,2,1,0:T(8,128)(2,1)S(1)} %get-tuple-element.41), channel_id=1, source_target_pairs={{0,2},{1,3},{2,0},{3,1},{4,6},{5,7},{6,4},{7,5},{8,10},{9,11},{10,... | collective-permute-start | bytes 294920 | tf_op jit(solution)/shard_map/ppermute | solution.py:498
  40.2 5.3 %transport.6 = (bf16[3,8,16,128]{3,2,1,0:T(8,128)(2,1)S(1)}, bf16[3,8,16,128]{3,2,1,0:T(8,128)(2,1)S(1)}, bf16[3,8,16,128]{3,2,1,0:T(8,128)(2,1)S(1)}, bf16[3,8,16,128]{3,2,1,0:T(8,128)(2,1)S(1)}) custom-call(s32[2]{0:T(128)S(1)} %pad_add_fusion.place_ref, f32[64,3,32,128]{3,2,1,0:T(8,128)S(1)} %copy-done, ...), custom_call_target="tpu_custom_call" | custom-call | bytes 18000000 | tf_op jit(solution)/shard_map/transport/pallas_call | solution.py:232
  46.2 3.8 %collective-permute-start.15 = (bf16[3,8,16,128]{3,2,1,0:T(8,128)(2,1)S(1)}, bf16[3,8,16,128]{3,2,1,0:T(8,128)(2,1)S(1)}, u32[]{:S(2)}, u32[]{:S(2)}) collective-permute-start(bf16[3,8,16,128]{3,2,1,0:T(8,128)(2,1)S(1)} %get-tuple-element.48), channel_id=1, source_target_pairs={{0,2},{1,3},{2,0},{3,1},{4,6},{5,7},{6,4},{7,5},{8,10},{9,11},{10,... | collective-permute-start | bytes 294920 | tf_op jit(solution)/shard_map/ppermute | solution.py:498
  50.0 5.3 %transport.7 = (bf16[3,8,16,128]{3,2,1,0:T(8,128)(2,1)S(1)}, bf16[3,8,16,128]{3,2,1,0:T(8,128)(2,1)S(1)}, bf16[3,8,16,128]{3,2,1,0:T(8,128)(2,1)S(1)}, bf16[3,8,16,128]{3,2,1,0:T(8,128)(2,1)S(1)}) custom-call(s32[2]{0:T(128)S(1)} %pad_add_fusion.place_ref, f32[64,3,32,128]{3,2,1,0:T(8,128)S(1)} %copy-done, ...), custom_call_target="tpu_custom_call" | custom-call | bytes 18000000 | tf_op jit(solution)/shard_map/transport/pallas_call | solution.py:232
  56.0 3.8 %collective-permute-start.12 = (bf16[3,8,16,128]{3,2,1,0:T(8,128)(2,1)S(1)}, bf16[3,8,16,128]{3,2,1,0:T(8,128)(2,1)S(1)}, u32[]{:S(2)}, u32[]{:S(2)}) collective-permute-start(bf16[3,8,16,128]{3,2,1,0:T(8,128)(2,1)S(1)} %get-tuple-element.45), channel_id=1, source_target_pairs={{0,2},{1,3},{2,0},{3,1},{4,6},{5,7},{6,4},{7,5},{8,10},{9,11},{10,... | collective-permute-start | bytes 294920 | tf_op jit(solution)/shard_map/ppermute | solution.py:498
  60.4 2.0 %unpack.1.rest_4_ = f32[3,2048,128]{2,1,0:T(8,128)S(1)} custom-call(s32[2]{0:T(128)S(1)} %pad_add_fusion.place_ref, bf16[3,8,16,128]{3,2,1,0:T(8,128)(2,1)S(1)} %get-tuple-element.34.rest_0_.refs_0_, bf16[3,8,16,128]{3,2,1,0:T(8,128)(2,1)S(1)} %get-tuple-element.35.rest_0_.refs_1_, bf16[3,8,16,128]{3,2,1,0:T(8,128)(2,1)S(1)} %get-tuple-element.39.rest_0_.refs_2_, ...), custom_call_target="tpu_custom_call" | custom-call | bytes 12000000 | tf_op jit(solution)/shard_map/unpack/pallas_call | solution.py:323
  62.5 5.0 %collective-permute-done.12.rest_2_ = bf16[3,8,16,128]{3,2,1,0:T(8,128)(2,1)S(1)} collective-permute-done((bf16[3,8,16,128]{3,2,1,0:T(8,128)(2,1)S(1)}, bf16[3,8,16,128]{3,2,1,0:T(8,128)(2,1)S(1)}, u32[]{:S(2)}, u32[]{:S(2)}) %collective-permute-start.12) | collective-permute-done | bytes 98336 | tf_op jit(solution)/shard_map/ppermute | solution.py:498
  67.5 13.2 %kinetics.1 = (f32[256,3,8,128]{3,2,1,0:T(8,128)}, f32[3,8,128]{2,1,0:T(8,128)S(1)}) custom-call(s32[2]{0:T(128)S(1)} %pad_add_fusion.place_ref, f32[3,8,128]{2,1,0:T(8,128)S(1)} %copy-done.2, bf16[256,256]{1,0:T(8,128)(2,1)S(1)} %get-tuple-element.27.toeplitz_ref, f32[256,128]{1,0:T(8,128)S(1)} %get-tuple-element.28.column_ref, ...), custom_call_target="tpu_custom_call" | custom-call | bytes 50000000 | tf_op jit(solution)/shard_map/kinetics/pallas_call | solution.py:455
  80.7 2.5 %collective-permute-start.19 = (f32[3,8,128]{2,1,0:T(8,128)S(1)}, f32[3,8,128]{2,1,0:T(8,128)S(1)}, u32[]{:S(2)}, u32[]{:S(2)}) collective-permute-start(f32[3,8,128]{2,1,0:T(8,128)S(1)} %get-tuple-element.51.refs_0_), channel_id=1, source_target_pairs={{0,3},{1,2},{2,1},{3,0},{4,7},{5,6},{6,5},{7,4},{8,11},{9,10},{10,... | collective-permute-start | bytes 36872 | tf_op jit(solution)/shard_map/ppermute | solution.py:498
  83.2 1.2 %collective-permute-start.18 = (f32[3,8,128]{2,1,0:T(8,128)S(1)}, f32[3,8,128]{2,1,0:T(8,128)S(1)}, u32[]{:S(2)}, u32[]{:S(2)}) collective-permute-start(f32[3,8,128]{2,1,0:T(8,128)S(1)} %get-tuple-element.51.refs_0_), channel_id=1, source_target_pairs={{0,2},{1,3},{2,0},{3,1},{4,6},{5,7},{6,4},{7,5},{8,10},{9,11},{10,... | collective-permute-start | bytes 36872 | tf_op jit(solution)/shard_map/ppermute | solution.py:498
  85.1 1.2 %collective-permute-done.19.refs_3_ = f32[3,8,128]{2,1,0:T(8,128)S(1)} collective-permute-done((f32[3,8,128]{2,1,0:T(8,128)S(1)}, f32[3,8,128]{2,1,0:T(8,128)S(1)}, u32[]{:S(2)}, u32[]{:S(2)}) %collective-permute-start.19) | collective-permute-done | bytes 12320 | tf_op jit(solution)/shard_map/ppermute | solution.py:498
  86.3 1.5 %collective-permute-done.18.refs_2_ = f32[3,8,128]{2,1,0:T(8,128)S(1)} collective-permute-done((f32[3,8,128]{2,1,0:T(8,128)S(1)}, f32[3,8,128]{2,1,0:T(8,128)S(1)}, u32[]{:S(2)}, u32[]{:S(2)}) %collective-permute-start.18) | collective-permute-done | bytes 12320 | tf_op jit(solution)/shard_map/ppermute | solution.py:498
  88.1 1.2 %assemble.1 = f32[3,4,8,128]{3,2,1,0:T(8,128)} custom-call(s32[2]{0:T(128)S(1)} %pad_add_fusion.place_ref, f32[3,8,128]{2,1,0:T(8,128)S(1)} %get-tuple-element.51.refs_0_, f32[3,8,128]{2,1,0:T(8,128)S(1)} %collective-permute-done.17.refs_1_, f32[3,8,128]{2,1,0:T(8,128)S(1)} %collective-permute-done.18.refs_2_, f32[3,8,128]{2,1,0:T(8,128)S(1)} %collective-permute-done.19.refs_3_), custom_call_target="tpu_custom_call" | custom-call | tf_op jit(solution)/shard_map/assemble/pallas_call | solution.py:484
  (36 shorter events, 5.3 us)
Async XLA Ops:
  0.6 19.2 %copy-start = (f32[64,3,32,128]{3,2,1,0:T(8,128)S(1)}, f32[64,3,32,128]{3,2,1,0:T(8,128)}, u32[]{:S(2)}) copy-start(f32[64,3,32,128]{3,2,1,0:T(8,128)} %pop_ref.7) | copy-start | bytes 9437188
  4.7 12.5 %collective-permute-start = (bf16[80,3,32,128]{3,2,1,0:T(8,128)(2,1)}, bf16[80,3,32,128]{3,2,1,0:T(8,128)(2,1)}, u32[]{:S(2)}, u32[]{:S(2)}) collective-permute-start(bf16[80,3,32,128]{3,2,1,0:T(8,128)(2,1)} %get-tuple-element.29), channel_id=1, source_target_pairs={{0,4},{4,0},{8,12},{12,8},{16,20},{20,16},{24,28},{28,24},{1,5},{5... | collective-permute-start | bytes 5898248 | tf_op jit(solution)/shard_map/ppermute | solution.py:498
  4.7 12.4 %collective-permute-start.2 = (bf16[19,3,32,128]{3,2,1,0:T(8,128)(2,1)}, bf16[19,3,32,128]{3,2,1,0:T(8,128)(2,1)}, u32[]{:S(2)}, u32[]{:S(2)}) collective-permute-start(bf16[19,3,32,128]{3,2,1,0:T(8,128)(2,1)} %get-tuple-element.31), channel_id=1, source_target_pairs={{4,8},{8,4},{12,16},{16,12},{20,24},{24,20},{5,9},{9,5},{13,17},{1... | collective-permute-start | bytes 1400840 | tf_op jit(solution)/shard_map/ppermute | solution.py:498
  6.7 23.9 %collective-permute-start.4 = (bf16[16,3,32,128]{3,2,1,0:T(8,128)(2,1)}, bf16[16,3,32,128]{3,2,1,0:T(8,128)(2,1)S(1)}, u32[]{:S(2)}, u32[]{:S(2)}) collective-permute-start(bf16[16,3,32,128]{3,2,1,0:T(8,128)(2,1)} %get-tuple-element.33), channel_id=1, source_target_pairs={{4,8},{8,4},{12,16},{16,12},{20,24},{24,20},{5,9},{9,5},{13,17},{1... | collective-permute-start | bytes 1179656 | tf_op jit(solution)/shard_map/ppermute | solution.py:498
  10.3 25.4 %collective-permute-start.3 = (bf16[16,3,32,128]{3,2,1,0:T(8,128)(2,1)}, bf16[16,3,32,128]{3,2,1,0:T(8,128)(2,1)}, u32[]{:S(2)}, u32[]{:S(2)}) collective-permute-start(bf16[16,3,32,128]{3,2,1,0:T(8,128)(2,1)} %get-tuple-element.32), channel_id=1, source_target_pairs={{4,8},{8,4},{12,16},{16,12},{20,24},{24,20},{5,9},{9,5},{13,17},{1... | collective-permute-start | bytes 1179656 | tf_op jit(solution)/shard_map/ppermute | solution.py:498
  12.2 33.9 %collective-permute-start.1 = (bf16[16,3,32,128]{3,2,1,0:T(8,128)(2,1)}, bf16[16,3,32,128]{3,2,1,0:T(8,128)(2,1)}, u32[]{:S(2)}, u32[]{:S(2)}) collective-permute-start(bf16[16,3,32,128]{3,2,1,0:T(8,128)(2,1)} %get-tuple-element.30), channel_id=1, source_target_pairs={{4,8},{8,4},{12,16},{16,12},{20,24},{24,20},{5,9},{9,5},{13,17},{1... | collective-permute-start | bytes 1179656 | tf_op jit(solution)/shard_map/ppermute | solution.py:498
  17.2 0.9 copy-start.1
  25.1 11.7 %collective-permute-start.5 = (bf16[3,8,16,128]{3,2,1,0:T(8,128)(2,1)S(1)}, bf16[3,8,16,128]{3,2,1,0:T(8,128)(2,1)S(1)}, u32[]{:S(2)}, u32[]{:S(2)}) collective-permute-start(bf16[3,8,16,128]{3,2,1,0:T(8,128)(2,1)S(1)} %get-tuple-element.36), channel_id=1, source_target_pairs={{0,1},{1,0},{2,3},{3,2},{4,5},{5,4},{6,7},{7,6},{8,9},{9,8},{10,11... | collective-permute-start | bytes 294920 | tf_op jit(solution)/shard_map/ppermute | solution.py:498
  27.9 12.2 %collective-permute-start.6 = (bf16[3,8,16,128]{3,2,1,0:T(8,128)(2,1)S(1)}, bf16[3,8,16,128]{3,2,1,0:T(8,128)(2,1)S(1)}, u32[]{:S(2)}, u32[]{:S(2)}) collective-permute-start(bf16[3,8,16,128]{3,2,1,0:T(8,128)(2,1)S(1)} %get-tuple-element.37), channel_id=1, source_target_pairs={{0,2},{1,3},{2,0},{3,1},{4,6},{5,7},{6,4},{7,5},{8,10},{9,11},{10,... | collective-permute-start | bytes 294920 | tf_op jit(solution)/shard_map/ppermute | solution.py:498
  30.5 9.7 %collective-permute-start.7 = (bf16[3,8,16,128]{3,2,1,0:T(8,128)(2,1)S(1)}, bf16[3,8,16,128]{3,2,1,0:T(8,128)(2,1)S(1)}, u32[]{:S(2)}, u32[]{:S(2)}) collective-permute-start(bf16[3,8,16,128]{3,2,1,0:T(8,128)(2,1)S(1)} %get-tuple-element.38), channel_id=1, source_target_pairs={{0,3},{1,2},{2,1},{3,0},{4,7},{5,6},{6,5},{7,4},{8,11},{9,10},{10,... | collective-permute-start | bytes 294920 | tf_op jit(solution)/shard_map/ppermute | solution.py:498
  35.7 14.2 %collective-permute-start.8 = (bf16[3,8,16,128]{3,2,1,0:T(8,128)(2,1)S(1)}, bf16[3,8,16,128]{3,2,1,0:T(8,128)(2,1)S(1)}, u32[]{:S(2)}, u32[]{:S(2)}) collective-permute-start(bf16[3,8,16,128]{3,2,1,0:T(8,128)(2,1)S(1)} %get-tuple-element.40), channel_id=1, source_target_pairs={{0,1},{1,0},{2,3},{3,2},{4,5},{5,4},{6,7},{7,6},{8,9},{9,8},{10,11... | collective-permute-start | bytes 294920 | tf_op jit(solution)/shard_map/ppermute | solution.py:498
  36.8 13.1 %collective-permute-start.9 = (bf16[3,8,16,128]{3,2,1,0:T(8,128)(2,1)S(1)}, bf16[3,8,16,128]{3,2,1,0:T(8,128)(2,1)S(1)}, u32[]{:S(2)}, u32[]{:S(2)}) collective-permute-start(bf16[3,8,16,128]{3,2,1,0:T(8,128)(2,1)S(1)} %get-tuple-element.41), channel_id=1, source_target_pairs={{0,2},{1,3},{2,0},{3,1},{4,6},{5,7},{6,4},{7,5},{8,10},{9,11},{10,... | collective-permute-start | bytes 294920 | tf_op jit(solution)/shard_map/ppermute | solution.py:498
  40.2 9.8 %collective-permute-start.10 = (bf16[3,8,16,128]{3,2,1,0:T(8,128)(2,1)S(1)}, bf16[3,8,16,128]{3,2,1,0:T(8,128)(2,1)S(1)}, u32[]{:S(2)}, u32[]{:S(2)}) collective-permute-start(bf16[3,8,16,128]{3,2,1,0:T(8,128)(2,1)S(1)} %get-tuple-element.42), channel_id=1, source_target_pairs={{0,3},{1,2},{2,1},{3,0},{4,7},{5,6},{6,5},{7,4},{8,11},{9,10},{10,... | collective-permute-start | bytes 294920 | tf_op jit(solution)/shard_map/ppermute | solution.py:498
  45.5 14.2 %collective-permute-start.14 = (bf16[3,8,16,128]{3,2,1,0:T(8,128)(2,1)S(1)}, bf16[3,8,16,128]{3,2,1,0:T(8,128)(2,1)S(1)}, u32[]{:S(2)}, u32[]{:S(2)}) collective-permute-start(bf16[3,8,16,128]{3,2,1,0:T(8,128)(2,1)S(1)} %get-tuple-element.47), channel_id=1, source_target_pairs={{0,1},{1,0},{2,3},{3,2},{4,5},{5,4},{6,7},{7,6},{8,9},{9,8},{10,11... | collective-permute-start | bytes 294920 | tf_op jit(solution)/shard_map/ppermute | solution.py:498
  46.2 14.3 %collective-permute-start.15 = (bf16[3,8,16,128]{3,2,1,0:T(8,128)(2,1)S(1)}, bf16[3,8,16,128]{3,2,1,0:T(8,128)(2,1)S(1)}, u32[]{:S(2)}, u32[]{:S(2)}) collective-permute-start(bf16[3,8,16,128]{3,2,1,0:T(8,128)(2,1)S(1)} %get-tuple-element.48), channel_id=1, source_target_pairs={{0,2},{1,3},{2,0},{3,1},{4,6},{5,7},{6,4},{7,5},{8,10},{9,11},{10,... | collective-permute-start | bytes 294920 | tf_op jit(solution)/shard_map/ppermute | solution.py:498
  49.9 10.5 %collective-permute-start.16 = (bf16[3,8,16,128]{3,2,1,0:T(8,128)(2,1)S(1)}, bf16[3,8,16,128]{3,2,1,0:T(8,128)(2,1)S(1)}, u32[]{:S(2)}, u32[]{:S(2)}) collective-permute-start(bf16[3,8,16,128]{3,2,1,0:T(8,128)(2,1)S(1)} %get-tuple-element.49), channel_id=1, source_target_pairs={{0,3},{1,2},{2,1},{3,0},{4,7},{5,6},{6,5},{7,4},{8,11},{9,10},{10,... | collective-permute-start | bytes 294920 | tf_op jit(solution)/shard_map/ppermute | solution.py:498
  49.9 9.8 %copy-start.3 = (f32[256]{0:T(256)S(1)}, f32[256]{0:T(256)}, u32[]{:S(2)}) copy-start(f32[256]{0:T(256)} %param.7) | copy-start | bytes 3076
  55.3 12.3 %copy-start.2 = (f32[3,8,128]{2,1,0:T(8,128)S(1)}, f32[3,8,128]{2,1,0:T(8,128)}, u32[]{:S(2)}) copy-start(f32[3,8,128]{2,1,0:T(8,128)} %supersat_ref.1) | copy-start | bytes 36868
  55.3 7.2 %collective-permute-start.11 = (bf16[3,8,16,128]{3,2,1,0:T(8,128)(2,1)S(1)}, bf16[3,8,16,128]{3,2,1,0:T(8,128)(2,1)S(1)}, u32[]{:S(2)}, u32[]{:S(2)}) collective-permute-start(bf16[3,8,16,128]{3,2,1,0:T(8,128)(2,1)S(1)} %get-tuple-element.44), channel_id=1, source_target_pairs={{0,1},{1,0},{2,3},{3,2},{4,5},{5,4},{6,7},{7,6},{8,9},{9,8},{10,11... | collective-permute-start | bytes 294920 | tf_op jit(solution)/shard_map/ppermute | solution.py:498
  56.0 11.6 %collective-permute-start.12 = (bf16[3,8,16,128]{3,2,1,0:T(8,128)(2,1)S(1)}, bf16[3,8,16,128]{3,2,1,0:T(8,128)(2,1)S(1)}, u32[]{:S(2)}, u32[]{:S(2)}) collective-permute-start(bf16[3,8,16,128]{3,2,1,0:T(8,128)(2,1)S(1)} %get-tuple-element.45), channel_id=1, source_target_pairs={{0,2},{1,3},{2,0},{3,1},{4,6},{5,7},{6,4},{7,5},{8,10},{9,11},{10,... | collective-permute-start | bytes 294920 | tf_op jit(solution)/shard_map/ppermute | solution.py:498
  59.7 7.8 %collective-permute-start.13 = (bf16[3,8,16,128]{3,2,1,0:T(8,128)(2,1)S(1)}, bf16[3,8,16,128]{3,2,1,0:T(8,128)(2,1)S(1)}, u32[]{:S(2)}, u32[]{:S(2)}) collective-permute-start(bf16[3,8,16,128]{3,2,1,0:T(8,128)(2,1)S(1)} %get-tuple-element.46), channel_id=1, source_target_pairs={{0,3},{1,2},{2,1},{3,0},{4,7},{5,6},{6,5},{7,4},{8,11},{9,10},{10,... | collective-permute-start | bytes 294920 | tf_op jit(solution)/shard_map/ppermute | solution.py:498
  80.7 5.6 %collective-permute-start.19 = (f32[3,8,128]{2,1,0:T(8,128)S(1)}, f32[3,8,128]{2,1,0:T(8,128)S(1)}, u32[]{:S(2)}, u32[]{:S(2)}) collective-permute-start(f32[3,8,128]{2,1,0:T(8,128)S(1)} %get-tuple-element.51.refs_0_), channel_id=1, source_target_pairs={{0,3},{1,2},{2,1},{3,0},{4,7},{5,6},{6,5},{7,4},{8,11},{9,10},{10,... | collective-permute-start | bytes 36872 | tf_op jit(solution)/shard_map/ppermute | solution.py:498
  83.2 4.6 %collective-permute-start.18 = (f32[3,8,128]{2,1,0:T(8,128)S(1)}, f32[3,8,128]{2,1,0:T(8,128)S(1)}, u32[]{:S(2)}, u32[]{:S(2)}) collective-permute-start(f32[3,8,128]{2,1,0:T(8,128)S(1)} %get-tuple-element.51.refs_0_), channel_id=1, source_target_pairs={{0,2},{1,3},{2,0},{3,1},{4,6},{5,7},{6,4},{7,5},{8,10},{9,11},{10,... | collective-permute-start | bytes 36872 | tf_op jit(solution)/shard_map/ppermute | solution.py:498
  84.4 3.7 %collective-permute-start.17 = (f32[3,8,128]{2,1,0:T(8,128)S(1)}, f32[3,8,128]{2,1,0:T(8,128)S(1)}, u32[]{:S(2)}, u32[]{:S(2)}) collective-permute-start(f32[3,8,128]{2,1,0:T(8,128)S(1)} %get-tuple-element.51.refs_0_), channel_id=1, source_target_pairs={{0,1},{1,0},{2,3},{3,2},{4,5},{5,4},{6,7},{7,6},{8,9},{9,8},{10,11... | collective-permute-start | bytes 36872 | tf_op jit(solution)/shard_map/ppermute | solution.py:498
